TPU v7x, 512 devices: a whole 4x4x16 slice. The times are simulated.
512 devices in a mesh: dp: 64 (over x, z), mp: 8 (over y, core).
Axes of the slice: x: 4, y: 4, z: 16, core: 2. Of those that a mesh axis runs over, the one named last changes fastest.
Arguments:
- partial_grads: bfloat16 [64, 16, 512, 512], P('dp', None, 'mp'), may hold values from -2 to 2
- owner_slot: int32 [16], replicated, may hold values from 0 to 15, each once
- extent: int32 [16, 2], replicated, may hold values from 128 to 512, as said below
- left_roots: bfloat16 [16, 512, 512], P('mp')
- right_roots: bfloat16 [16, 512, 512], P('mp', None, 'dp')
- momentum: float32 [16, 512, 512], P('mp', None, 'dp'), may hold values from -4 to 4
- master: float32 [16, 512, 512], P('mp', None, 'dp'), may hold values from -6 to 6
Outputs:
- new_momentum: float32 [16, 512, 512], P('mp', None, 'dp')
- new_master: float32 [16, 512, 512], P('mp', None, 'dp')
- weights: bfloat16 [16, 512, 512], P(None, 'mp')
Inputs may be any that keep to these rules, and one draw needn't show every extreme that they name: owner_slot is a permutation of 0 to 15. `extent`: some block has both bounds equal to 512.
All inputs are finite; a program needn't handle non-finite values.
Results may differ from a plain program's by a relative error of at most 0.0035.
Values may be sent and summed in bfloat16 or wider, within the bound.
No kernel may reach another device: no remote copies, remote signals or barrier semaphores. Data moves between devices by JAX's collectives and lax.ppermute only.
A program may use at most 64 MiB of HBM per device.

v0:
```python
import jax
import jax.numpy as jnp
from jax import lax
from jax.sharding import PartitionSpec as P

epsilon = 1e-06
beta_decay = 0.9
step_rate = 0.5


def local(partial_grads, owner_slot, extent, left_roots, right_roots, momentum, master):
    blocks = partial_grads.shape[1]
    width = partial_grads.shape[3]
    owned = left_roots.shape[0]
    slab = right_roots.shape[2]
    slots = jnp.arange(blocks, dtype=jnp.int32)
    match = owner_slot[None, :] == slots[:, None]
    order = jnp.sum(jnp.where(match, slots[None, :], 0), axis=1)
    bounds_all = jnp.sum(jnp.where(match[:, :, None], extent[None, :, :], 0), axis=1)
    first_slot = lax.axis_index("mp") * owned
    bounds = lax.dynamic_slice_in_dim(bounds_all, first_slot, owned, 0)
    first_col = lax.axis_index("dp") * slab
    positions = jnp.arange(width, dtype=jnp.int32)
    row_mask = (positions[None, :] < bounds[:, 0:1]).astype(jnp.float32)
    col_mask = (positions[None, :] < bounds[:, 1:2]).astype(jnp.float32)
    slab_cols = lax.dynamic_slice_in_dim(col_mask, first_col, slab, 1)
    slab_mask = row_mask[:, :, None] * slab_cols[:, None, :]
    terms = jnp.take(partial_grads[0], order, axis=0).astype(jnp.float32)
    summed = lax.psum(terms, "dp")
    gathered = lax.all_to_all(
        summed.astype(jnp.bfloat16), "mp", split_axis=0, concat_axis=1, tiled=True
    ).astype(summed.dtype)
    full_grad = gathered * (row_mask[:, :, None] * col_mask[:, None, :])
    grad_slab = lax.dynamic_slice_in_dim(full_grad, first_col, slab, 2)
    grad_low = full_grad.astype(jnp.bfloat16)
    right_side = jnp.einsum(
        "kij,kjc->kic", grad_low, right_roots, preferred_element_type=jnp.float32
    ).astype(jnp.bfloat16)
    precond = jnp.einsum("kij,kjc->kic", left_roots, right_side, preferred_element_type=jnp.float32)
    grad_sq, pre_sq = lax.psum(
        (jnp.sum(grad_slab * grad_slab, axis=(1, 2)), jnp.sum(precond * precond, axis=(1, 2))), "dp"
    )
    scale = jnp.sqrt(grad_sq / (pre_sq + epsilon))
    new_momentum = beta_decay * momentum + scale[:, None, None] * precond * slab_mask
    new_master = master - step_rate * new_momentum
    fresh = new_master.astype(jnp.bfloat16)
    whole_blocks = lax.all_gather(fresh, "dp", axis=2, tiled=True)
    returned = lax.all_to_all(whole_blocks, "mp", split_axis=1, concat_axis=0, tiled=True)
    weights = jnp.take(returned, owner_slot, axis=0)
    return (new_momentum, new_master, weights)


def solution(mesh):
    placed = (
        P("dp", None, "mp", None),
        P(),
        P(),
        P("mp", None, None),
        P("mp", None, "dp"),
        P("mp", None, "dp"),
        P("mp", None, "dp"),
    )
    return jax.shard_map(
        local,
        mesh=mesh,
        in_specs=placed,
        out_specs=(P("mp", None, "dp"), P("mp", None, "dp"), P(None, "mp", None)),
        check_vma=False,
    )
```

profile of v0, /device:TPU:1, one launch (start us, length us, event | category | flops | bytes accessed | tf_op | source)
XLA Modules:
  0.0 634.9 jit_solution(15037931437215250713)
XLA Ops:
  7.2 0.9 select_reduce_fusion.1
  8.1 0.3 copy-done
  8.4 1.6 gather_fusion
  10.0 1.4 select_convert_fusion
  11.5 254.4 %all-reduce.2 = bf16[16,64,512]{2,1,0:T(8,128)(2,1)} all-reduce(f32[16,64,512]{2,1,0:T(8,128)S(1)} %select_convert_fusion), channel_id=1, replica_groups=mesh['dp'=64,'mp'=8] {'dp'}, use_global_device_ids=true, to_apply=%region_1.3 | all-reduce | flops 524288 | bytes 3145728 | tf_op jit(solution)/shard_map/psum | solution.py:29
  265.8 59.3 %all-to-all-start = ((bf16[16,64,512]{2,1,0:T(8,128)(2,1)}), bf16[16,64,512]{2,1,0:T(8,128)(2,1)S(1)}, u32[]{:S(2)}, u32[]{:S(2)}) async-start(bf16[16,64,512]{2,1,0:T(8,128)(2,1)} %all-reduce.2), calls=%async_computation | async-start | bytes 2097152 | tf_op jit(solution)/shard_map/all_to_all | solution.py:30
  325.1 0.1 select_reduce_fusion
  325.5 14.7 %all-to-all-done = bf16[16,64,512]{2,1,0:T(8,128)(2,1)S(1)} async-done(((bf16[16,64,512]{2,1,0:T(8,128)(2,1)}), bf16[16,64,512]{2,1,0:T(8,128)(2,1)S(1)}, u32[]{:S(2)}, u32[]{:S(2)}) %all-to-all-start) | async-done | bytes 1048608 | tf_op jit(solution)/shard_map/all_to_all | solution.py:30
  340.2 0.3 convert_bitcast_fusion
  340.5 0.2 copy.23
  340.7 0.2 bitcast_multiply_fusion
  341.0 0.3 multiply_reduce_fusion
  341.3 0.1 copy-done.3
  341.4 2.0 multiply_reduce_fusion.1
  343.4 110.4 %all-reduce = (f32[2]{0:T(128)S(1)}, f32[2]{0:T(128)S(1)}) all-reduce(f32[2]{0:T(128)S(1)} %multiply_reduce_fusion, f32[2]{0:T(128)S(1)} %get-tuple-element.11), channel_id=1, replica_groups=mesh['dp'=64,'mp'=8] {'dp'}, use_global_device_ids=true, to_apply=%region_4.6 | all-reduce | flops 4 | bytes 32 | tf_op jit(solution)/shard_map/psum | solution.py:40
  453.9 0.7 fusion.5
  454.6 136.7 %all-gather.2.cloned.1.call-done = bf16[2,512,512]{1,2,0:T(8,128)(2,1)} async-done(((bf16[2,512,8]{1,2,0:T(8,128)(2,1)}), bf16[2,512,512]{1,2,0:T(8,128)(2,1)}) %all-gather.2.cloned.1.call-update) | async-done | bytes 1048592 | tf_op jit(solution)/shard_map/all_gather | solution.py:47
  591.2 3.7 copy.24
  594.9 16.0 %all-to-all-start.1 = ((bf16[2,512,512]{2,0,1:T(2,128)(2,1)}), bf16[2,512,512]{2,0,1:T(2,128)(2,1)S(1)}, u32[]{:S(2)}, u32[]{:S(2)}) async-start(bf16[2,512,512]{2,0,1:T(2,128)(2,1)} %copy.24), calls=%async_computation.1 | async-start | bytes 2097152 | tf_op jit(solution)/shard_map/all_to_all | solution.py:48
  610.9 15.1 %all-to-all-done.1 = bf16[2,512,512]{2,0,1:T(2,128)(2,1)S(1)} async-done(((bf16[2,512,512]{2,0,1:T(2,128)(2,1)}), bf16[2,512,512]{2,0,1:T(2,128)(2,1)S(1)}, u32[]{:S(2)}, u32[]{:S(2)}) %all-to-all-start.1) | async-done | bytes 1048608 | tf_op jit(solution)/shard_map/all_to_all | solution.py:48
  626.0 0.2 copy.25
  626.2 0.1 copy.26
  626.3 0.6 gather_fusion.1
  626.9 1.1 broadcast_select_fusion
  (24 shorter events, 0.3 us)
Async XLA Ops:
  7.2 1.2 copy-start
  11.4 313.7 %copy-start.5 = (s32[16]{0:T(128)S(1)}, s32[16]{0:T(128)}, u32[]{:S(2)}) copy-start(s32[16]{0:T(128)} %param.10) | copy-start | bytes 196
  11.4 313.7 %copy-start.4 = (s32[16,2]{0,1:T(2,128)S(1)}, s32[16,2]{0,1:T(2,128)}, u32[]{:S(2)}) copy-start(s32[16,2]{0,1:T(2,128)} %param.11) | copy-start | bytes 388
  265.8 74.4 %all-to-all-start = ((bf16[16,64,512]{2,1,0:T(8,128)(2,1)}), bf16[16,64,512]{2,1,0:T(8,128)(2,1)S(1)}, u32[]{:S(2)}, u32[]{:S(2)}) async-start(bf16[16,64,512]{2,1,0:T(8,128)(2,1)} %all-reduce.2), calls=%async_computation | async-start | bytes 2097152 | tf_op jit(solution)/shard_map/all_to_all | solution.py:30
  325.1 266.2 %all-gather.2.cloned.1.call-start = ((), (), s32[]{:S(2)}) async-start(), calls=%async_computation.2 | async-start | bytes 1064960 | tf_op jit(solution)/shard_map/all_gather | solution.py:47
  340.7 0.7 copy-start.3
  341.0 112.9 %copy-start.1 = (f32[2,512,8]{1,2,0:T(8,128)S(1)}, f32[2,512,8]{1,2,0:T(8,128)}, u32[]{:S(2)}) copy-start(f32[2,512,8]{1,2,0:T(8,128)} %param.15) | copy-start | bytes 98308
  341.0 112.9 %copy-start.2 = (f32[2,512,8]{1,2,0:T(8,128)S(1)}, f32[2,512,8]{1,2,0:T(8,128)}, u32[]{:S(2)}) copy-start(f32[2,512,8]{1,2,0:T(8,128)} %param.14) | copy-start | bytes 98308
  594.9 31.1 %all-to-all-start.1 = ((bf16[2,512,512]{2,0,1:T(2,128)(2,1)}), bf16[2,512,512]{2,0,1:T(2,128)(2,1)S(1)}, u32[]{:S(2)}, u32[]{:S(2)}) async-start(bf16[2,512,512]{2,0,1:T(2,128)(2,1)} %copy.24), calls=%async_computation.1 | async-start | bytes 2097152 | tf_op jit(solution)/shard_map/all_to_all | solution.py:48
Sparse Core Ops, SparseCore 0:
  454.7 136.4 all-gather.1
where the time goes:
time: 635 us
  blocking collectives  365 us (57%)
  waiting for transfers between devices  166 us (26%)
  starting transfers between devices  75.3 us (12%)
  between operations  14.2 us (2%)
  local copies, waits for them, and re-layouts  7.01 us (1%)
    psum x1, blocking collectives, local(): summed = lax.psum(terms, 'dp')  254 us
    all_gather x1, waiting for transfers between devices, local(): whole_blocks = lax.all_gather(fresh, 'dp', axis=2, tiled=True)  137 us
    psum x1, blocking collectives, local(): lax.psum((jnp.sum(grad_slab * grad_slab, axis=(1, 2)), jnp.sum(precond *...  110 us
    all_to_all x1, starting transfers between devices, local(): lax.all_to_all(summed.astype(jnp.bfloat16), 'mp', split_axis=0, concat_ax...  59.3 us
    all_to_all x1, starting transfers between devices, local(): lax.all_to_all(whole_blocks, 'mp', split_axis=1, concat_axis=0, tiled=True)  16 us
    all_to_all x1, waiting for transfers between devices, local(): lax.all_to_all(whole_blocks, 'mp', split_axis=1, concat_axis=0, tiled=True)  15.1 us
    all_to_all x1, waiting for transfers between devices, local(): lax.all_to_all(summed.astype(jnp.bfloat16), 'mp', split_axis=0, concat_ax...  14.7 us
  transfers between devices with their start and end apart: 3, of which 3 were waited for; matrix products, arithmetic and copies ran while one was open for 0% of the time, Pallas kernels for 0%

commit v1 on v0

v1 whole, which is shorter than its diff:
```python
import jax
import jax.numpy as jnp
from jax import lax
from jax.sharding import Mesh, PartitionSpec as P

epsilon = 1e-06
beta_decay = 0.9
step_rate = 0.5
f32 = jnp.float32
bf16 = jnp.bfloat16


def split_low(value):
    high = lax.reduce_precision(value, 8, 7)
    return high.astype(bf16), (value - high).astype(bf16)


def split3(value):
    high = lax.reduce_precision(value, 8, 7)
    middle = lax.reduce_precision(value - high, 8, 7)
    return high.astype(bf16), middle.astype(bf16), (value - high - middle).astype(bf16)


def make_local(nx, nz, nm):
    def local(partial_grads, owner_slot, extent, left_roots, right_roots, momentum, master):
        blocks = partial_grads.shape[1]
        rows = partial_grads.shape[2]
        width = partial_grads.shape[3]
        owned = left_roots.shape[0]
        slab = right_roots.shape[2]
        cols = width // nx
        band = width // nz
        x, z, m = lax.axis_index("x"), lax.axis_index("z"), lax.axis_index("mp")
        slots = jnp.arange(blocks, dtype=jnp.int32)
        match = owner_slot[None, :] == slots[:, None]
        order = jnp.sum(jnp.where(match, slots[None, :], 0), axis=1)
        bounds_all = jnp.sum(jnp.where(match[:, :, None], extent[None, :, :], 0), axis=1)
        bounds = lax.dynamic_slice_in_dim(bounds_all, m * owned, owned, 0)
        row_ids = jnp.arange(width, dtype=jnp.int32)

        base_t = jnp.swapaxes(master - (step_rate * beta_decay) * momentum, 1, 2)
        high, low = split_low(base_t)
        right_t = jnp.swapaxes(right_roots, 1, 2)
        mine = jnp.concatenate([right_t, high, low, jnp.zeros_like(high)], axis=0)
        parts = lax.all_gather(mine, "z", axis=0, tiled=False)
        parts = jnp.swapaxes(parts, 0, 1).reshape(4 * owned, cols, width)
        right_cols_t = parts[:owned]
        base_cols = jnp.swapaxes(
            parts[owned : 2 * owned].astype(f32) + parts[2 * owned : 3 * owned].astype(f32), 1, 2
        )

        send = jnp.take(partial_grads[0], order, axis=0)
        send = send.reshape(nm * owned, rows, nx, cols).transpose(2, 0, 1, 3)
        send = send.reshape(nx * nm, owned, rows, cols)
        got = lax.all_to_all(send, ("x", "mp"), split_axis=0, concat_axis=0, tiled=True)
        got = got.reshape(nx, nm, owned, rows, cols)
        part = got[0].astype(f32)
        for i in range(1, nx):
            part = part + got[i].astype(f32)
        part = part.reshape(nm, owned, rows // band, band, cols).transpose(0, 2, 1, 3, 4)
        part = part.reshape(nz, owned, band, cols)
        pieces = lax.all_to_all(part, "z", split_axis=0, concat_axis=0, tiled=True)
        total = jnp.sum(pieces, axis=0)
        band_rows = z * band + jnp.arange(band, dtype=jnp.int32)
        band_cols = x * cols + jnp.arange(cols, dtype=jnp.int32)
        row_ok = band_rows[None, :, None] < bounds[:, 0][:, None, None]
        col_ok = band_cols[None, None, :] < bounds[:, 1][:, None, None]
        grad = jnp.where(row_ok & col_ok, total, 0.0)
        sq_piece = jnp.sum(grad * grad, axis=(1, 2))
        grad_low = grad.astype(bf16)
        spread = jnp.broadcast_to(grad_low[None], (nx,) + grad_low.shape)
        all_cols = lax.all_to_all(spread, "x", split_axis=0, concat_axis=0, tiled=True)
        grad_rows = all_cols.transpose(1, 2, 0, 3).reshape(owned, band, width)
        right_side = jnp.einsum(
            "kij,kcj->kic", grad_rows, right_cols_t, preferred_element_type=f32
        ).astype(bf16)
        extra = jnp.stack(split3(sq_piece), axis=0).reshape(3 * owned)
        extra = jnp.broadcast_to(extra[:, None], (3 * owned, cols))
        extra = jnp.pad(extra, ((0, 16 - 3 * owned), (0, 0)))
        packed = jnp.concatenate([right_side.reshape(owned * band, cols), extra], axis=0)
        spread = jnp.broadcast_to(packed[None], (nz,) + packed.shape)
        bands = lax.all_to_all(spread, "z", split_axis=0, concat_axis=0, tiled=True)
        sq = bands[:, owned * band : owned * band + 3 * owned, 0].astype(f32)
        grad_sq = jnp.sum(sq.reshape(nz, 3, owned), axis=(0, 1))
        side = bands[:, : owned * band].reshape(nz, owned, band, cols)
        side = side.transpose(1, 0, 2, 3).reshape(owned, width, cols)
        precond = jnp.einsum("kij,kjc->kic", left_roots, side, preferred_element_type=f32)
        pre_sq = jnp.sum(precond * precond, axis=(1, 2))
        grad_sq, pre_sq = lax.psum(jnp.stack([grad_sq, pre_sq]), "x")
        scale = jnp.sqrt(grad_sq / (pre_sq + epsilon))
        mask = (row_ids[None, :, None] < bounds[:, 0][:, None, None]) & col_ok
        step = jnp.where(mask, scale[:, None, None] * precond, 0.0)
        fresh = (base_cols - step_rate * step).astype(bf16)
        fresh = fresh.reshape(owned, nm, rows, cols).transpose(1, 0, 2, 3)
        fresh = jnp.broadcast_to(fresh[None], (nx,) + fresh.shape)
        fresh = fresh.reshape(nx * nm, owned, rows, cols)
        back = lax.all_to_all(fresh, ("x", "mp"), split_axis=0, concat_axis=0, tiled=True)
        back = back.reshape(nx, blocks, rows, cols)
        weights = jnp.take(back, owner_slot, axis=1)
        weights = weights.transpose(1, 2, 0, 3).reshape(blocks, rows, width)

        own_step = lax.dynamic_slice_in_dim(step, z * slab, slab, 2)
        new_momentum = beta_decay * momentum + own_step
        new_master = master - step_rate * new_momentum
        return (new_momentum, new_master, weights)

    return local


def solution(mesh):
    nm = mesh.shape["mp"]
    nz = 16 if mesh.shape["dp"] == 64 else mesh.shape["dp"] // 2
    nx = mesh.shape["dp"] // nz
    fine = Mesh(mesh.devices.reshape(nx, nz, nm), ("x", "z", "mp"))
    slab_spec = P("mp", None, ("x", "z"))
    return jax.shard_map(
        make_local(nx, nz, nm),
        mesh=fine,
        in_specs=(
            P(("x", "z"), None, "mp", None),
            P(),
            P(),
            P("mp", None, None),
            slab_spec,
            slab_spec,
            slab_spec,
        ),
        out_specs=(slab_spec, slab_spec, P(None, "mp", None)),
        check_vma=False,
    )
```

time: 635 us -> 188 us (0.30)
  blocking collectives: 365 us -> 28.3 us
  waiting for transfers between devices: 166 us -> 82 us
  starting transfers between devices: 75.3 us -> 45.2 us
    psum x2 -> x1, blocking collectives: 365 us -> 7.44 us  [local(): grad_sq, pre_sq = lax.psum(jnp.stack([grad_sq, pre_sq]), 'x')]
    all_gather x1, waiting for transfers between devices: 137 us -> 45.2 us  [local(): parts = lax.all_gather(mine, 'z', axis=0, tiled=False)]
    all_to_all x2 -> x4, starting transfers between devices: 75.3 us -> 45.2 us  [the longest x1 16.2 us: local(): lax.all_to_all(fresh, ('x', 'mp'), split_axis=0, concat_axis=0, tiled=True)]
    all_to_all x0 -> x1, blocking collectives: none -> 20.8 us  [local(): bands = lax.all_to_all(spread, 'z', split_axis=0, concat_axis=0, tiled=True)]
    all_to_all x2 -> x4, waiting for transfers between devices: 29.8 us -> 36.8 us  [the longest x1 16.3 us: local(): lax.all_to_all(fresh, ('x', 'mp'), split_axis=0, concat_axis=0, tiled=True)]
  transfers between devices with their start and end apart: 3 -> 5, of which waited for: 3 -> 4; matrix products, arithmetic and copies ran while one was open for 0% -> 2% of each run, Pallas kernels for 0% -> 0%
where the time goes in v1:
time: 188 us; the launch traced here: 187 us
  waiting for transfers between devices  82 us (44%)
  starting transfers between devices  45.2 us (24%)
  blocking collectives  28.3 us (15%)
  between operations  14.3 us (8%)
  local copies, waits for them, and re-layouts  8.38 us (4%)
  other arithmetic  6.32 us (3%)
  matrix products  2.01 us (1%)
    all_gather x1, waiting for transfers between devices, local(): parts = lax.all_gather(mine, 'z', axis=0, tiled=False)  45.2 us
    all_to_all x1, blocking collectives, local(): bands = lax.all_to_all(spread, 'z', split_axis=0, concat_axis=0, tiled=True)  20.8 us
    all_to_all x1, waiting for transfers between devices, local(): lax.all_to_all(fresh, ('x', 'mp'), split_axis=0, concat_axis=0, tiled=True)  16.3 us
    all_to_all x1, starting transfers between devices, local(): lax.all_to_all(fresh, ('x', 'mp'), split_axis=0, concat_axis=0, tiled=True)  16.2 us
    all_to_all x1, waiting for transfers between devices, local(): lax.all_to_all(send, ('x', 'mp'), split_axis=0, concat_axis=0, tiled=True)  16.1 us
    all_to_all x1, starting transfers between devices, local(): pieces = lax.all_to_all(part, 'z', split_axis=0, concat_axis=0, tiled=True)  13 us
    all_to_all x1, starting transfers between devices, local(): lax.all_to_all(send, ('x', 'mp'), split_axis=0, concat_axis=0, tiled=True)  10.6 us
    psum x1, blocking collectives, local(): grad_sq, pre_sq = lax.psum(jnp.stack([grad_sq, pre_sq]), 'x')  7.44 us
  transfers between devices with their start and end apart: 5, of which 4 were waited for; matrix products, arithmetic and copies ran while one was open for 2% of the time, Pallas kernels for 0%

profile of v1, /device:TPU:1, one launch (start us, length us, event | category | flops | bytes accessed | tf_op | source)
XLA Modules:
  0.0 186.6 jit_solution(11189169623683962072)
XLA Ops:
  7.2 0.9 select_reduce_fusion.1
  8.4 0.6 gather_fusion
  9.9 1.2 copy.36
  11.1 10.6 %all-to-all-start = ((bf16[32,2,64,128]{3,2,1,0:T(8,128)(2,1)}), bf16[32,2,64,128]{3,2,1,0:T(8,128)(2,1)S(1)}, u32[]{:S(2)}, u32[]{:S(2)}) async-start(bf16[32,2,64,128]{3,2,1,0:T(8,128)(2,1)} %bitcast.6), calls=%async_computation | async-start | bytes 2097152 | tf_op jit(solution)/shard_map/all_to_all | solution.py:55
  21.9 0.7 maximum_maximum_fusion
  22.6 16.1 %all-to-all-done = bf16[32,2,64,128]{3,2,1,0:T(8,128)(2,1)S(1)} async-done(((bf16[32,2,64,128]{3,2,1,0:T(8,128)(2,1)}), bf16[32,2,64,128]{3,2,1,0:T(8,128)(2,1)S(1)}, u32[]{:S(2)}, u32[]{:S(2)}) %all-to-all-start) | async-done | bytes 1048608 | tf_op jit(solution)/shard_map/all_to_all | solution.py:55
  38.9 0.8 pad_maximum_fusion
  39.8 13.0 %all-to-all-start.1 = ((f32[16,2,32,128]{3,2,1,0:T(8,128)}), f32[16,2,32,128]{3,2,1,0:T(8,128)S(1)}, u32[]{:S(2)}, u32[]{:S(2)}) async-start(f32[16,2,32,128]{3,2,1,0:T(8,128)} %bitcast.7), calls=%async_computation.1 | async-start | bytes 1048576 | tf_op jit(solution)/shard_map/all_to_all | solution.py:62
  52.8 0.6 copy-done.5
  53.4 0.7 copy-done.4
  54.4 45.2 %all-gather.3.cloned.1.call-done = bf16[128,8,512]{2,1,0:T(8,128)(2,1)} async-done(((bf16[8,8,512]{2,1,0:T(8,128)(2,1)}), bf16[128,8,512]{2,1,0:T(8,128)(2,1)}) %all-gather.3.cloned.1.call-update) | async-done | bytes 1048592 | tf_op jit(solution)/shard_map/all_gather | solution.py:45
  99.6 1.3 copy.53
  101.4 0.6 broadcast_in_dim.105
  102.0 5.4 %all-to-all-start.2 = ((bf16[4,2,32,128]{3,2,1,0:T(8,128)(2,1)}), bf16[4,2,32,128]{3,2,1,0:T(8,128)(2,1)S(1)}, u32[]{:S(2)}, u32[]{:S(2)}) async-start(bf16[4,2,32,128]{3,2,1,0:T(8,128)(2,1)} %broadcast_in_dim.105), calls=%async_computation.2 | async-start | bytes 131072 | tf_op jit(solution)/shard_map/all_to_all | solution.py:72
  107.5 4.4 %all-to-all-done.2 = bf16[4,2,32,128]{3,2,1,0:T(8,128)(2,1)S(1)} async-done(((bf16[4,2,32,128]{3,2,1,0:T(8,128)(2,1)}), bf16[4,2,32,128]{3,2,1,0:T(8,128)(2,1)S(1)}, u32[]{:S(2)}, u32[]{:S(2)}) %all-to-all-start.2) | async-done | bytes 65568 | tf_op jit(solution)/shard_map/all_to_all | solution.py:72
  112.2 20.8 %all_to_all.25 = bf16[16,80,128]{2,1,0:T(8,128)(2,1)S(1)} all-to-all(bf16[16,80,128]{2,1,0:T(8,128)(2,1)S(1)} %broadcast_in_dim.108), channel_id=1, replica_groups=mesh['x'=4,'z'=16,'mp'=8] {'z'}, dimensions={0} | all-to-all | bytes 655360 | tf_op jit(solution)/shard_map/all_to_all | solution.py:82
  133.4 1.8 multiply_reduce_fusion
  135.3 7.4 %psum.7 = f32[2,2]{1,0:T(2,128)S(1)} all-reduce(f32[2,2]{1,0:T(2,128)S(1)} %pad_maximum_fusion.3), channel_id=1, replica_groups=mesh['x'=4,'z'=16,'mp'=8] {'x'}, use_global_device_ids=true, to_apply=%region_7.8 | all-reduce | flops 4 | bytes 32 | tf_op jit(solution)/shard_map/psum | solution.py:89
  143.2 1.2 broadcast_in_dim.111
  144.4 16.2 %all-to-all-start.4 = ((bf16[32,2,64,128]{3,2,1,0:T(8,128)(2,1)}), bf16[32,2,64,128]{3,2,1,0:T(8,128)(2,1)S(1)}, u32[]{:S(2)}, u32[]{:S(2)}) async-start(bf16[32,2,64,128]{3,2,1,0:T(8,128)(2,1)} %bitcast.27), calls=%async_computation.4 | async-start | bytes 2097152 | tf_op jit(solution)/shard_map/all_to_all | solution.py:97
  160.7 0.6 multiply_subtract_fusion
  161.3 16.3 %all-to-all-done.4 = bf16[32,2,64,128]{3,2,1,0:T(8,128)(2,1)S(1)} async-done(((bf16[32,2,64,128]{3,2,1,0:T(8,128)(2,1)}), bf16[32,2,64,128]{3,2,1,0:T(8,128)(2,1)S(1)}, u32[]{:S(2)}, u32[]{:S(2)}) %all-to-all-start.4) | async-done | bytes 1048608 | tf_op jit(solution)/shard_map/all_to_all | solution.py:97
  177.7 0.7 gather_fusion.1
  178.4 1.3 copy_bitcast_fusion
  (55 shorter events, 3.5 us)
Async XLA Ops:
  7.2 1.2 copy-start
  11.1 10.7 %copy-start.1 = (f32[2,512,8]{1,2,0:T(8,128)S(1)}, f32[2,512,8]{1,2,0:T(8,128)}, u32[]{:S(2)}) copy-start(f32[2,512,8]{1,2,0:T(8,128)} %param.13) | copy-start | bytes 98308
  11.1 10.7 %copy-start.2 = (f32[2,512,8]{1,2,0:T(8,128)S(1)}, f32[2,512,8]{1,2,0:T(8,128)}, u32[]{:S(2)}) copy-start(f32[2,512,8]{1,2,0:T(8,128)} %param.12) | copy-start | bytes 98308
  11.1 10.8 %copy-start.3 = (bf16[2,512,8]{1,2,0:T(8,128)(2,1)S(1)}, bf16[2,512,8]{1,2,0:T(8,128)(2,1)}, u32[]{:S(2)}) copy-start(bf16[2,512,8]{1,2,0:T(8,128)(2,1)} %param.11) | copy-start | bytes 49156
  11.1 27.6 %all-to-all-start = ((bf16[32,2,64,128]{3,2,1,0:T(8,128)(2,1)}), bf16[32,2,64,128]{3,2,1,0:T(8,128)(2,1)S(1)}, u32[]{:S(2)}, u32[]{:S(2)}) async-start(bf16[32,2,64,128]{3,2,1,0:T(8,128)(2,1)} %bitcast.6), calls=%async_computation | async-start | bytes 2097152 | tf_op jit(solution)/shard_map/all_to_all | solution.py:55
  21.7 77.9 %all-gather.3.cloned.1.call-start = ((), (), s32[]{:S(2)}) async-start(), calls=%async_computation.5 | async-start | bytes 1114112 | tf_op jit(solution)/shard_map/all_gather | solution.py:45
  39.8 61.2 %all-to-all-start.1 = ((f32[16,2,32,128]{3,2,1,0:T(8,128)}), f32[16,2,32,128]{3,2,1,0:T(8,128)S(1)}, u32[]{:S(2)}, u32[]{:S(2)}) async-start(f32[16,2,32,128]{3,2,1,0:T(8,128)} %bitcast.7), calls=%async_computation.1 | async-start | bytes 1048576 | tf_op jit(solution)/shard_map/all_to_all | solution.py:62
  52.7 0.7 copy-start.5
  53.4 0.7 copy-start.4
  102.0 9.9 %all-to-all-start.2 = ((bf16[4,2,32,128]{3,2,1,0:T(8,128)(2,1)}), bf16[4,2,32,128]{3,2,1,0:T(8,128)(2,1)S(1)}, u32[]{:S(2)}, u32[]{:S(2)}) async-start(bf16[4,2,32,128]{3,2,1,0:T(8,128)(2,1)} %broadcast_in_dim.105), calls=%async_computation.2 | async-start | bytes 131072 | tf_op jit(solution)/shard_map/all_to_all | solution.py:72
  144.4 33.2 %all-to-all-start.4 = ((bf16[32,2,64,128]{3,2,1,0:T(8,128)(2,1)}), bf16[32,2,64,128]{3,2,1,0:T(8,128)(2,1)S(1)}, u32[]{:S(2)}, u32[]{:S(2)}) async-start(bf16[32,2,64,128]{3,2,1,0:T(8,128)(2,1)} %bitcast.27), calls=%async_computation.4 | async-start | bytes 2097152 | tf_op jit(solution)/shard_map/all_to_all | solution.py:97
Sparse Core Ops, SparseCore 0:
  24.6 74.9 all-gather.2

commit v2 on v1

v2 whole, which is shorter than its diff:
```python
import jax
import jax.numpy as jnp
from jax import lax
from jax.sharding import Mesh, PartitionSpec as P

epsilon = 1e-06
beta_decay = 0.9
step_rate = 0.5
f32 = jnp.float32
bf16 = jnp.bfloat16


def split_low(value):
    high = lax.reduce_precision(value, 8, 7)
    return high.astype(bf16), (value - high).astype(bf16)


def exchange(value, axes):
    return lax.all_to_all(value, axes, split_axis=0, concat_axis=0, tiled=True)


def spread(value, count):
    return jnp.broadcast_to(value[None], (count,) + value.shape)


def make_local(nx, nzh, nzl, nm):
    ng = nx * nzl
    group = ("x", "zl")
    wide = ("x", "zl", "mp")

    def gather_along(value):
        zh = lax.axis_index("zh")
        held = value[None]
        stride = nzh // 2
        while stride:
            pairs = [(i, i ^ stride) for i in range(nzh)]
            other = lax.ppermute(held, "zh", pairs)
            first = (zh & stride) == 0
            low = jnp.where(first, held, other)
            high = jnp.where(first, other, held)
            held = jnp.stack([low, high], axis=1).reshape((-1,) + value.shape)
            stride //= 2
        return held

    def local(partial_grads, owner_slot, extent, left_roots, right_roots, momentum, master):
        blocks = partial_grads.shape[1]
        rows = partial_grads.shape[2]
        width = partial_grads.shape[3]
        owned = left_roots.shape[0]
        slab = right_roots.shape[2]
        cols = width // nx
        half = rows // nzl
        mine_cols = slab * nzh
        x, zh, zl, m = (lax.axis_index(a) for a in ("x", "zh", "zl", "mp"))
        slots = jnp.arange(blocks, dtype=jnp.int32)
        match = owner_slot[None, :] == slots[:, None]
        order = jnp.sum(jnp.where(match, slots[None, :], 0), axis=1)
        bounds_all = jnp.sum(jnp.where(match[:, :, None], extent[None, :, :], 0), axis=1)
        bounds = lax.dynamic_slice_in_dim(bounds_all, m * owned, owned, 0)

        base_t = jnp.swapaxes(master - (step_rate * beta_decay) * momentum, 1, 2)
        high, low = split_low(base_t)
        right_t = jnp.swapaxes(right_roots, 1, 2)
        mine = jnp.concatenate([right_t, high, low], axis=0)
        parts = gather_along(mine)
        parts = jnp.swapaxes(parts, 0, 1).reshape(3 * owned, mine_cols, width)
        right_cols_t = parts[:owned]
        base_cols = parts[owned : 2 * owned].astype(f32) + parts[2 * owned :].astype(f32)
        base_cols = base_cols.reshape(owned * mine_cols, width).T

        send = jnp.take(partial_grads[0], order, axis=0)
        send = send.reshape(nm, owned, nzl, half, nx, cols).transpose(4, 2, 0, 1, 3, 5)
        got = exchange(send.reshape(ng * nm, owned, half, cols), wide)
        got = got.reshape(ng, nm, owned, half, cols)
        part = got[0].astype(f32)
        for i in range(1, ng):
            part = part + got[i].astype(f32)
        pieces = exchange(part, "zh")
        total = jnp.sum(pieces, axis=0)
        piece_rows = zh * rows + zl * half + jnp.arange(half, dtype=jnp.int32)
        piece_cols = x * cols + jnp.arange(cols, dtype=jnp.int32)
        row_ok = piece_rows[None, :, None] < bounds[:, 0][:, None, None]
        col_ok = piece_cols[None, None, :] < bounds[:, 1][:, None, None]
        grad = jnp.where(row_ok & col_ok, total, 0.0)
        sq_piece = jnp.sum(grad * grad, axis=(1, 2))
        all_cols = exchange(spread(grad.astype(bf16), ng), group)
        all_cols = all_cols.reshape(nx, nzl, owned, half, cols)
        grad_rows = all_cols.transpose(2, 1, 3, 0, 4).reshape(owned, rows, width)
        right_side = jnp.einsum(
            "kij,kcj->ikc", grad_rows, right_cols_t, preferred_element_type=f32
        ).astype(bf16)
        sq_high = lax.reduce_precision(sq_piece, 8, 7)
        sq_middle = lax.reduce_precision(sq_piece - sq_high, 8, 7)
        sq_low = sq_piece - sq_high - sq_middle
        extra = jnp.concatenate([sq_high, sq_middle, sq_low]).astype(bf16)
        extra = jnp.broadcast_to(extra[:, None], (3 * owned, owned * mine_cols))
        extra = jnp.pad(extra, ((0, 16 - 3 * owned), (0, 0)))
        packed = jnp.concatenate([right_side.reshape(rows, owned * mine_cols), extra], axis=0)
        bands = exchange(spread(packed, nzh), "zh")
        sq = bands[:, rows : rows + 3 * owned, 0].astype(f32)
        grad_sq = jnp.sum(sq.reshape(nzh, 3, owned), axis=(0, 1))
        side = bands[:, :rows].reshape(width, owned, mine_cols)
        precond = jnp.einsum("kij,jkc->ikc", left_roots, side, preferred_element_type=f32)
        pre_sq = jnp.sum(precond * precond, axis=(0, 2))
        sums = jnp.concatenate([grad_sq, pre_sq])
        sums = jnp.broadcast_to(sums[:, None], (2 * owned, 128))
        sums = jnp.pad(sums, ((0, 8 - 2 * owned), (0, 0)))
        sums = jnp.sum(exchange(spread(sums, ng), group), axis=0)[: 2 * owned, 0]
        grad_sq, pre_sq = sums[:owned], sums[owned:]
        scale = jnp.sqrt(grad_sq / (pre_sq + epsilon))
        all_rows = jnp.arange(width, dtype=jnp.int32)
        c = jnp.arange(mine_cols, dtype=jnp.int32)
        own_cols = x * cols + (c // slab) * (slab * nzl) + zl * slab + c % slab
        mask = (all_rows[:, None, None] < bounds[:, 0][None, :, None]) & (
            own_cols[None, None, :] < bounds[:, 1][None, :, None]
        )
        step = jnp.where(mask, scale[None, :, None] * precond, 0.0)
        fresh = (base_cols - step_rate * step.reshape(width, owned * mine_cols)).astype(bf16)
        fresh = spread(fresh.reshape(nm, rows, owned * mine_cols), ng)
        back = exchange(fresh.reshape(ng * nm, rows, owned * mine_cols), wide)
        back = back.reshape(nx, nzl, nm, rows, owned * mine_cols)
        lane = jnp.arange(owned * mine_cols, dtype=jnp.int32)
        s_in, c_in = lane // mine_cols, lane % mine_cols
        to = s_in * cols + (c_in // slab) * (slab * nzl) + c_in % slab
        to = jnp.arange(nzl, dtype=jnp.int32)[:, None] * slab + to[None, :]
        place = (to[:, :, None] == jnp.arange(owned * cols, dtype=jnp.int32)).astype(bf16)
        spread_out = jnp.einsum(
            "xzmrl,zln->mrxn", back, place, preferred_element_type=f32
        ).astype(bf16)
        spread_out = spread_out.reshape(nm, rows, nx, owned, cols).transpose(0, 3, 1, 2, 4)
        weights = jnp.take(spread_out.reshape(blocks, rows, width), owner_slot, axis=0)

        own_step = lax.dynamic_slice_in_dim(step, zh * slab, slab, 2).transpose(1, 0, 2)
        new_momentum = beta_decay * momentum + own_step
        new_master = master - step_rate * new_momentum
        return (new_momentum, new_master, weights)

    return local


def solution(mesh):
    nm = mesh.shape["mp"]
    nzl, nzh = 2, nm
    nx = mesh.shape["dp"] // (nzl * nzh)
    fine = Mesh(mesh.devices.reshape(nx, nzh, nzl, nm), ("x", "zh", "zl", "mp"))
    dp = ("x", "zh", "zl")
    slab_spec = P("mp", None, dp)
    return jax.shard_map(
        make_local(nx, nzh, nzl, nm),
        mesh=fine,
        in_specs=(
            P(dp, None, "mp", None),
            P(),
            P(),
            P("mp", None, None),
            slab_spec,
            slab_spec,
            slab_spec,
        ),
        out_specs=(slab_spec, slab_spec, P(None, "mp", None)),
        check_vma=False,
    )
```

time: 188 us -> 158 us (0.84)
  blocking collectives: 28.3 us -> 0 us
  starting transfers between devices: 45.2 us -> 61.7 us
  between operations: 14.3 us -> 1.02 us
  waiting for transfers between devices: 82 us -> 76.6 us
  local copies, waits for them, and re-layouts: 8.38 us -> 10.4 us
    all_gather x1 -> x0, waiting for transfers between devices: 45.2 us -> none  [local(): parts = lax.all_gather(mine, 'z', axis=0, tiled=False)]
    ppermute x0 -> x3, waiting for transfers between devices: none -> 35.8 us  [gather_along(): other = lax.ppermute(held, 'zh', pairs)]
    all_to_all x1 -> x0, blocking collectives: 20.8 us -> none  [local(): bands = lax.all_to_all(spread, 'z', split_axis=0, concat_axis=0, tiled=True)]
    ppermute x0 -> x3, starting transfers between devices: none -> 17.8 us  [gather_along(): other = lax.ppermute(held, 'zh', pairs)]
    psum x1 -> x0, blocking collectives: 7.44 us -> none  [local(): grad_sq, pre_sq = lax.psum(jnp.stack([grad_sq, pre_sq]), 'x')]
    all_to_all x4 -> x6, waiting for transfers between devices: 36.8 us -> 40.9 us  [exchange(): return lax.all_to_all(value, axes, split_axis=0, concat_axis=0, tiled=True)]
    reshape x0 -> x6, local copies, waits for them, and re-layouts: none -> 4.02 us  [the longest x2 2.08 us: local(): spread_out.reshape(nm, rows, nx, owned, cols).transpose(0, 3, 1, 2, 4)]
    all_to_all x4 -> x6, starting transfers between devices: 45.2 us -> 43.9 us  [exchange(): return lax.all_to_all(value, axes, split_axis=0, concat_axis=0, tiled=True)]
  transfers between devices with their start and end apart: 5 -> 9, of which waited for: 4 -> 7; matrix products, arithmetic and copies ran while one was open for 2% -> 2% of each run, Pallas kernels for 0% -> 0%
where the time goes in v2:
time: 158 us
  waiting for transfers between devices  76.6 us (48%)
  starting transfers between devices  61.7 us (39%)
  local copies, waits for them, and re-layouts  10.4 us (7%)
  other arithmetic  6.62 us (4%)
    all_to_all x6, starting transfers between devices, exchange(): return lax.all_to_all(value, axes, split_axis=0, concat_axis=0, tiled=True)  43.9 us
    all_to_all x6, waiting for transfers between devices, exchange(): return lax.all_to_all(value, axes, split_axis=0, concat_axis=0, tiled=True)  40.9 us
    ppermute x3, waiting for transfers between devices, gather_along(): other = lax.ppermute(held, 'zh', pairs)  35.8 us
    ppermute x3, starting transfers between devices, gather_along(): other = lax.ppermute(held, 'zh', pairs)  17.8 us
    broadcast_in_dim x4, local copies, waits for them, and re-layouts, spread(): return jnp.broadcast_to(value[None], (count,) + value.shape)  3.3 us
  transfers between devices with their start and end apart: 9, of which 7 were waited for; matrix products, arithmetic and copies ran while one was open for 2% of the time, Pallas kernels for 0%

profile of v2, /device:TPU:1, one launch (start us, length us, event | category | flops | bytes accessed | tf_op | source)
XLA Modules:
  0.0 157.6 jit_solution(12322174234568539416)
XLA Ops:
  0.6 0.9 select_reduce_fusion.1
  3.9 1.2 copy.56
  5.2 11.1 %all-to-all-start = ((bf16[64,2,32,128]{3,2,1,0:T(8,128)(2,1)}), bf16[64,2,32,128]{3,2,1,0:T(8,128)(2,1)S(1)}, u32[]{:S(2)}, u32[]{:S(2)}) async-start(bf16[64,2,32,128]{3,2,1,0:T(8,128)(2,1)} %bitcast.19), calls=%async_computation | async-start | bytes 2097152 | tf_op jit(solution)/shard_map/all_to_all | solution.py:19
  16.4 13.9 %collective-permute-start = (bf16[1,6,8,512]{3,2,1,0:T(8,128)(2,1)S(1)}, bf16[1,6,8,512]{3,2,1,0:T(8,128)(2,1)S(1)}, u32[]{:S(2)}, u32[]{:S(2)}) collective-permute-start(bf16[1,6,8,512]{3,2,1,0:T(8,128)(2,1)S(1)} %maximum_bitcast_fusion.1), channel_id=1, source_target_pairs={{0,64},{16,80},{32,96},{48,112},{64,0},{80,16},{96,32},{112,48},{1... | collective-permute-start | bytes 147464 | tf_op jit(solution)/shard_map/ppermute | solution.py:37
  30.6 12.7 %collective-permute-done = bf16[1,6,8,512]{3,2,1,0:T(8,128)(2,1)S(1)} collective-permute-done((bf16[1,6,8,512]{3,2,1,0:T(8,128)(2,1)S(1)}, bf16[1,6,8,512]{3,2,1,0:T(8,128)(2,1)S(1)}, u32[]{:S(2)}, u32[]{:S(2)}) %collective-permute-start) | collective-permute-done | bytes 49184 | tf_op jit(solution)/shard_map/ppermute | solution.py:37
  43.4 1.9 %collective-permute-start.1 = (bf16[2,6,8,512]{3,2,1,0:T(8,128)(2,1)S(1)}, bf16[2,6,8,512]{3,2,1,0:T(8,128)(2,1)S(1)}, u32[]{:S(2)}, u32[]{:S(2)}) collective-permute-start(bf16[2,6,8,512]{3,2,1,0:T(8,128)(2,1)S(1)} %maximum_bitcast_fusion), channel_id=1, source_target_pairs={{0,32},{16,48},{32,0},{48,16},{64,96},{80,112},{96,64},{112,80},{1... | collective-permute-start | bytes 294920 | tf_op jit(solution)/shard_map/ppermute | solution.py:37
  45.3 0.9 convert_add_fusion.1
  46.2 7.7 %all-to-all-start.1 = ((f32[8,2,32,128]{3,2,1,0:T(8,128)}), f32[8,2,32,128]{3,2,1,0:T(8,128)S(1)}, u32[]{:S(2)}, u32[]{:S(2)}) async-start(f32[8,2,32,128]{3,2,1,0:T(8,128)} %convert_add_fusion.1), calls=%async_computation.1 | async-start | bytes 524288 | tf_op jit(solution)/shard_map/all_to_all | solution.py:19
  53.9 5.4 %collective-permute-done.1 = bf16[2,6,8,512]{3,2,1,0:T(8,128)(2,1)S(1)} collective-permute-done((bf16[2,6,8,512]{3,2,1,0:T(8,128)(2,1)S(1)}, bf16[2,6,8,512]{3,2,1,0:T(8,128)(2,1)S(1)}, u32[]{:S(2)}, u32[]{:S(2)}) %collective-permute-start.1) | collective-permute-done | bytes 98336 | tf_op jit(solution)/shard_map/ppermute | solution.py:37
  59.4 1.9 %collective-permute-start.2 = (bf16[4,6,8,512]{3,2,1,0:T(8,128)(2,1)S(1)}, bf16[4,6,8,512]{3,2,1,0:T(8,128)(2,1)S(1)}, u32[]{:S(2)}, u32[]{:S(2)}) collective-permute-start(bf16[4,6,8,512]{3,2,1,0:T(8,128)(2,1)S(1)} %bitcast.101), channel_id=1, source_target_pairs={{0,16},{16,0},{32,48},{48,32},{64,80},{80,64},{96,112},{112,96},{1... | collective-permute-start | bytes 589832 | tf_op jit(solution)/shard_map/ppermute | solution.py:37
  61.4 17.6 %collective-permute-done.2 = bf16[4,6,8,512]{3,2,1,0:T(8,128)(2,1)S(1)} collective-permute-done((bf16[4,6,8,512]{3,2,1,0:T(8,128)(2,1)S(1)}, bf16[4,6,8,512]{3,2,1,0:T(8,128)(2,1)S(1)}, u32[]{:S(2)}, u32[]{:S(2)}) %collective-permute-start.2) | collective-permute-done | bytes 196640 | tf_op jit(solution)/shard_map/ppermute | solution.py:37
  79.8 4.1 %all-to-all-start.2 = ((bf16[8,2,32,128]{3,2,1,0:T(8,128)(2,1)}), bf16[8,2,32,128]{3,2,1,0:T(8,128)(2,1)S(1)}, u32[]{:S(2)}, u32[]{:S(2)}) async-start(bf16[8,2,32,128]{3,2,1,0:T(8,128)(2,1)} %broadcast_in_dim.68), calls=%async_computation.2 | async-start | bytes 262144 | tf_op jit(solution)/shard_map/all_to_all | solution.py:19
  84.4 5.2 %all-to-all-done.2 = bf16[8,2,32,128]{3,2,1,0:T(8,128)(2,1)S(1)} async-done(((bf16[8,2,32,128]{3,2,1,0:T(8,128)(2,1)}), bf16[8,2,32,128]{3,2,1,0:T(8,128)(2,1)S(1)}, u32[]{:S(2)}, u32[]{:S(2)}) %all-to-all-start.2) | async-done | bytes 131104 | tf_op jit(solution)/shard_map/all_to_all | solution.py:19
  90.0 0.7 broadcast_in_dim.69
  90.7 6.7 %all-to-all-start.3 = ((bf16[8,80,128]{2,1,0:T(8,128)(2,1)}), bf16[8,80,128]{2,1,0:T(8,128)(2,1)S(1)}, u32[]{:S(2)}, u32[]{:S(2)}) async-start(bf16[8,80,128]{2,1,0:T(8,128)(2,1)} %broadcast_in_dim.69), calls=%async_computation.3 | async-start | bytes 327680 | tf_op jit(solution)/shard_map/all_to_all | solution.py:19
  97.6 13.5 %all-to-all-done.3 = bf16[8,80,128]{2,1,0:T(8,128)(2,1)S(1)} async-done(((bf16[8,80,128]{2,1,0:T(8,128)(2,1)}), bf16[8,80,128]{2,1,0:T(8,128)(2,1)S(1)}, u32[]{:S(2)}, u32[]{:S(2)}) %all-to-all-start.3) | async-done | bytes 163872 | tf_op jit(solution)/shard_map/all_to_all | solution.py:19
  112.8 3.3 %all-to-all-start.4 = ((f32[8,8,128]{2,1,0:T(8,128)}), f32[8,8,128]{2,1,0:T(8,128)S(1)}, u32[]{:S(2)}, u32[]{:S(2)}) async-start(f32[8,8,128]{2,1,0:T(8,128)} %broadcast_in_dim.108), calls=%async_computation.4 | async-start | bytes 65536 | tf_op jit(solution)/shard_map/all_to_all | solution.py:19
  116.3 5.0 %all-to-all-done.4 = f32[8,8,128]{2,1,0:T(8,128)S(1)} async-done(((f32[8,8,128]{2,1,0:T(8,128)}), f32[8,8,128]{2,1,0:T(8,128)S(1)}, u32[]{:S(2)}, u32[]{:S(2)}) %all-to-all-start.4) | async-done | bytes 32800 | tf_op jit(solution)/shard_map/all_to_all | solution.py:19
  121.7 1.2 broadcast_in_dim.111
  122.9 10.9 %all-to-all-start.5 = ((bf16[64,64,128]{2,1,0:T(8,128)(2,1)}), bf16[64,64,128]{2,1,0:T(8,128)(2,1)S(1)}, u32[]{:S(2)}, u32[]{:S(2)}) async-start(bf16[64,64,128]{2,1,0:T(8,128)(2,1)} %bitcast.33), calls=%async_computation.5 | async-start | bytes 2097152 | tf_op jit(solution)/shard_map/all_to_all | solution.py:19
  134.6 17.2 %all-to-all-done.5 = bf16[64,64,128]{2,1,0:T(8,128)(2,1)S(1)} async-done(((bf16[64,64,128]{2,1,0:T(8,128)(2,1)}), bf16[64,64,128]{2,1,0:T(8,128)(2,1)S(1)}, u32[]{:S(2)}, u32[]{:S(2)}) %all-to-all-start.5) | async-done | bytes 1048608 | tf_op jit(solution)/shard_map/all_to_all | solution.py:19
  152.6 1.8 %copy.76 = bf16[8,64,4,2,128]{4,2,1,3,0:T(4,128)(2,1)} copy(bf16[8,64,4,2,128]{4,3,1,0,2:T(2,128)(2,1)S(1)} %reshape.395) | data formatting | bytes 2097152 | tf_op jit(solution)/shard_map/reshape | solution.py:130
  154.4 1.5 reshape.396
  156.5 1.1 broadcast_select_fusion
  (77 shorter events, 9.0 us)
Async XLA Ops:
  0.6 2.2 %copy-start = (bf16[1,16,64,512]{3,2,1,0:T(8,128)(2,1)S(1)}, bf16[1,16,64,512]{3,2,1,0:T(8,128)(2,1)}, u32[]{:S(2)}) copy-start(bf16[1,16,64,512]{3,2,1,0:T(8,128)(2,1)} %param.9) | copy-start | bytes 3145732
  5.2 11.1 %copy-start.2 = (f32[2,512,8]{1,2,0:T(8,128)S(1)}, f32[2,512,8]{1,2,0:T(8,128)}, u32[]{:S(2)}) copy-start(f32[2,512,8]{1,2,0:T(8,128)} %param.15) | copy-start | bytes 98308
  5.2 11.2 %copy-start.3 = (f32[2,512,8]{1,2,0:T(8,128)S(1)}, f32[2,512,8]{1,2,0:T(8,128)}, u32[]{:S(2)}) copy-start(f32[2,512,8]{1,2,0:T(8,128)} %param.14) | copy-start | bytes 98308
  5.2 11.2 %copy-start.4 = (bf16[2,512,8]{1,2,0:T(8,128)(2,1)S(1)}, bf16[2,512,8]{1,2,0:T(8,128)(2,1)}, u32[]{:S(2)}) copy-start(bf16[2,512,8]{1,2,0:T(8,128)(2,1)} %param.13) | copy-start | bytes 49156
  5.2 25.2 %copy-start.5 = (s32[16]{0:T(128)S(1)}, s32[16]{0:T(128)}, u32[]{:S(2)}) copy-start(s32[16]{0:T(128)} %param.10) | copy-start | bytes 196
  5.2 25.2 %copy-start.6 = (s32[16,2]{0,1:T(2,128)S(1)}, s32[16,2]{0,1:T(2,128)}, u32[]{:S(2)}) copy-start(s32[16,2]{0,1:T(2,128)} %param.11) | copy-start | bytes 388
  5.2 40.1 %all-to-all-start = ((bf16[64,2,32,128]{3,2,1,0:T(8,128)(2,1)}), bf16[64,2,32,128]{3,2,1,0:T(8,128)(2,1)S(1)}, u32[]{:S(2)}, u32[]{:S(2)}) async-start(bf16[64,2,32,128]{3,2,1,0:T(8,128)(2,1)} %bitcast.19), calls=%async_computation | async-start | bytes 2097152 | tf_op jit(solution)/shard_map/all_to_all | solution.py:19
  16.4 27.0 %collective-permute-start = (bf16[1,6,8,512]{3,2,1,0:T(8,128)(2,1)S(1)}, bf16[1,6,8,512]{3,2,1,0:T(8,128)(2,1)S(1)}, u32[]{:S(2)}, u32[]{:S(2)}) collective-permute-start(bf16[1,6,8,512]{3,2,1,0:T(8,128)(2,1)S(1)} %maximum_bitcast_fusion.1), channel_id=1, source_target_pairs={{0,64},{16,80},{32,96},{48,112},{64,0},{80,16},{96,32},{112,48},{1... | collective-permute-start | bytes 147464 | tf_op jit(solution)/shard_map/ppermute | solution.py:37
  43.4 15.9 %collective-permute-start.1 = (bf16[2,6,8,512]{3,2,1,0:T(8,128)(2,1)S(1)}, bf16[2,6,8,512]{3,2,1,0:T(8,128)(2,1)S(1)}, u32[]{:S(2)}, u32[]{:S(2)}) collective-permute-start(bf16[2,6,8,512]{3,2,1,0:T(8,128)(2,1)S(1)} %maximum_bitcast_fusion), channel_id=1, source_target_pairs={{0,32},{16,48},{32,0},{48,16},{64,96},{80,112},{96,64},{112,80},{1... | collective-permute-start | bytes 294920 | tf_op jit(solution)/shard_map/ppermute | solution.py:37
  46.2 32.8 %all-to-all-start.1 = ((f32[8,2,32,128]{3,2,1,0:T(8,128)}), f32[8,2,32,128]{3,2,1,0:T(8,128)S(1)}, u32[]{:S(2)}, u32[]{:S(2)}) async-start(f32[8,2,32,128]{3,2,1,0:T(8,128)} %convert_add_fusion.1), calls=%async_computation.1 | async-start | bytes 524288 | tf_op jit(solution)/shard_map/all_to_all | solution.py:19
  59.4 19.6 %collective-permute-start.2 = (bf16[4,6,8,512]{3,2,1,0:T(8,128)(2,1)S(1)}, bf16[4,6,8,512]{3,2,1,0:T(8,128)(2,1)S(1)}, u32[]{:S(2)}, u32[]{:S(2)}) collective-permute-start(bf16[4,6,8,512]{3,2,1,0:T(8,128)(2,1)S(1)} %bitcast.101), channel_id=1, source_target_pairs={{0,16},{16,0},{32,48},{48,32},{64,80},{80,64},{96,112},{112,96},{1... | collective-permute-start | bytes 589832 | tf_op jit(solution)/shard_map/ppermute | solution.py:37
  79.8 9.7 %all-to-all-start.2 = ((bf16[8,2,32,128]{3,2,1,0:T(8,128)(2,1)}), bf16[8,2,32,128]{3,2,1,0:T(8,128)(2,1)S(1)}, u32[]{:S(2)}, u32[]{:S(2)}) async-start(bf16[8,2,32,128]{3,2,1,0:T(8,128)(2,1)} %broadcast_in_dim.68), calls=%async_computation.2 | async-start | bytes 262144 | tf_op jit(solution)/shard_map/all_to_all | solution.py:19
  89.5 22.0 %copy-start.1 = (bf16[2,512,512]{2,1,0:T(8,128)(2,1)S(1)}, bf16[2,512,512]{2,1,0:T(8,128)(2,1)}, u32[]{:S(2)}) copy-start(bf16[2,512,512]{2,1,0:T(8,128)(2,1)} %param.12) | copy-start | bytes 3145732
  90.7 20.4 %all-to-all-start.3 = ((bf16[8,80,128]{2,1,0:T(8,128)(2,1)}), bf16[8,80,128]{2,1,0:T(8,128)(2,1)S(1)}, u32[]{:S(2)}, u32[]{:S(2)}) async-start(bf16[8,80,128]{2,1,0:T(8,128)(2,1)} %broadcast_in_dim.69), calls=%async_computation.3 | async-start | bytes 327680 | tf_op jit(solution)/shard_map/all_to_all | solution.py:19
  112.8 8.4 %all-to-all-start.4 = ((f32[8,8,128]{2,1,0:T(8,128)}), f32[8,8,128]{2,1,0:T(8,128)S(1)}, u32[]{:S(2)}, u32[]{:S(2)}) async-start(f32[8,8,128]{2,1,0:T(8,128)} %broadcast_in_dim.108), calls=%async_computation.4 | async-start | bytes 65536 | tf_op jit(solution)/shard_map/all_to_all | solution.py:19
  122.9 28.9 %all-to-all-start.5 = ((bf16[64,64,128]{2,1,0:T(8,128)(2,1)}), bf16[64,64,128]{2,1,0:T(8,128)(2,1)S(1)}, u32[]{:S(2)}, u32[]{:S(2)}) async-start(bf16[64,64,128]{2,1,0:T(8,128)(2,1)} %bitcast.33), calls=%async_computation.5 | async-start | bytes 2097152 | tf_op jit(solution)/shard_map/all_to_all | solution.py:19

commit v3 on v2

v3 whole, which is shorter than its diff:
```python
import functools

import jax
import jax.numpy as jnp
from jax import lax
from jax.experimental import pallas as pl
from jax.experimental.pallas import tpu as pltpu
from jax.sharding import Mesh, PartitionSpec as P

epsilon = 1e-06
beta_decay = 0.9
step_rate = 0.5
f32 = jnp.float32
bf16 = jnp.bfloat16
in_vmem = pl.BlockSpec(memory_space=pltpu.VMEM)
in_smem = pl.BlockSpec(memory_space=pltpu.SMEM)
params = pltpu.CompilerParams(vmem_limit_bytes=24 * 2**20)


def exchange(value, axes):
    return lax.all_to_all(value, axes, split_axis=0, concat_axis=0, tiled=True)


def bounds_of(slot, owner_ref, extent_ref):
    height, width = jnp.int32(0), jnp.int32(0)
    for b in range(owner_ref.shape[0]):
        hit = owner_ref[b] == slot
        height = jnp.where(hit, extent_ref[b, 0], height)
        width = jnp.where(hit, extent_ref[b, 1], width)
    return height, width


def iota(shape, dim):
    return lax.broadcasted_iota(jnp.int32, shape, dim)


def send_kernel(nx, nm, owned, owner_ref, grads_ref, out_ref):
    blocks, rows, width = grads_ref.shape
    cols = width // nx
    for b in range(blocks):
        slot = owner_ref[b]
        owner, place = slot // owned, slot % owned
        for x in range(nx):
            out_ref[(x * owned + place) * nm + owner] = grads_ref[b, :, x * cols : (x + 1) * cols]


def grad_kernel(owned, owner_ref, extent_ref, pieces_ref, out_ref, sq_ref):
    _, rows, cols = pieces_ref.shape
    x, zh = lax.axis_index("x"), lax.axis_index("zh")
    zl, m = lax.axis_index("zl"), lax.axis_index("mp")
    height, width = bounds_of(m * owned + zl, owner_ref, extent_ref)
    total = pieces_ref[0]
    for i in range(1, pieces_ref.shape[0]):
        total = total + pieces_ref[i]
    ok = (zh * rows + iota((rows, cols), 0) < height) & (x * cols + iota((rows, cols), 1) < width)
    grad = jnp.where(ok, total, 0.0)
    sq_ref[...] = jnp.broadcast_to(jnp.sum(grad * grad, axis=0, keepdims=True), sq_ref.shape)
    low = grad.astype(bf16)
    for i in range(out_ref.shape[0]):
        out_ref[i] = low


def side_kernel(nx, owned, cols_ref, roots_ref, sq_ref, high_ref, low_ref, out_ref):
    nzh, height, lanes = out_ref.shape
    rows = cols_ref.shape[1]
    mine = roots_ref.shape[1]
    parts = []
    for s in range(owned):
        acc = jnp.zeros((rows, mine), f32)
        for x in range(nx):
            acc = acc + lax.dot_general(
                cols_ref[x * owned + s],
                roots_ref[s, :, x * lanes : (x + 1) * lanes],
                (((1,), (1,)), ((), ())),
                preferred_element_type=f32,
            )
        parts.append(acc)
    right = jnp.concatenate(parts, axis=1).astype(bf16)
    sq = sq_ref[...]
    first = sq.astype(bf16).astype(f32)
    second = (sq - first).astype(bf16).astype(f32)
    third = sq - first - second
    row = iota(sq.shape, 0)
    extra = jnp.where(row == 0, first, jnp.where(row == 1, second, jnp.where(row == 2, third, 0.0)))
    extra = jnp.concatenate([extra, jnp.zeros_like(extra)], axis=0).astype(bf16)
    for i in range(nzh):
        out_ref[i, :rows] = right
        out_ref[i, rows : rows + 16] = extra
        at = rows + 16
        for part_ref in (high_ref, low_ref):
            for x in range(nx):
                out_ref[i, at : at + 16] = part_ref[:, x * lanes : (x + 1) * lanes]
                at += 16


def left_kernel(nx, bands_ref, left_ref, precond_ref, base_ref, sums_ref, flip_ref):
    nzh, _, lanes = bands_ref.shape
    owned, width, _ = left_ref.shape
    rows = width // nzh
    mine = lanes // owned
    slab = mine // nzh
    side = bands_ref[:, :rows, :].reshape(width, lanes)
    lane = iota((width, lanes), 1)
    precond = jnp.zeros((width, lanes), f32)
    for s in range(owned):
        part = jnp.dot(left_ref[s], side, preferred_element_type=f32)
        precond = jnp.where(lane // mine == s, part, precond)
    precond_ref[...] = precond
    pre_sq = jnp.sum(precond * precond, axis=0, keepdims=True)
    extra = jnp.sum(bands_ref[:, rows : rows + 16, :].astype(f32), axis=0)
    grad_sq = jnp.sum(extra[:8], axis=0, keepdims=True)
    row = iota((8, lanes), 0)
    sums = jnp.where(row == 0, grad_sq, jnp.where(row == 1, pre_sq, 0.0))
    for i in range(sums_ref.shape[0]):
        sums_ref[i] = sums
    step = owned * slab
    for zh in range(nzh):
        for x in range(nx):
            at = rows + 16 + x * step
            value = bands_ref[zh, at : at + step, :].astype(f32)
            at = at + nx * step
            value = value + bands_ref[zh, at : at + step, :].astype(f32)
            for s in range(owned):
                flip_ref[s * mine + zh * slab : s * mine + (zh + 1) * slab, x * lanes : (x + 1) * lanes] = (
                    value[s * slab : (s + 1) * slab]
                )
    base_ref[...] = flip_ref[...].T


def fresh_kernel(
    nm, owned, slab, owner_ref, extent_ref, sums_ref, precond_ref, base_ref, out_ref, step_ref
):
    width, lanes = precond_ref.shape
    mine = lanes // owned
    ng = sums_ref.shape[0]
    nzl = owned
    x, zl, m = lax.axis_index("x"), lax.axis_index("zl"), lax.axis_index("mp")
    lane = iota((1, lanes), 1)
    place = lane // mine
    c = lane % mine
    column = x * lanes + (c // slab) * (slab * nzl) + zl * slab + c % slab
    scale = jnp.zeros((1, lanes), f32)
    height = jnp.zeros((1, lanes), jnp.int32)
    total = jnp.sum(sums_ref[...], axis=0)
    for s in range(owned):
        grad_rows = sums_ref[s]
        for g in range(s + nzl, ng, nzl):
            grad_rows = grad_rows + sums_ref[g]
        grad_sq = jnp.sum(grad_rows[0:1], axis=1, keepdims=True)
        pre_sq = jnp.sum(jnp.where(place == s, total[1:2], 0.0), axis=1, keepdims=True)
        tall, wide = bounds_of(m * owned + s, owner_ref, extent_ref)
        scale = jnp.where(place == s, jnp.sqrt(grad_sq / (pre_sq + epsilon)), scale)
        height = jnp.where(place == s, jnp.where(column < wide, tall, 0), height)
    rows = width // nm
    for i in range(nm):
        at = slice(i * rows, (i + 1) * rows)
        ok = i * rows + iota((rows, lanes), 0) < height
        step = jnp.where(ok, scale * precond_ref[at], 0.0)
        step_ref[at] = step
        fresh = (base_ref[at] - step_rate * step).astype(bf16)
        for g in range(ng):
            out_ref[g * nm + i] = fresh


def place_kernel(nx, nm, owned, owner_ref, back_ref, place_ref, out_ref):
    blocks, rows, width = out_ref.shape
    cols = width // nx
    for b in range(blocks):
        slot = owner_ref[b]
        owner, s = slot // owned, slot % owned
        lanes = []
        for zl in range(owned):
            lanes.append(
                jnp.concatenate([back_ref[(x * owned + zl) * nm + owner] for x in range(nx)], axis=0)
            )
        value = jnp.concatenate(lanes, axis=1)
        done = jnp.dot(value, place_ref[s], preferred_element_type=f32).astype(bf16)
        for x in range(nx):
            out_ref[b, :, x * cols : (x + 1) * cols] = done[x * rows : (x + 1) * rows]


def call(kernel, name, out, *args, scratch=()):
    specs = [in_smem if a.dtype == jnp.int32 else in_vmem for a in args]
    return pl.pallas_call(
        kernel,
        out_shape=out,
        in_specs=specs,
        out_specs=jax.tree.map(lambda _: in_vmem, out),
        scratch_shapes=list(scratch),
        compiler_params=params,
        name=name,
    )(*args)


def shape(dims, dtype):
    return jax.ShapeDtypeStruct(dims, dtype)


def make_local(nx, nzh, nzl, nm):
    ng = nx * nzl
    group = ("x", "zl")
    wide = ("x", "zl", "mp")

    def gather_along(value):
        zh = lax.axis_index("zh")
        held = value[None]
        stride = nzh // 2
        while stride:
            pairs = [(i, i ^ stride) for i in range(nzh)]
            other = lax.ppermute(held, "zh", pairs)
            first = (zh & stride) == 0
            low = jnp.where(first, held, other)
            high = jnp.where(first, other, held)
            held = jnp.stack([low, high], axis=1).reshape((-1,) + value.shape)
            stride //= 2
        return held

    def local(partial_grads, owner_slot, extent, left_roots, right_roots, momentum, master):
        blocks, rows, width = partial_grads.shape[1:]
        owned = left_roots.shape[0]
        slab = right_roots.shape[2]
        cols = width // nx
        mine_cols = slab * nzh
        lanes = owned * mine_cols
        zh = lax.axis_index("zh")

        roots = gather_along(jnp.swapaxes(right_roots, 1, 2))
        roots = jnp.swapaxes(roots, 0, 1).reshape(owned, mine_cols, width)
        base_t = jnp.swapaxes(master - (step_rate * beta_decay) * momentum, 1, 2)
        base_t = base_t.reshape(owned * slab, width)
        high = lax.reduce_precision(base_t, 8, 7)
        low = (base_t - high).astype(bf16)
        high = high.astype(bf16)

        send = call(
            functools.partial(send_kernel, nx, nm, owned),
            "blocks_to_owners",
            shape((ng * nm, rows, cols), bf16),
            owner_slot,
            partial_grads[0],
        )
        got = exchange(send, wide).reshape(ng, nm, rows, cols)
        part = got[0].astype(f32)
        for i in range(1, ng):
            part = part + got[i].astype(f32)
        pieces = exchange(part, "zh")
        grads, sq = call(
            functools.partial(grad_kernel, owned),
            "masked_grad",
            (shape((ng, rows, cols), bf16), shape((8, cols), f32)),
            owner_slot,
            extent,
            pieces,
        )
        all_cols = exchange(grads, group)
        packed = call(
            functools.partial(side_kernel, nx, owned),
            "right_side",
            shape((nzh, rows + 16 + 2 * nx * owned * slab, lanes), bf16),
            all_cols,
            roots,
            sq,
            high,
            low,
        )
        bands = exchange(packed, "zh")
        precond, base, sums = call(
            functools.partial(left_kernel, nx),
            "left_side",
            (shape((width, lanes), f32), shape((width, lanes), f32), shape((ng, 8, lanes), f32)),
            bands,
            left_roots,
            scratch=[pltpu.VMEM((lanes, width), f32)],
        )
        sums = exchange(sums, group)
        fresh, step = call(
            functools.partial(fresh_kernel, nm, owned, slab),
            "new_weights",
            (shape((ng * nm, rows, lanes), bf16), shape((width, lanes), f32)),
            owner_slot,
            extent,
            sums,
            precond,
            base,
        )
        back = exchange(fresh, wide)
        lane = jnp.arange(lanes, dtype=jnp.int32)
        c = lane % mine_cols
        to = jnp.arange(nzl, dtype=jnp.int32)[:, None] * slab + (c // slab) * (slab * nzl) + c % slab
        to = to.reshape(nzl * lanes)
        from_slot = jnp.tile(lane // mine_cols, nzl)
        place = (to[None, :, None] == jnp.arange(cols, dtype=jnp.int32)) & (
            from_slot[None, :, None] == jnp.arange(owned, dtype=jnp.int32)[:, None, None]
        )
        weights = call(
            functools.partial(place_kernel, nx, nm, owned),
            "blocks_in_order",
            shape((blocks, rows, width), bf16),
            owner_slot,
            back,
            place.astype(bf16),
        )

        step = step.reshape(width, owned, mine_cols)
        own_step = lax.dynamic_slice_in_dim(step, zh * slab, slab, 2).transpose(1, 0, 2)
        new_momentum = beta_decay * momentum + own_step
        new_master = master - step_rate * new_momentum
        return (new_momentum, new_master, weights)

    return local


def solution(mesh):
    nm = mesh.shape["mp"]
    nzl, nzh = 2, nm
    nx = mesh.shape["dp"] // (nzl * nzh)
    fine = Mesh(mesh.devices.reshape(nx, nzh, nzl, nm), ("x", "zh", "zl", "mp"))
    dp = ("x", "zh", "zl")
    slab_spec = P("mp", None, dp)
    return jax.shard_map(
        make_local(nx, nzh, nzl, nm),
        mesh=fine,
        in_specs=(
            P(dp, None, "mp", None),
            P(),
            P(),
            P("mp", None, None),
            slab_spec,
            slab_spec,
            slab_spec,
        ),
        out_specs=(slab_spec, slab_spec, P(None, "mp", None)),
        check_vma=False,
    )
```

time: 158 us -> 152 us (0.962)
  blocking collectives: 0 us -> 40 us
  waiting for transfers between devices: 76.6 us -> 37.8 us
  local copies, waits for them, and re-layouts: 10.4 us -> 2.15 us
  Pallas kernels: 0 us -> 7.95 us
  other arithmetic: 6.62 us -> 1.93 us
    all_to_all x0 -> x2, blocking collectives: none -> 40 us  [exchange(): return lax.all_to_all(value, axes, split_axis=0, concat_axis=0, tiled=True)]
    ppermute x3, waiting for transfers between devices: 35.8 us -> 11.4 us  [gather_along(): other = lax.ppermute(held, 'zh', pairs)]
    all_to_all x6 -> x4, waiting for transfers between devices: 40.9 us -> 26.4 us  [exchange(): return lax.all_to_all(value, axes, split_axis=0, concat_axis=0, tiled=True)]
    pallas_call x0 -> x6, Pallas kernels: none -> 7.95 us  [call(): pl.pallas_call(kernel, out_shape=out, in_specs=specs, out_specs=jax.tree....]
    all_to_all x6 -> x4, starting transfers between devices: 43.9 us -> 37.5 us  [exchange(): return lax.all_to_all(value, axes, split_axis=0, concat_axis=0, tiled=True)]
    ppermute x3, starting transfers between devices: 17.8 us -> 23.1 us  [gather_along(): other = lax.ppermute(held, 'zh', pairs)]
    reshape x6 -> x1, local copies, waits for them, and re-layouts: 4.02 us -> 0.02 us  [local(): roots = jnp.swapaxes(roots, 0, 1).reshape(owned, mine_cols, width)]
    broadcast_in_dim x4 -> x0, local copies, waits for them, and re-layouts: 3.3 us -> none  [spread(): return jnp.broadcast_to(value[None], (count,) + value.shape)]
  transfers between devices with their start and end apart: 9 -> 7, of which waited for: 7 -> 4; matrix products, arithmetic and copies ran while one was open for 2% -> 1% of each run, Pallas kernels for 0% -> 1%
where the time goes in v3:
time: 152 us; the launch traced here: 151 us
  starting transfers between devices  60.6 us (40%)
  blocking collectives  40 us (26%)
  waiting for transfers between devices  37.8 us (25%)
  Pallas kernels  7.95 us (5%)
  local copies, waits for them, and re-layouts  2.15 us (1%)
  other arithmetic  1.93 us (1%)
    all_to_all x2, blocking collectives, exchange(): return lax.all_to_all(value, axes, split_axis=0, concat_axis=0, tiled=True)  40 us
    all_to_all x4, starting transfers between devices, exchange(): return lax.all_to_all(value, axes, split_axis=0, concat_axis=0, tiled=True)  37.5 us
    all_to_all x4, waiting for transfers between devices, exchange(): return lax.all_to_all(value, axes, split_axis=0, concat_axis=0, tiled=True)  26.4 us
    ppermute x3, starting transfers between devices, gather_along(): other = lax.ppermute(held, 'zh', pairs)  23.1 us
    ppermute x3, waiting for transfers between devices, gather_along(): other = lax.ppermute(held, 'zh', pairs)  11.4 us
    pallas_call x6, Pallas kernels, call(): pl.pallas_call(kernel, out_shape=out, in_specs=specs, out_specs=jax.tree....  7.95 us
  transfers between devices with their start and end apart: 7, of which 4 were waited for; matrix products, arithmetic and copies ran while one was open for 1% of the time, Pallas kernels for 1%

profile of v3, /device:TPU:1, one launch (start us, length us, event | category | flops | bytes accessed | tf_op | source)
XLA Modules:
  0.0 151.4 jit_solution(6786687471744570197)
XLA Ops:
  0.6 0.6 copy-done.2
  1.3 1.2 copy-done
  2.5 1.7 %blocks_to_owners.1 = bf16[64,64,128]{2,1,0:T(8,128)(2,1)} custom-call(s32[16]{0:T(128)S(1)} %copy-done.2, bf16[16,64,512]{2,1,0:T(8,128)(2,1)S(1)} %bitcast.49), custom_call_target="tpu_custom_call" | custom-call | tf_op jit(solution)/shard_map/blocks_to_owners/pallas_call | solution.py:184
  4.2 11.1 %all-to-all-start = ((bf16[64,64,128]{2,1,0:T(8,128)(2,1)}), bf16[64,64,128]{2,1,0:T(8,128)(2,1)S(1)}, u32[]{:S(2)}, u32[]{:S(2)}) async-start(bf16[64,64,128]{2,1,0:T(8,128)(2,1)} %blocks_to_owners.1), calls=%async_computation | async-start | bytes 2097152 | tf_op jit(solution)/shard_map/all_to_all | solution.py:21
  15.3 13.9 %collective-permute-start = (bf16[1,2,8,512]{3,2,1,0:T(8,128)(2,1)S(1)}, bf16[1,2,8,512]{3,2,1,0:T(8,128)(2,1)S(1)}, u32[]{:S(2)}, u32[]{:S(2)}) collective-permute-start(bf16[1,2,8,512]{3,2,1,0:T(8,128)(2,1)S(1)} %bitcast.52), channel_id=1, source_target_pairs={{0,64},{16,80},{32,96},{48,112},{64,0},{80,16},{96,32},{112,48},{1... | collective-permute-start | bytes 49160 | tf_op jit(solution)/shard_map/ppermute | solution.py:210
  29.3 4.1 %all-to-all-done = bf16[64,64,128]{2,1,0:T(8,128)(2,1)S(1)} async-done(((bf16[64,64,128]{2,1,0:T(8,128)(2,1)}), bf16[64,64,128]{2,1,0:T(8,128)(2,1)S(1)}, u32[]{:S(2)}, u32[]{:S(2)}) %all-to-all-start) | async-done | bytes 1048608 | tf_op jit(solution)/shard_map/all_to_all | solution.py:21
  33.4 0.9 convert_add_fusion
  34.3 13.4 %all-to-all-start.1 = ((f32[8,64,128]{2,1,0:T(8,128)}), f32[8,64,128]{2,1,0:T(8,128)S(1)}, u32[]{:S(2)}, u32[]{:S(2)}) async-start(f32[8,64,128]{2,1,0:T(8,128)} %convert_add_fusion), calls=%async_computation.1 | async-start | bytes 524288 | tf_op jit(solution)/shard_map/all_to_all | solution.py:21
  47.7 7.3 %collective-permute-start.1 = (bf16[2,2,8,512]{3,2,1,0:T(8,128)(2,1)S(1)}, bf16[2,2,8,512]{3,2,1,0:T(8,128)(2,1)S(1)}, u32[]{:S(2)}, u32[]{:S(2)}) collective-permute-start(bf16[2,2,8,512]{3,2,1,0:T(8,128)(2,1)S(1)} %maximum_bitcast_fusion), channel_id=1, source_target_pairs={{0,32},{16,48},{32,0},{48,16},{64,96},{80,112},{96,64},{112,80},{1... | collective-permute-start | bytes 98312 | tf_op jit(solution)/shard_map/ppermute | solution.py:210
  54.9 11.4 %collective-permute-done.1 = bf16[2,2,8,512]{3,2,1,0:T(8,128)(2,1)S(1)} collective-permute-done((bf16[2,2,8,512]{3,2,1,0:T(8,128)(2,1)S(1)}, bf16[2,2,8,512]{3,2,1,0:T(8,128)(2,1)S(1)}, u32[]{:S(2)}, u32[]{:S(2)}) %collective-permute-start.1) | collective-permute-done | bytes 32800 | tf_op jit(solution)/shard_map/ppermute | solution.py:210
  66.4 1.9 %collective-permute-start.2 = (bf16[4,2,8,512]{3,2,1,0:T(8,128)(2,1)S(1)}, bf16[4,2,8,512]{3,2,1,0:T(8,128)(2,1)S(1)}, u32[]{:S(2)}, u32[]{:S(2)}) collective-permute-start(bf16[4,2,8,512]{3,2,1,0:T(8,128)(2,1)S(1)} %bitcast.51), channel_id=1, source_target_pairs={{0,16},{16,0},{32,48},{48,32},{64,80},{80,64},{96,112},{112,96},{1... | collective-permute-start | bytes 196616 | tf_op jit(solution)/shard_map/ppermute | solution.py:210
  68.5 1.4 masked_grad.1
  69.9 3.4 %all-to-all-start.2 = ((bf16[8,64,128]{2,1,0:T(8,128)(2,1)}), bf16[8,64,128]{2,1,0:T(8,128)(2,1)S(1)}, u32[]{:S(2)}, u32[]{:S(2)}) async-start(bf16[8,64,128]{2,1,0:T(8,128)(2,1)} %get-tuple-element.10), calls=%async_computation.2 | async-start | bytes 262144 | tf_op jit(solution)/shard_map/all_to_all | solution.py:21
  73.4 5.4 %all-to-all-done.2.cols_ref = bf16[8,64,128]{2,1,0:T(8,128)(2,1)S(1)} async-done(((bf16[8,64,128]{2,1,0:T(8,128)(2,1)}), bf16[8,64,128]{2,1,0:T(8,128)(2,1)S(1)}, u32[]{:S(2)}, u32[]{:S(2)}) %all-to-all-start.2) | async-done | bytes 131104 | tf_op jit(solution)/shard_map/all_to_all | solution.py:21
  78.7 0.3 right_side.1
  79.0 29.2 %all_to_all.30.bands_ref = bf16[8,208,128]{2,1,0:T(8,128)(2,1)S(1)} all-to-all(bf16[8,208,128]{2,1,0:T(8,128)(2,1)S(1)} %right_side.1), channel_id=1, replica_groups=mesh['x'=4,'zh'=8,'zl'=2,'mp'=8] {'zh'}, dimensions={0} | all-to-all | bytes 851968 | tf_op jit(solution)/shard_map/all_to_all | solution.py:21
  108.2 0.4 left_side.1
  108.7 10.8 %all_to_all.31.sums_ref = f32[8,8,128]{2,1,0:T(8,128)S(1)} all-to-all(f32[8,8,128]{2,1,0:T(8,128)S(1)} %get-tuple-element.12), channel_id=1, replica_groups=mesh['x'=4,'zh'=8,'zl'=2,'mp'=8] {'x','zl'}, dimensions={0} | all-to-all | bytes 65536 | tf_op jit(solution)/shard_map/all_to_all | solution.py:21
  119.5 1.9 %new_weights.1 = (bf16[64,64,128]{2,1,0:T(8,128)(2,1)}, f32[512,128]{1,0:T(8,128)S(1)}) custom-call(s32[16]{0:T(128)S(1)} %copy-done.2, s32[16,2]{1,0:T(8,128)S(1)} %copy.22.extent_ref, f32[8,8,128]{2,1,0:T(8,128)S(1)} %all_to_all.31.sums_ref, f32[512,128]{1,0:T(8,128)S(1)} %get-tuple-element.13.precond_ref, f32[512,128]{1,0:T(8,128)S(1)} %get-tuple-element.14.base_ref), custom_call_target="tpu_custom_call" | custom-call | tf_op jit(solution)/shard_map/new_weights/pallas_call | solution.py:184
  121.4 9.7 %all-to-all-start.5 = ((bf16[64,64,128]{2,1,0:T(8,128)(2,1)}), bf16[64,64,128]{2,1,0:T(8,128)(2,1)S(1)}, u32[]{:S(2)}, u32[]{:S(2)}) async-start(bf16[64,64,128]{2,1,0:T(8,128)(2,1)} %get-tuple-element.16), calls=%async_computation.5 | async-start | bytes 2097152 | tf_op jit(solution)/shard_map/all_to_all | solution.py:21
  131.3 0.1 and_convert_fusion.place_ref
  131.6 0.6 multiply_subtract_fusion
  132.2 16.9 %all-to-all-done.5.back_ref = bf16[64,64,128]{2,1,0:T(8,128)(2,1)S(1)} async-done(((bf16[64,64,128]{2,1,0:T(8,128)(2,1)}), bf16[64,64,128]{2,1,0:T(8,128)(2,1)S(1)}, u32[]{:S(2)}, u32[]{:S(2)}) %all-to-all-start.5) | async-done | bytes 1048608 | tf_op jit(solution)/shard_map/all_to_all | solution.py:21
  149.1 2.2 %blocks_in_order.1 = bf16[16,64,512]{2,1,0:T(8,128)(2,1)} custom-call(s32[16]{0:T(128)S(1)} %copy-done.2, bf16[64,64,128]{2,1,0:T(8,128)(2,1)S(1)} %all-to-all-done.5.back_ref, bf16[2,256,128]{2,1,0:T(8,128)(2,1)S(1)} %and_convert_fusion.place_ref), custom_call_target="tpu_custom_call" | custom-call | tf_op jit(solution)/shard_map/blocks_in_order/pallas_call | solution.py:184
  (33 shorter events, 0.6 us)
Async XLA Ops:
  0.6 0.7 copy-start.2
  1.3 1.2 copy-start
  4.2 11.1 %copy-start.5 = (bf16[2,512,8]{1,2,0:T(8,128)(2,1)S(1)}, bf16[2,512,8]{1,2,0:T(8,128)(2,1)}, u32[]{:S(2)}) copy-start(bf16[2,512,8]{1,2,0:T(8,128)(2,1)} %param.11) | copy-start | bytes 49156
  4.2 29.2 %all-to-all-start = ((bf16[64,64,128]{2,1,0:T(8,128)(2,1)}), bf16[64,64,128]{2,1,0:T(8,128)(2,1)S(1)}, u32[]{:S(2)}, u32[]{:S(2)}) async-start(bf16[64,64,128]{2,1,0:T(8,128)(2,1)} %blocks_to_owners.1), calls=%async_computation | async-start | bytes 2097152 | tf_op jit(solution)/shard_map/all_to_all | solution.py:21
  15.3 32.3 %collective-permute-start = (bf16[1,2,8,512]{3,2,1,0:T(8,128)(2,1)S(1)}, bf16[1,2,8,512]{3,2,1,0:T(8,128)(2,1)S(1)}, u32[]{:S(2)}, u32[]{:S(2)}) collective-permute-start(bf16[1,2,8,512]{3,2,1,0:T(8,128)(2,1)S(1)} %bitcast.52), channel_id=1, source_target_pairs={{0,64},{16,80},{32,96},{48,112},{64,0},{80,16},{96,32},{112,48},{1... | collective-permute-start | bytes 49160 | tf_op jit(solution)/shard_map/ppermute | solution.py:210
  34.3 34.2 %all-to-all-start.1 = ((f32[8,64,128]{2,1,0:T(8,128)}), f32[8,64,128]{2,1,0:T(8,128)S(1)}, u32[]{:S(2)}, u32[]{:S(2)}) async-start(f32[8,64,128]{2,1,0:T(8,128)} %convert_add_fusion), calls=%async_computation.1 | async-start | bytes 524288 | tf_op jit(solution)/shard_map/all_to_all | solution.py:21
  47.7 18.7 %collective-permute-start.1 = (bf16[2,2,8,512]{3,2,1,0:T(8,128)(2,1)S(1)}, bf16[2,2,8,512]{3,2,1,0:T(8,128)(2,1)S(1)}, u32[]{:S(2)}, u32[]{:S(2)}) collective-permute-start(bf16[2,2,8,512]{3,2,1,0:T(8,128)(2,1)S(1)} %maximum_bitcast_fusion), channel_id=1, source_target_pairs={{0,32},{16,48},{32,0},{48,16},{64,96},{80,112},{96,64},{112,80},{1... | collective-permute-start | bytes 98312 | tf_op jit(solution)/shard_map/ppermute | solution.py:210
  66.4 2.0 %copy-start.3 = (f32[2,512,8]{1,2,0:T(8,128)S(1)}, f32[2,512,8]{1,2,0:T(8,128)}, u32[]{:S(2)}) copy-start(f32[2,512,8]{1,2,0:T(8,128)} %param.13) | copy-start | bytes 98308
  66.4 2.0 %copy-start.4 = (f32[2,512,8]{1,2,0:T(8,128)S(1)}, f32[2,512,8]{1,2,0:T(8,128)}, u32[]{:S(2)}) copy-start(f32[2,512,8]{1,2,0:T(8,128)} %param.12) | copy-start | bytes 98308
  66.4 2.0 %copy-start.6 = (s32[16,2]{0,1:T(2,128)S(1)}, s32[16,2]{0,1:T(2,128)}, u32[]{:S(2)}) copy-start(s32[16,2]{0,1:T(2,128)} %param.9) | copy-start | bytes 388
  66.4 6.8 %collective-permute-start.2 = (bf16[4,2,8,512]{3,2,1,0:T(8,128)(2,1)S(1)}, bf16[4,2,8,512]{3,2,1,0:T(8,128)(2,1)S(1)}, u32[]{:S(2)}, u32[]{:S(2)}) collective-permute-start(bf16[4,2,8,512]{3,2,1,0:T(8,128)(2,1)S(1)} %bitcast.51), channel_id=1, source_target_pairs={{0,16},{16,0},{32,48},{48,32},{64,80},{80,64},{96,112},{112,96},{1... | collective-permute-start | bytes 196616 | tf_op jit(solution)/shard_map/ppermute | solution.py:210
  69.9 8.9 %all-to-all-start.2 = ((bf16[8,64,128]{2,1,0:T(8,128)(2,1)}), bf16[8,64,128]{2,1,0:T(8,128)(2,1)S(1)}, u32[]{:S(2)}, u32[]{:S(2)}) async-start(bf16[8,64,128]{2,1,0:T(8,128)(2,1)} %get-tuple-element.10), calls=%async_computation.2 | async-start | bytes 262144 | tf_op jit(solution)/shard_map/all_to_all | solution.py:21
  73.3 34.9 %copy-start.1 = (bf16[2,512,512]{2,1,0:T(8,128)(2,1)S(1)}, bf16[2,512,512]{2,1,0:T(8,128)(2,1)}, u32[]{:S(2)}) copy-start(bf16[2,512,512]{2,1,0:T(8,128)(2,1)} %left_ref.1) | copy-start | bytes 3145732
  121.4 27.8 %all-to-all-start.5 = ((bf16[64,64,128]{2,1,0:T(8,128)(2,1)}), bf16[64,64,128]{2,1,0:T(8,128)(2,1)S(1)}, u32[]{:S(2)}, u32[]{:S(2)}) async-start(bf16[64,64,128]{2,1,0:T(8,128)(2,1)} %get-tuple-element.16), calls=%async_computation.5 | async-start | bytes 2097152 | tf_op jit(solution)/shard_map/all_to_all | solution.py:21

commit v4 on v3

--- a/solution.py
+++ b/solution.py
@@ -10,15 +10,23 @@
 epsilon = 1e-06
 beta_decay = 0.9
 step_rate = 0.5
+sum_unit = 2.0**11
+base_unit = 2.0**12
+f16 = jnp.float16
 f32 = jnp.float32
 bf16 = jnp.bfloat16
 in_vmem = pl.BlockSpec(memory_space=pltpu.VMEM)
+anywhere = pl.BlockSpec(memory_space=pl.ANY)
 in_smem = pl.BlockSpec(memory_space=pltpu.SMEM)
 params = pltpu.CompilerParams(vmem_limit_bytes=24 * 2**20)
 
 
 def exchange(value, axes):
     return lax.all_to_all(value, axes, split_axis=0, concat_axis=0, tiled=True)
+
+
+def spread(value, count):
+    return jnp.broadcast_to(value[None], (count,) + value.shape)
 
 
 def bounds_of(slot, owner_ref, extent_ref):
@@ -34,14 +42,23 @@
     return lax.broadcasted_iota(jnp.int32, shape, dim)
 
 
-def send_kernel(nx, nm, owned, owner_ref, grads_ref, out_ref):
+def send_kernel(nx, nm, owned, owner_ref, grads_ref, out_ref, sem):
     blocks, rows, width = grads_ref.shape
     cols = width // nx
+    copies = []
     for b in range(blocks):
         slot = owner_ref[b]
         owner, place = slot // owned, slot % owned
         for x in range(nx):
-            out_ref[(x * owned + place) * nm + owner] = grads_ref[b, :, x * cols : (x + 1) * cols]
+            copy = pltpu.make_async_copy(
+                grads_ref.at[b, :, x * cols : (x + 1) * cols],
+                out_ref.at[(x * owned + place) * nm + owner],
+                sem.at[b * nx + x],
+            )
+            copy.start()
+            copies.append(copy)
+    for copy in copies:
+        copy.wait()
 
 
 def grad_kernel(owned, owner_ref, extent_ref, pieces_ref, out_ref, sq_ref):
@@ -60,7 +77,7 @@
         out_ref[i] = low
 
 
-def side_kernel(nx, owned, cols_ref, roots_ref, sq_ref, high_ref, low_ref, out_ref):
+def side_kernel(nx, owned, cols_ref, roots_ref, sq_ref, out_ref):
     nzh, height, lanes = out_ref.shape
     rows = cols_ref.shape[1]
     mine = roots_ref.shape[1]
@@ -86,19 +103,13 @@
     for i in range(nzh):
         out_ref[i, :rows] = right
         out_ref[i, rows : rows + 16] = extra
-        at = rows + 16
-        for part_ref in (high_ref, low_ref):
-            for x in range(nx):
-                out_ref[i, at : at + 16] = part_ref[:, x * lanes : (x + 1) * lanes]
-                at += 16
-
-
-def left_kernel(nx, bands_ref, left_ref, precond_ref, base_ref, sums_ref, flip_ref):
+
+
+def left_kernel(bands_ref, left_ref, base_t_ref, precond_ref, base_ref, sums_ref):
     nzh, _, lanes = bands_ref.shape
     owned, width, _ = left_ref.shape
     rows = width // nzh
     mine = lanes // owned
-    slab = mine // nzh
     side = bands_ref[:, :rows, :].reshape(width, lanes)
     lane = iota((width, lanes), 1)
     precond = jnp.zeros((width, lanes), f32)
@@ -113,22 +124,11 @@
     sums = jnp.where(row == 0, grad_sq, jnp.where(row == 1, pre_sq, 0.0))
     for i in range(sums_ref.shape[0]):
         sums_ref[i] = sums
-    step = owned * slab
-    for zh in range(nzh):
-        for x in range(nx):
-            at = rows + 16 + x * step
-            value = bands_ref[zh, at : at + step, :].astype(f32)
-            at = at + nx * step
-            value = value + bands_ref[zh, at : at + step, :].astype(f32)
-            for s in range(owned):
-                flip_ref[s * mine + zh * slab : s * mine + (zh + 1) * slab, x * lanes : (x + 1) * lanes] = (
-                    value[s * slab : (s + 1) * slab]
-                )
-    base_ref[...] = flip_ref[...].T
+    base_ref[...] = base_t_ref[...].T
 
 
 def fresh_kernel(
-    nm, owned, slab, owner_ref, extent_ref, sums_ref, precond_ref, base_ref, out_ref, step_ref
+    nm, owned, slab, owner_ref, extent_ref, sums_ref, precond_ref, base_ref, out_ref, step_ref, held_ref, sem
 ):
     width, lanes = precond_ref.shape
     mine = lanes // owned
@@ -158,13 +158,20 @@
         step = jnp.where(ok, scale * precond_ref[at], 0.0)
         step_ref[at] = step
         fresh = (base_ref[at] - step_rate * step).astype(bf16)
-        for g in range(ng):
-            out_ref[g * nm + i] = fresh
-
-
-def place_kernel(nx, nm, owned, owner_ref, back_ref, place_ref, out_ref):
+        held_ref[i] = fresh
+    copies = []
+    for g in range(ng):
+        copy = pltpu.make_async_copy(held_ref, out_ref.at[g * nm : (g + 1) * nm], sem.at[g])
+        copy.start()
+        copies.append(copy)
+    for copy in copies:
+        copy.wait()
+
+
+def place_kernel(nx, nm, owned, owner_ref, back_ref, place_ref, out_ref, held_ref, sem):
     blocks, rows, width = out_ref.shape
     cols = width // nx
+    copies = []
     for b in range(blocks):
         slot = owner_ref[b]
         owner, s = slot // owned, slot % owned
@@ -176,16 +183,23 @@
         value = jnp.concatenate(lanes, axis=1)
         done = jnp.dot(value, place_ref[s], preferred_element_type=f32).astype(bf16)
         for x in range(nx):
-            out_ref[b, :, x * cols : (x + 1) * cols] = done[x * rows : (x + 1) * rows]
-
-
-def call(kernel, name, out, *args, scratch=()):
+            held_ref[b, :, x * cols : (x + 1) * cols] = done[x * rows : (x + 1) * rows]
+        copy = pltpu.make_async_copy(held_ref.at[b], out_ref.at[b], sem.at[b])
+        copy.start()
+        copies.append(copy)
+    for copy in copies:
+        copy.wait()
+
+
+def call(kernel, name, out, *args, scratch=(), far=(), far_out=()):
     specs = [in_smem if a.dtype == jnp.int32 else in_vmem for a in args]
+    for i in far:
+        specs[i] = anywhere
     return pl.pallas_call(
         kernel,
         out_shape=out,
         in_specs=specs,
-        out_specs=jax.tree.map(lambda _: in_vmem, out),
+        out_specs=[anywhere if i in far_out else in_vmem for i in range(len(out))],
         scratch_shapes=list(scratch),
         compiler_params=params,
         name=name,
@@ -201,19 +215,24 @@
     group = ("x", "zl")
     wide = ("x", "zl", "mp")
 
-    def gather_along(value):
-        zh = lax.axis_index("zh")
-        held = value[None]
-        stride = nzh // 2
-        while stride:
-            pairs = [(i, i ^ stride) for i in range(nzh)]
-            other = lax.ppermute(held, "zh", pairs)
-            first = (zh & stride) == 0
-            low = jnp.where(first, held, other)
-            high = jnp.where(first, other, held)
-            held = jnp.stack([low, high], axis=1).reshape((-1,) + value.shape)
-            stride //= 2
-        return held
+    def to_rows(value):
+        owned, slab, width = value.shape
+        value = value.reshape(owned * slab, nx, width // nx)
+        return jnp.swapaxes(value, 0, 1).reshape(nx * owned * slab, width // nx)
+
+    def from_rows(value, owned):
+        count, height, cols = value.shape
+        slab = height // (nx * owned)
+        value = value.reshape(count, nx, owned, slab, cols).transpose(2, 0, 3, 1, 4)
+        return value.reshape(owned * count * slab, nx * cols)
+
+    def swap(held, stride):
+        pairs = [(i, i ^ stride) for i in range(nzh)]
+        other = lax.ppermute(held, "zh", pairs)
+        first = (lax.axis_index("zh") & stride) == 0
+        low = jnp.where(first, held, other)
+        high = jnp.where(first, other, held)
+        return jnp.stack([low, high], axis=1).reshape((-1,) + held.shape[1:])
 
     def local(partial_grads, owner_slot, extent, left_roots, right_roots, momentum, master):
         blocks, rows, width = partial_grads.shape[1:]
@@ -224,26 +243,35 @@
         lanes = owned * mine_cols
         zh = lax.axis_index("zh")
 
-        roots = gather_along(jnp.swapaxes(right_roots, 1, 2))
-        roots = jnp.swapaxes(roots, 0, 1).reshape(owned, mine_cols, width)
+        roots = jnp.swapaxes(right_roots, 1, 2)[None]
+        strides = [nzh >> i for i in range(1, nzh.bit_length())]
         base_t = jnp.swapaxes(master - (step_rate * beta_decay) * momentum, 1, 2)
-        base_t = base_t.reshape(owned * slab, width)
-        high = lax.reduce_precision(base_t, 8, 7)
-        low = (base_t - high).astype(bf16)
-        high = high.astype(bf16)
-
-        send = call(
+        (send,) = call(
             functools.partial(send_kernel, nx, nm, owned),
             "blocks_to_owners",
-            shape((ng * nm, rows, cols), bf16),
+            [shape((ng * nm, rows, cols), bf16)],
             owner_slot,
             partial_grads[0],
-        )
+            scratch=[pltpu.SemaphoreType.DMA((blocks * nx,))],
+            far=(1,),
+            far_out=(0,),
+        )
+        roots, send = lax.optimization_barrier((roots, send))
+        roots = swap(roots, strides[0])
         got = exchange(send, wide).reshape(ng, nm, rows, cols)
         part = got[0].astype(f32)
         for i in range(1, ng):
             part = part + got[i].astype(f32)
-        pieces = exchange(part, "zh")
+        part = (part * sum_unit).astype(f16)
+        base_rows = to_rows((base_t * base_unit).astype(f16))
+        packed = jnp.concatenate([part, spread(base_rows, nzh)], axis=1)
+        roots, packed = lax.optimization_barrier((roots, packed))
+        for stride in strides[1:]:
+            roots = swap(roots, stride)
+        roots = jnp.swapaxes(roots, 0, 1).reshape(owned, mine_cols, width)
+        pieces = exchange(packed, "zh")
+        base_t = from_rows(pieces[:, rows:], owned).astype(f32) * (1.0 / base_unit)
+        pieces = pieces[:, :rows].astype(f32) * (1.0 / sum_unit)
         grads, sq = call(
             functools.partial(grad_kernel, owned),
             "masked_grad",
@@ -253,24 +281,22 @@
             pieces,
         )
         all_cols = exchange(grads, group)
-        packed = call(
+        (packed,) = call(
             functools.partial(side_kernel, nx, owned),
             "right_side",
-            shape((nzh, rows + 16 + 2 * nx * owned * slab, lanes), bf16),
+            [shape((nzh, rows + 16, lanes), bf16)],
             all_cols,
             roots,
             sq,
-            high,
-            low,
         )
         bands = exchange(packed, "zh")
         precond, base, sums = call(
-            functools.partial(left_kernel, nx),
+            left_kernel,
             "left_side",
             (shape((width, lanes), f32), shape((width, lanes), f32), shape((ng, 8, lanes), f32)),
             bands,
             left_roots,
-            scratch=[pltpu.VMEM((lanes, width), f32)],
+            base_t,
         )
         sums = exchange(sums, group)
         fresh, step = call(
@@ -282,6 +308,8 @@
             sums,
             precond,
             base,
+            scratch=[pltpu.VMEM((nm, rows, lanes), bf16), pltpu.SemaphoreType.DMA((ng,))],
+            far_out=(0,),
         )
         back = exchange(fresh, wide)
         lane = jnp.arange(lanes, dtype=jnp.int32)
@@ -292,13 +320,15 @@
         place = (to[None, :, None] == jnp.arange(cols, dtype=jnp.int32)) & (
             from_slot[None, :, None] == jnp.arange(owned, dtype=jnp.int32)[:, None, None]
         )
-        weights = call(
+        (weights,) = call(
             functools.partial(place_kernel, nx, nm, owned),
             "blocks_in_order",
-            shape((blocks, rows, width), bf16),
+            [shape((blocks, rows, width), bf16)],
             owner_slot,
             back,
             place.astype(bf16),
+            scratch=[pltpu.VMEM((blocks, rows, width), bf16), pltpu.SemaphoreType.DMA((blocks,))],
+            far_out=(0,),
         )
 
         step = step.reshape(width, owned, mine_cols)

time: 152 us -> 142 us (0.934)
  blocking collectives: 40 us -> 7.7 us
  waiting for transfers between devices: 37.8 us -> 58.2 us
    all_to_all x2 -> x1, blocking collectives: 40 us -> 7.7 us  [exchange(): return lax.all_to_all(value, axes, split_axis=0, concat_axis=0, tiled=True)]
    ppermute x3, waiting for transfers between devices: 11.4 us -> 22 us  [swap(): other = lax.ppermute(held, 'zh', pairs)]
    all_to_all x4 -> x5, waiting for transfers between devices: 26.4 us -> 36.1 us  [exchange(): return lax.all_to_all(value, axes, split_axis=0, concat_axis=0, tiled=True)]
    all_to_all x4 -> x5, starting transfers between devices: 37.5 us -> 38.4 us  [exchange(): return lax.all_to_all(value, axes, split_axis=0, concat_axis=0, tiled=True)]
  transfers between devices with their start and end apart: 7 -> 8, of which waited for: 4 -> 5; matrix products, arithmetic and copies ran while one was open for 1% -> 1% of each run, Pallas kernels for 1% -> 1%
where the time goes in v4:
time: 142 us; the launch traced here: 141 us
  starting transfers between devices  61.6 us (43%)
  waiting for transfers between devices  58.2 us (41%)
  Pallas kernels  8.8 us (6%)
  blocking collectives  7.7 us (5%)
  local copies, waits for them, and re-layouts  2.21 us (2%)
  other arithmetic  2.06 us (1%)
    all_to_all x5, starting transfers between devices, exchange(): return lax.all_to_all(value, axes, split_axis=0, concat_axis=0, tiled=True)  38.4 us
    all_to_all x5, waiting for transfers between devices, exchange(): return lax.all_to_all(value, axes, split_axis=0, concat_axis=0, tiled=True)  36.1 us
    ppermute x3, starting transfers between devices, swap(): other = lax.ppermute(held, 'zh', pairs)  23.1 us
    ppermute x3, waiting for transfers between devices, swap(): other = lax.ppermute(held, 'zh', pairs)  22 us
    pallas_call x6, Pallas kernels, call(): pl.pallas_call(kernel, out_shape=out, in_specs=specs, out_specs=[anywhere...  8.8 us
    all_to_all x1, blocking collectives, exchange(): return lax.all_to_all(value, axes, split_axis=0, concat_axis=0, tiled=True)  7.7 us
  transfers between devices with their start and end apart: 8, of which 5 were waited for; matrix products, arithmetic and copies ran while one was open for 1% of the time, Pallas kernels for 1%

profile of v4, /device:TPU:1, one launch (start us, length us, event | category | flops | bytes accessed | tf_op | source)
XLA Modules:
  0.0 141.4 jit_solution(17226418843773308867)
XLA Ops:
  0.6 0.6 copy-done.2
  1.3 1.2 copy-done
  2.5 2.1 %blocks_to_owners.1 = bf16[64,64,128]{2,1,0:T(8,128)(2,1)} custom-call(s32[16]{0:T(128)S(1)} %copy-done.2, bf16[16,64,512]{2,1,0:T(8,128)(2,1)S(1)} %bitcast.46), custom_call_target="tpu_custom_call" | custom-call | tf_op jit(solution)/shard_map/blocks_to_owners/pallas_call | solution.py:198
  4.6 11.1 %all-to-all-start = ((bf16[64,64,128]{2,1,0:T(8,128)(2,1)}), bf16[64,64,128]{2,1,0:T(8,128)(2,1)S(1)}, u32[]{:S(2)}, u32[]{:S(2)}) async-start(bf16[64,64,128]{2,1,0:T(8,128)(2,1)} %blocks_to_owners.1), calls=%async_computation | async-start | bytes 2097152 | tf_op jit(solution)/shard_map/all_to_all | solution.py:25
  15.7 13.9 %collective-permute-start = (bf16[1,2,8,512]{3,2,1,0:T(8,128)(2,1)S(1)}, bf16[1,2,8,512]{3,2,1,0:T(8,128)(2,1)S(1)}, u32[]{:S(2)}, u32[]{:S(2)}) collective-permute-start(bf16[1,2,8,512]{3,2,1,0:T(8,128)(2,1)S(1)} %bitcast.53), channel_id=1, source_target_pairs={{0,64},{16,80},{32,96},{48,112},{64,0},{80,16},{96,32},{112,48},{1... | collective-permute-start | bytes 49160 | tf_op jit(solution)/shard_map/ppermute | solution.py:231
  29.8 10.6 %collective-permute-done = bf16[1,2,8,512]{3,2,1,0:T(8,128)(2,1)S(1)} collective-permute-done((bf16[1,2,8,512]{3,2,1,0:T(8,128)(2,1)S(1)}, bf16[1,2,8,512]{3,2,1,0:T(8,128)(2,1)S(1)}, u32[]{:S(2)}, u32[]{:S(2)}) %collective-permute-start) | collective-permute-done | bytes 16416 | tf_op jit(solution)/shard_map/ppermute | solution.py:231
  40.6 0.8 pad_maximum_fusion
  41.4 6.9 %all-to-all-start.1 = ((f16[8,128,128]{2,1,0:T(8,128)(2,1)}), f16[8,128,128]{2,1,0:T(8,128)(2,1)S(1)}, u32[]{:S(2)}, u32[]{:S(2)}) async-start(f16[8,128,128]{2,1,0:T(8,128)(2,1)} %pad_maximum_fusion), calls=%async_computation.1 | async-start | bytes 524288 | tf_op jit(solution)/shard_map/all_to_all | solution.py:25
  48.3 7.3 %collective-permute-start.1 = (bf16[2,2,8,512]{3,2,1,0:T(8,128)(2,1)S(1)}, bf16[2,2,8,512]{3,2,1,0:T(8,128)(2,1)S(1)}, u32[]{:S(2)}, u32[]{:S(2)}) collective-permute-start(bf16[2,2,8,512]{3,2,1,0:T(8,128)(2,1)S(1)} %maximum_bitcast_fusion), channel_id=1, source_target_pairs={{0,32},{16,48},{32,0},{48,16},{64,96},{80,112},{96,64},{112,80},{1... | collective-permute-start | bytes 98312 | tf_op jit(solution)/shard_map/ppermute | solution.py:231
  55.6 11.4 %collective-permute-done.1 = bf16[2,2,8,512]{3,2,1,0:T(8,128)(2,1)S(1)} collective-permute-done((bf16[2,2,8,512]{3,2,1,0:T(8,128)(2,1)S(1)}, bf16[2,2,8,512]{3,2,1,0:T(8,128)(2,1)S(1)}, u32[]{:S(2)}, u32[]{:S(2)}) %collective-permute-start.1) | collective-permute-done | bytes 32800 | tf_op jit(solution)/shard_map/ppermute | solution.py:231
  67.1 1.9 %collective-permute-start.2 = (bf16[4,2,8,512]{3,2,1,0:T(8,128)(2,1)S(1)}, bf16[4,2,8,512]{3,2,1,0:T(8,128)(2,1)S(1)}, u32[]{:S(2)}, u32[]{:S(2)}) collective-permute-start(bf16[4,2,8,512]{3,2,1,0:T(8,128)(2,1)S(1)} %bitcast.50), channel_id=1, source_target_pairs={{0,16},{16,0},{32,48},{48,32},{64,80},{80,64},{96,112},{112,96},{1... | collective-permute-start | bytes 196616 | tf_op jit(solution)/shard_map/ppermute | solution.py:231
  69.1 1.4 masked_grad.1
  70.4 3.4 %all-to-all-start.2 = ((bf16[8,64,128]{2,1,0:T(8,128)(2,1)}), bf16[8,64,128]{2,1,0:T(8,128)(2,1)S(1)}, u32[]{:S(2)}, u32[]{:S(2)}) async-start(bf16[8,64,128]{2,1,0:T(8,128)(2,1)} %get-tuple-element.17), calls=%async_computation.2 | async-start | bytes 262144 | tf_op jit(solution)/shard_map/all_to_all | solution.py:25
  73.9 5.4 %all-to-all-done.2.cols_ref = bf16[8,64,128]{2,1,0:T(8,128)(2,1)S(1)} async-done(((bf16[8,64,128]{2,1,0:T(8,128)(2,1)}), bf16[8,64,128]{2,1,0:T(8,128)(2,1)S(1)}, u32[]{:S(2)}, u32[]{:S(2)}) %all-to-all-start.2) | async-done | bytes 131104 | tf_op jit(solution)/shard_map/all_to_all | solution.py:25
  79.3 0.9 right_side.1
  80.2 7.9 %all-to-all-start.3 = ((bf16[8,80,128]{2,1,0:T(8,128)(2,1)}), bf16[8,80,128]{2,1,0:T(8,128)(2,1)S(1)}, u32[]{:S(2)}, u32[]{:S(2)}) async-start(bf16[8,80,128]{2,1,0:T(8,128)(2,1)} %right_side.1), calls=%async_computation.3 | async-start | bytes 327680 | tf_op jit(solution)/shard_map/all_to_all | solution.py:25
  88.2 13.9 %all-to-all-done.3.bands_ref = bf16[8,80,128]{2,1,0:T(8,128)(2,1)S(1)} async-done(((bf16[8,80,128]{2,1,0:T(8,128)(2,1)}), bf16[8,80,128]{2,1,0:T(8,128)(2,1)S(1)}, u32[]{:S(2)}, u32[]{:S(2)}) %all-to-all-start.3) | async-done | bytes 163872 | tf_op jit(solution)/shard_map/all_to_all | solution.py:25
  102.0 0.4 left_side.1
  102.5 7.7 %all_to_all.30.sums_ref = f32[8,8,128]{2,1,0:T(8,128)S(1)} all-to-all(f32[8,8,128]{2,1,0:T(8,128)S(1)} %get-tuple-element.20), channel_id=1, replica_groups=mesh['x'=4,'zh'=8,'zl'=2,'mp'=8] {'x','zl'}, dimensions={0} | all-to-all | bytes 65536 | tf_op jit(solution)/shard_map/all_to_all | solution.py:25
  110.2 1.9 %new_weights.1 = (bf16[64,64,128]{2,1,0:T(8,128)(2,1)}, f32[512,128]{1,0:T(8,128)S(1)}) custom-call(s32[16]{0:T(128)S(1)} %copy-done.2, s32[16,2]{1,0:T(8,128)S(1)} %copy.28.extent_ref, f32[8,8,128]{2,1,0:T(8,128)S(1)} %all_to_all.30.sums_ref, f32[512,128]{1,0:T(8,128)S(1)} %get-tuple-element.21.precond_ref, f32[512,128]{1,0:T(8,128)S(1)} %get-tuple-element.22.base_ref), custom_call_target="tpu_custom_call" | custom-call | tf_op jit(solution)/shard_map/new_weights/pallas_call | solution.py:198
  112.1 9.2 %all-to-all-start.5 = ((bf16[64,64,128]{2,1,0:T(8,128)(2,1)}), bf16[64,64,128]{2,1,0:T(8,128)(2,1)S(1)}, u32[]{:S(2)}, u32[]{:S(2)}) async-start(bf16[64,64,128]{2,1,0:T(8,128)(2,1)} %get-tuple-element.24), calls=%async_computation.5 | async-start | bytes 2097152 | tf_op jit(solution)/shard_map/all_to_all | solution.py:25
  121.9 0.6 multiply_subtract_fusion
  122.5 16.9 %all-to-all-done.5.back_ref = bf16[64,64,128]{2,1,0:T(8,128)(2,1)S(1)} async-done(((bf16[64,64,128]{2,1,0:T(8,128)(2,1)}), bf16[64,64,128]{2,1,0:T(8,128)(2,1)S(1)}, u32[]{:S(2)}, u32[]{:S(2)}) %all-to-all-start.5) | async-done | bytes 1048608 | tf_op jit(solution)/shard_map/all_to_all | solution.py:25
  139.4 2.0 %blocks_in_order.1 = bf16[16,64,512]{2,1,0:T(8,128)(2,1)} custom-call(s32[16]{0:T(128)S(1)} %copy-done.2, bf16[64,64,128]{2,1,0:T(8,128)(2,1)S(1)} %all-to-all-done.5.back_ref, bf16[2,256,128]{2,1,0:T(8,128)(2,1)S(1)} %and_convert_fusion.place_ref), custom_call_target="tpu_custom_call" | custom-call | tf_op jit(solution)/shard_map/blocks_in_order/pallas_call | solution.py:198
  (40 shorter events, 1.0 us)
Async XLA Ops:
  0.6 0.7 copy-start.2
  1.3 1.2 copy-start
  4.6 11.2 %copy-start.5 = (bf16[2,512,8]{1,2,0:T(8,128)(2,1)S(1)}, bf16[2,512,8]{1,2,0:T(8,128)(2,1)}, u32[]{:S(2)}) copy-start(bf16[2,512,8]{1,2,0:T(8,128)(2,1)} %param.11) | copy-start | bytes 49156
  4.6 25.1 %copy-start.3 = (f32[2,512,8]{1,2,0:T(8,128)S(1)}, f32[2,512,8]{1,2,0:T(8,128)}, u32[]{:S(2)}) copy-start(f32[2,512,8]{1,2,0:T(8,128)} %param.13) | copy-start | bytes 98308
  4.6 25.1 %copy-start.4 = (f32[2,512,8]{1,2,0:T(8,128)S(1)}, f32[2,512,8]{1,2,0:T(8,128)}, u32[]{:S(2)}) copy-start(f32[2,512,8]{1,2,0:T(8,128)} %param.12) | copy-start | bytes 98308
  4.6 35.8 %all-to-all-start = ((bf16[64,64,128]{2,1,0:T(8,128)(2,1)}), bf16[64,64,128]{2,1,0:T(8,128)(2,1)S(1)}, u32[]{:S(2)}, u32[]{:S(2)}) async-start(bf16[64,64,128]{2,1,0:T(8,128)(2,1)} %blocks_to_owners.1), calls=%async_computation | async-start | bytes 2097152 | tf_op jit(solution)/shard_map/all_to_all | solution.py:25
  15.7 24.6 %collective-permute-start = (bf16[1,2,8,512]{3,2,1,0:T(8,128)(2,1)S(1)}, bf16[1,2,8,512]{3,2,1,0:T(8,128)(2,1)S(1)}, u32[]{:S(2)}, u32[]{:S(2)}) collective-permute-start(bf16[1,2,8,512]{3,2,1,0:T(8,128)(2,1)S(1)} %bitcast.53), channel_id=1, source_target_pairs={{0,64},{16,80},{32,96},{48,112},{64,0},{80,16},{96,32},{112,48},{1... | collective-permute-start | bytes 49160 | tf_op jit(solution)/shard_map/ppermute | solution.py:231
  41.4 14.1 %copy-start.6 = (s32[16,2]{0,1:T(2,128)S(1)}, s32[16,2]{0,1:T(2,128)}, u32[]{:S(2)}) copy-start(s32[16,2]{0,1:T(2,128)} %param.9) | copy-start | bytes 388
  41.4 27.6 %all-to-all-start.1 = ((f16[8,128,128]{2,1,0:T(8,128)(2,1)}), f16[8,128,128]{2,1,0:T(8,128)(2,1)S(1)}, u32[]{:S(2)}, u32[]{:S(2)}) async-start(f16[8,128,128]{2,1,0:T(8,128)(2,1)} %pad_maximum_fusion), calls=%async_computation.1 | async-start | bytes 524288 | tf_op jit(solution)/shard_map/all_to_all | solution.py:25
  48.3 18.8 %collective-permute-start.1 = (bf16[2,2,8,512]{3,2,1,0:T(8,128)(2,1)S(1)}, bf16[2,2,8,512]{3,2,1,0:T(8,128)(2,1)S(1)}, u32[]{:S(2)}, u32[]{:S(2)}) collective-permute-start(bf16[2,2,8,512]{3,2,1,0:T(8,128)(2,1)S(1)} %maximum_bitcast_fusion), channel_id=1, source_target_pairs={{0,32},{16,48},{32,0},{48,16},{64,96},{80,112},{96,64},{112,80},{1... | collective-permute-start | bytes 98312 | tf_op jit(solution)/shard_map/ppermute | solution.py:231
  67.1 6.8 %collective-permute-start.2 = (bf16[4,2,8,512]{3,2,1,0:T(8,128)(2,1)S(1)}, bf16[4,2,8,512]{3,2,1,0:T(8,128)(2,1)S(1)}, u32[]{:S(2)}, u32[]{:S(2)}) collective-permute-start(bf16[4,2,8,512]{3,2,1,0:T(8,128)(2,1)S(1)} %bitcast.50), channel_id=1, source_target_pairs={{0,16},{16,0},{32,48},{48,32},{64,80},{80,64},{96,112},{112,96},{1... | collective-permute-start | bytes 196616 | tf_op jit(solution)/shard_map/ppermute | solution.py:231
  70.4 8.9 %all-to-all-start.2 = ((bf16[8,64,128]{2,1,0:T(8,128)(2,1)}), bf16[8,64,128]{2,1,0:T(8,128)(2,1)S(1)}, u32[]{:S(2)}, u32[]{:S(2)}) async-start(bf16[8,64,128]{2,1,0:T(8,128)(2,1)} %get-tuple-element.17), calls=%async_computation.2 | async-start | bytes 262144 | tf_op jit(solution)/shard_map/all_to_all | solution.py:25
  73.8 28.2 %copy-start.1 = (bf16[2,512,512]{2,1,0:T(8,128)(2,1)S(1)}, bf16[2,512,512]{2,1,0:T(8,128)(2,1)}, u32[]{:S(2)}) copy-start(bf16[2,512,512]{2,1,0:T(8,128)(2,1)} %left_ref.1) | copy-start | bytes 3145732
  80.2 21.8 %all-to-all-start.3 = ((bf16[8,80,128]{2,1,0:T(8,128)(2,1)}), bf16[8,80,128]{2,1,0:T(8,128)(2,1)S(1)}, u32[]{:S(2)}, u32[]{:S(2)}) async-start(bf16[8,80,128]{2,1,0:T(8,128)(2,1)} %right_side.1), calls=%async_computation.3 | async-start | bytes 327680 | tf_op jit(solution)/shard_map/all_to_all | solution.py:25
  112.1 27.3 %all-to-all-start.5 = ((bf16[64,64,128]{2,1,0:T(8,128)(2,1)}), bf16[64,64,128]{2,1,0:T(8,128)(2,1)S(1)}, u32[]{:S(2)}, u32[]{:S(2)}) async-start(bf16[64,64,128]{2,1,0:T(8,128)(2,1)} %get-tuple-element.24), calls=%async_computation.5 | async-start | bytes 2097152 | tf_op jit(solution)/shard_map/all_to_all | solution.py:25

commit v5 on v4

--- a/solution.py
+++ b/solution.py
@@ -16,9 +16,8 @@
 f32 = jnp.float32
 bf16 = jnp.bfloat16
 in_vmem = pl.BlockSpec(memory_space=pltpu.VMEM)
-anywhere = pl.BlockSpec(memory_space=pl.ANY)
+in_hbm = pl.BlockSpec(memory_space=pltpu.HBM)
 in_smem = pl.BlockSpec(memory_space=pltpu.SMEM)
-params = pltpu.CompilerParams(vmem_limit_bytes=24 * 2**20)
 
 
 def exchange(value, axes):
@@ -29,12 +28,13 @@
     return jnp.broadcast_to(value[None], (count,) + value.shape)
 
 
-def bounds_of(slot, owner_ref, extent_ref):
+def bounds_of(slot, meta_ref):
     height, width = jnp.int32(0), jnp.int32(0)
-    for b in range(owner_ref.shape[0]):
-        hit = owner_ref[b] == slot
-        height = jnp.where(hit, extent_ref[b, 0], height)
-        width = jnp.where(hit, extent_ref[b, 1], width)
+    blocks = meta_ref.shape[0] // 3
+    for b in range(blocks):
+        hit = meta_ref[b] == slot
+        height = jnp.where(hit, meta_ref[blocks + b], height)
+        width = jnp.where(hit, meta_ref[2 * blocks + b], width)
     return height, width
 
 
@@ -42,18 +42,29 @@
     return lax.broadcasted_iota(jnp.int32, shape, dim)
 
 
-def send_kernel(nx, nm, owned, owner_ref, grads_ref, out_ref, sem):
+def send_kernel(
+    nx, nm, owned, slots_ref, grads_ref, out_ref, owner_ref, held_ref, sem_slots, sem_in, sem_out
+):
     blocks, rows, width = grads_ref.shape
     cols = width // nx
+    slots = pltpu.make_async_copy(slots_ref, owner_ref, sem_slots)
+    slots.start()
+    reads = []
+    for b in range(blocks):
+        read = pltpu.make_async_copy(grads_ref.at[b], held_ref.at[b], sem_in.at[b])
+        read.start()
+        reads.append(read)
+    slots.wait()
     copies = []
     for b in range(blocks):
         slot = owner_ref[b]
         owner, place = slot // owned, slot % owned
+        reads[b].wait()
         for x in range(nx):
             copy = pltpu.make_async_copy(
-                grads_ref.at[b, :, x * cols : (x + 1) * cols],
+                held_ref.at[b, :, x * cols : (x + 1) * cols],
                 out_ref.at[(x * owned + place) * nm + owner],
-                sem.at[b * nx + x],
+                sem_out.at[b * nx + x],
             )
             copy.start()
             copies.append(copy)
@@ -61,11 +72,11 @@
         copy.wait()
 
 
-def grad_kernel(owned, owner_ref, extent_ref, pieces_ref, out_ref, sq_ref):
+def grad_kernel(owned, meta_ref, pieces_ref, out_ref, sq_ref):
     _, rows, cols = pieces_ref.shape
     x, zh = lax.axis_index("x"), lax.axis_index("zh")
     zl, m = lax.axis_index("zl"), lax.axis_index("mp")
-    height, width = bounds_of(m * owned + zl, owner_ref, extent_ref)
+    height, width = bounds_of(m * owned + zl, meta_ref)
     total = pieces_ref[0]
     for i in range(1, pieces_ref.shape[0]):
         total = total + pieces_ref[i]
@@ -128,7 +139,7 @@
 
 
 def fresh_kernel(
-    nm, owned, slab, owner_ref, extent_ref, sums_ref, precond_ref, base_ref, out_ref, step_ref, held_ref, sem
+    nm, owned, slab, meta_ref, sums_ref, precond_ref, base_ref, out_ref, step_ref, held_ref, sem
 ):
     width, lanes = precond_ref.shape
     mine = lanes // owned
@@ -148,10 +159,11 @@
             grad_rows = grad_rows + sums_ref[g]
         grad_sq = jnp.sum(grad_rows[0:1], axis=1, keepdims=True)
         pre_sq = jnp.sum(jnp.where(place == s, total[1:2], 0.0), axis=1, keepdims=True)
-        tall, wide = bounds_of(m * owned + s, owner_ref, extent_ref)
+        tall, wide = bounds_of(m * owned + s, meta_ref)
         scale = jnp.where(place == s, jnp.sqrt(grad_sq / (pre_sq + epsilon)), scale)
         height = jnp.where(place == s, jnp.where(column < wide, tall, 0), height)
     rows = width // nm
+    copies = []
     for i in range(nm):
         at = slice(i * rows, (i + 1) * rows)
         ok = i * rows + iota((rows, lanes), 0) < height
@@ -159,21 +171,26 @@
         step_ref[at] = step
         fresh = (base_ref[at] - step_rate * step).astype(bf16)
         held_ref[i] = fresh
-    copies = []
-    for g in range(ng):
-        copy = pltpu.make_async_copy(held_ref, out_ref.at[g * nm : (g + 1) * nm], sem.at[g])
-        copy.start()
-        copies.append(copy)
+        if i % 2 == 0:
+            continue
+        for g in range(ng):
+            copy = pltpu.make_async_copy(
+                held_ref.at[i - 1 : i + 1],
+                out_ref.at[g * nm + i - 1 : g * nm + i + 1],
+                sem.at[i // 2 * ng + g],
+            )
+            copy.start()
+            copies.append(copy)
     for copy in copies:
         copy.wait()
 
 
-def place_kernel(nx, nm, owned, owner_ref, back_ref, place_ref, out_ref, held_ref, sem):
+def place_kernel(nx, nm, owned, meta_ref, back_ref, place_ref, out_ref, held_ref, sem):
     blocks, rows, width = out_ref.shape
     cols = width // nx
     copies = []
     for b in range(blocks):
-        slot = owner_ref[b]
+        slot = meta_ref[b]
         owner, s = slot // owned, slot % owned
         lanes = []
         for zl in range(owned):
@@ -191,17 +208,17 @@
         copy.wait()
 
 
-def call(kernel, name, out, *args, scratch=(), far=(), far_out=()):
+def call(kernel, name, out, *args, scratch=(), far=(), far_out=(), vmem=24):
     specs = [in_smem if a.dtype == jnp.int32 else in_vmem for a in args]
     for i in far:
-        specs[i] = anywhere
+        specs[i] = in_hbm
     return pl.pallas_call(
         kernel,
         out_shape=out,
         in_specs=specs,
-        out_specs=[anywhere if i in far_out else in_vmem for i in range(len(out))],
+        out_specs=[in_hbm if i in far_out else in_vmem for i in range(len(out))],
         scratch_shapes=list(scratch),
-        compiler_params=params,
+        compiler_params=pltpu.CompilerParams(vmem_limit_bytes=vmem * 2**20),
         name=name,
     )(*args)
 
@@ -252,9 +269,16 @@
             [shape((ng * nm, rows, cols), bf16)],
             owner_slot,
             partial_grads[0],
-            scratch=[pltpu.SemaphoreType.DMA((blocks * nx,))],
-            far=(1,),
+            scratch=[
+                pltpu.SMEM((blocks,), jnp.int32),
+                pltpu.VMEM((blocks, rows, width), bf16),
+                pltpu.SemaphoreType.DMA,
+                pltpu.SemaphoreType.DMA((blocks,)),
+                pltpu.SemaphoreType.DMA((blocks * nx,)),
+            ],
+            far=(0, 1),
             far_out=(0,),
+            vmem=60,
         )
         roots, send = lax.optimization_barrier((roots, send))
         roots = swap(roots, strides[0])
@@ -265,7 +289,8 @@
         part = (part * sum_unit).astype(f16)
         base_rows = to_rows((base_t * base_unit).astype(f16))
         packed = jnp.concatenate([part, spread(base_rows, nzh)], axis=1)
-        roots, packed = lax.optimization_barrier((roots, packed))
+        meta = jnp.concatenate([owner_slot, extent[:, 0], extent[:, 1]])
+        meta, roots, packed = lax.optimization_barrier((meta, roots, packed))
         for stride in strides[1:]:
             roots = swap(roots, stride)
         roots = jnp.swapaxes(roots, 0, 1).reshape(owned, mine_cols, width)
@@ -276,8 +301,7 @@
             functools.partial(grad_kernel, owned),
             "masked_grad",
             (shape((ng, rows, cols), bf16), shape((8, cols), f32)),
-            owner_slot,
-            extent,
+            meta,
             pieces,
         )
         all_cols = exchange(grads, group)
@@ -303,12 +327,11 @@
             functools.partial(fresh_kernel, nm, owned, slab),
             "new_weights",
             (shape((ng * nm, rows, lanes), bf16), shape((width, lanes), f32)),
-            owner_slot,
-            extent,
+            meta,
             sums,
             precond,
             base,
-            scratch=[pltpu.VMEM((nm, rows, lanes), bf16), pltpu.SemaphoreType.DMA((ng,))],
+            scratch=[pltpu.VMEM((nm, rows, lanes), bf16), pltpu.SemaphoreType.DMA((nm // 2 * ng,))],
             far_out=(0,),
         )
         back = exchange(fresh, wide)
@@ -324,7 +347,7 @@
             functools.partial(place_kernel, nx, nm, owned),
             "blocks_in_order",
             [shape((blocks, rows, width), bf16)],
-            owner_slot,
+            meta,
             back,
             place.astype(bf16),
             scratch=[pltpu.VMEM((blocks, rows, width), bf16), pltpu.SemaphoreType.DMA((blocks,))],

time: 142 us -> 141 us (level)
  no operation moved by 1% of the time
where the time goes in v5:
time: 141 us; the launch traced here: 140 us
  starting transfers between devices  61.4 us (44%)
  waiting for transfers between devices  57.5 us (41%)
  Pallas kernels  9.24 us (7%)
  blocking collectives  7.7 us (5%)
  other arithmetic  2.14 us (2%)
    all_to_all x5, starting transfers between devices, exchange(): return lax.all_to_all(value, axes, split_axis=0, concat_axis=0, tiled=True)  38.3 us
    all_to_all x5, waiting for transfers between devices, exchange(): return lax.all_to_all(value, axes, split_axis=0, concat_axis=0, tiled=True)  36.1 us
    ppermute x3, starting transfers between devices, swap(): other = lax.ppermute(held, 'zh', pairs)  23.1 us
    ppermute x3, waiting for transfers between devices, swap(): other = lax.ppermute(held, 'zh', pairs)  21.4 us
    pallas_call x6, Pallas kernels, call(): pl.pallas_call(kernel, out_shape=out, in_specs=specs, out_specs=[in_hbm i...  9.24 us
    all_to_all x1, blocking collectives, exchange(): return lax.all_to_all(value, axes, split_axis=0, concat_axis=0, tiled=True)  7.7 us
  transfers between devices with their start and end apart: 8, of which 5 were waited for; matrix products, arithmetic and copies ran while one was open for 1% of the time, Pallas kernels for 1%

profile of v5, /device:TPU:1, one launch (start us, length us, event | category | flops | bytes accessed | tf_op | source)
XLA Modules:
  0.0 139.9 jit_solution(9564108256603837733)
XLA Ops:
  0.6 2.6 %blocks_to_owners.1 = bf16[64,64,128]{2,1,0:T(8,128)(2,1)} custom-call(s32[16]{0:T(128)} %slots_ref.1, bf16[16,64,512]{2,1,0:T(8,128)(2,1)} %bitcast.51), custom_call_target="tpu_custom_call" | custom-call | tf_op jit(solution)/shard_map/blocks_to_owners/pallas_call | solution.py:215
  3.3 11.1 %all-to-all-start = ((bf16[64,64,128]{2,1,0:T(8,128)(2,1)}), bf16[64,64,128]{2,1,0:T(8,128)(2,1)S(1)}, u32[]{:S(2)}, u32[]{:S(2)}) async-start(bf16[64,64,128]{2,1,0:T(8,128)(2,1)} %blocks_to_owners.1), calls=%async_computation | async-start | bytes 2097152 | tf_op jit(solution)/shard_map/all_to_all | solution.py:24
  14.4 13.9 %collective-permute-start = (bf16[1,2,8,512]{3,2,1,0:T(8,128)(2,1)S(1)}, bf16[1,2,8,512]{3,2,1,0:T(8,128)(2,1)S(1)}, u32[]{:S(2)}, u32[]{:S(2)}) collective-permute-start(bf16[1,2,8,512]{3,2,1,0:T(8,128)(2,1)S(1)} %bitcast.57), channel_id=1, source_target_pairs={{0,64},{16,80},{32,96},{48,112},{64,0},{80,16},{96,32},{112,48},{1... | collective-permute-start | bytes 49160 | tf_op jit(solution)/shard_map/ppermute | solution.py:248
  28.4 0.6 copy-done.4
  29.2 9.9 %collective-permute-done = bf16[1,2,8,512]{3,2,1,0:T(8,128)(2,1)S(1)} collective-permute-done((bf16[1,2,8,512]{3,2,1,0:T(8,128)(2,1)S(1)}, bf16[1,2,8,512]{3,2,1,0:T(8,128)(2,1)S(1)}, u32[]{:S(2)}, u32[]{:S(2)}) %collective-permute-start) | collective-permute-done | bytes 16416 | tf_op jit(solution)/shard_map/ppermute | solution.py:248
  39.1 0.2 multiply_convert_fusion
  39.3 0.8 pad_maximum_fusion
  40.1 6.7 %all-to-all-start.1 = ((f16[8,128,128]{2,1,0:T(8,128)(2,1)}), f16[8,128,128]{2,1,0:T(8,128)(2,1)S(1)}, u32[]{:S(2)}, u32[]{:S(2)}) async-start(f16[8,128,128]{2,1,0:T(8,128)(2,1)} %pad_maximum_fusion), calls=%async_computation.1 | async-start | bytes 524288 | tf_op jit(solution)/shard_map/all_to_all | solution.py:24
  46.8 7.3 %collective-permute-start.1 = (bf16[2,2,8,512]{3,2,1,0:T(8,128)(2,1)S(1)}, bf16[2,2,8,512]{3,2,1,0:T(8,128)(2,1)S(1)}, u32[]{:S(2)}, u32[]{:S(2)}) collective-permute-start(bf16[2,2,8,512]{3,2,1,0:T(8,128)(2,1)S(1)} %maximum_bitcast_fusion), channel_id=1, source_target_pairs={{0,32},{16,48},{32,0},{48,16},{64,96},{80,112},{96,64},{112,80},{1... | collective-permute-start | bytes 98312 | tf_op jit(solution)/shard_map/ppermute | solution.py:248
  54.1 11.5 %collective-permute-done.1 = bf16[2,2,8,512]{3,2,1,0:T(8,128)(2,1)S(1)} collective-permute-done((bf16[2,2,8,512]{3,2,1,0:T(8,128)(2,1)S(1)}, bf16[2,2,8,512]{3,2,1,0:T(8,128)(2,1)S(1)}, u32[]{:S(2)}, u32[]{:S(2)}) %collective-permute-start.1) | collective-permute-done | bytes 32800 | tf_op jit(solution)/shard_map/ppermute | solution.py:248
  65.6 1.9 %collective-permute-start.2 = (bf16[4,2,8,512]{3,2,1,0:T(8,128)(2,1)S(1)}, bf16[4,2,8,512]{3,2,1,0:T(8,128)(2,1)S(1)}, u32[]{:S(2)}, u32[]{:S(2)}) collective-permute-start(bf16[4,2,8,512]{3,2,1,0:T(8,128)(2,1)S(1)} %bitcast.54), channel_id=1, source_target_pairs={{0,16},{16,0},{32,48},{48,32},{64,80},{80,64},{96,112},{112,96},{1... | collective-permute-start | bytes 196616 | tf_op jit(solution)/shard_map/ppermute | solution.py:248
  67.6 1.2 masked_grad.1
  68.8 3.4 %all-to-all-start.2 = ((bf16[8,64,128]{2,1,0:T(8,128)(2,1)}), bf16[8,64,128]{2,1,0:T(8,128)(2,1)S(1)}, u32[]{:S(2)}, u32[]{:S(2)}) async-start(bf16[8,64,128]{2,1,0:T(8,128)(2,1)} %get-tuple-element.19), calls=%async_computation.2 | async-start | bytes 262144 | tf_op jit(solution)/shard_map/all_to_all | solution.py:24
  72.3 5.4 %all-to-all-done.2.cols_ref = bf16[8,64,128]{2,1,0:T(8,128)(2,1)S(1)} async-done(((bf16[8,64,128]{2,1,0:T(8,128)(2,1)}), bf16[8,64,128]{2,1,0:T(8,128)(2,1)S(1)}, u32[]{:S(2)}, u32[]{:S(2)}) %all-to-all-start.2) | async-done | bytes 131104 | tf_op jit(solution)/shard_map/all_to_all | solution.py:24
  77.7 0.9 right_side.1
  78.6 7.9 %all-to-all-start.3 = ((bf16[8,80,128]{2,1,0:T(8,128)(2,1)}), bf16[8,80,128]{2,1,0:T(8,128)(2,1)S(1)}, u32[]{:S(2)}, u32[]{:S(2)}) async-start(bf16[8,80,128]{2,1,0:T(8,128)(2,1)} %right_side.1), calls=%async_computation.3 | async-start | bytes 327680 | tf_op jit(solution)/shard_map/all_to_all | solution.py:24
  86.6 13.9 %all-to-all-done.3.bands_ref = bf16[8,80,128]{2,1,0:T(8,128)(2,1)S(1)} async-done(((bf16[8,80,128]{2,1,0:T(8,128)(2,1)}), bf16[8,80,128]{2,1,0:T(8,128)(2,1)S(1)}, u32[]{:S(2)}, u32[]{:S(2)}) %all-to-all-start.3) | async-done | bytes 163872 | tf_op jit(solution)/shard_map/all_to_all | solution.py:24
  100.4 0.4 left_side.1
  100.9 7.7 %all_to_all.30.sums_ref = f32[8,8,128]{2,1,0:T(8,128)S(1)} all-to-all(f32[8,8,128]{2,1,0:T(8,128)S(1)} %get-tuple-element.22), channel_id=1, replica_groups=mesh['x'=4,'zh'=8,'zl'=2,'mp'=8] {'x','zl'}, dimensions={0} | all-to-all | bytes 65536 | tf_op jit(solution)/shard_map/all_to_all | solution.py:24
  108.6 2.0 %new_weights.1 = (bf16[64,64,128]{2,1,0:T(8,128)(2,1)}, f32[512,128]{1,0:T(8,128)S(1)}) custom-call(s32[48]{0:T(128)S(1)} %pad_add_fusion.meta_ref, f32[8,8,128]{2,1,0:T(8,128)S(1)} %all_to_all.30.sums_ref, f32[512,128]{1,0:T(8,128)S(1)} %get-tuple-element.23.precond_ref, f32[512,128]{1,0:T(8,128)S(1)} %get-tuple-element.24.base_ref), custom_call_target="tpu_custom_call" | custom-call | tf_op jit(solution)/shard_map/new_weights/pallas_call | solution.py:215
  110.6 9.2 %all-to-all-start.5 = ((bf16[64,64,128]{2,1,0:T(8,128)(2,1)}), bf16[64,64,128]{2,1,0:T(8,128)(2,1)S(1)}, u32[]{:S(2)}, u32[]{:S(2)}) async-start(bf16[64,64,128]{2,1,0:T(8,128)(2,1)} %get-tuple-element.26), calls=%async_computation.5 | async-start | bytes 2097152 | tf_op jit(solution)/shard_map/all_to_all | solution.py:24
  120.3 0.6 multiply_subtract_fusion
  120.9 16.9 %all-to-all-done.5.back_ref = bf16[64,64,128]{2,1,0:T(8,128)(2,1)S(1)} async-done(((bf16[64,64,128]{2,1,0:T(8,128)(2,1)}), bf16[64,64,128]{2,1,0:T(8,128)(2,1)S(1)}, u32[]{:S(2)}, u32[]{:S(2)}) %all-to-all-start.5) | async-done | bytes 1048608 | tf_op jit(solution)/shard_map/all_to_all | solution.py:24
  137.8 2.0 %blocks_in_order.1 = bf16[16,64,512]{2,1,0:T(8,128)(2,1)} custom-call(s32[48]{0:T(128)S(1)} %pad_add_fusion.meta_ref, bf16[64,64,128]{2,1,0:T(8,128)(2,1)S(1)} %all-to-all-done.5.back_ref, bf16[2,256,128]{2,1,0:T(8,128)(2,1)S(1)} %and_convert_fusion.place_ref), custom_call_target="tpu_custom_call" | custom-call | tf_op jit(solution)/shard_map/blocks_in_order/pallas_call | solution.py:215
  (39 shorter events, 0.8 us)
Async XLA Ops:
  3.2 11.2 %copy-start.3 = (bf16[2,512,8]{1,2,0:T(8,128)(2,1)S(1)}, bf16[2,512,8]{1,2,0:T(8,128)(2,1)}, u32[]{:S(2)}) copy-start(bf16[2,512,8]{1,2,0:T(8,128)(2,1)} %param.11) | copy-start | bytes 49156
  3.2 25.1 %copy-start.5 = (s32[16,2]{0,1:T(2,128)S(1)}, s32[16,2]{0,1:T(2,128)}, u32[]{:S(2)}) copy-start(s32[16,2]{0,1:T(2,128)} %param.9) | copy-start | bytes 388
  3.2 25.1 %copy-start.1 = (f32[2,512,8]{1,2,0:T(8,128)S(1)}, f32[2,512,8]{1,2,0:T(8,128)}, u32[]{:S(2)}) copy-start(f32[2,512,8]{1,2,0:T(8,128)} %param.13) | copy-start | bytes 98308
  3.3 25.1 %copy-start.2 = (f32[2,512,8]{1,2,0:T(8,128)S(1)}, f32[2,512,8]{1,2,0:T(8,128)}, u32[]{:S(2)}) copy-start(f32[2,512,8]{1,2,0:T(8,128)} %param.12) | copy-start | bytes 98308
  3.3 35.8 %all-to-all-start = ((bf16[64,64,128]{2,1,0:T(8,128)(2,1)}), bf16[64,64,128]{2,1,0:T(8,128)(2,1)S(1)}, u32[]{:S(2)}, u32[]{:S(2)}) async-start(bf16[64,64,128]{2,1,0:T(8,128)(2,1)} %blocks_to_owners.1), calls=%async_computation | async-start | bytes 2097152 | tf_op jit(solution)/shard_map/all_to_all | solution.py:24
  14.4 24.6 %collective-permute-start = (bf16[1,2,8,512]{3,2,1,0:T(8,128)(2,1)S(1)}, bf16[1,2,8,512]{3,2,1,0:T(8,128)(2,1)S(1)}, u32[]{:S(2)}, u32[]{:S(2)}) collective-permute-start(bf16[1,2,8,512]{3,2,1,0:T(8,128)(2,1)S(1)} %bitcast.57), channel_id=1, source_target_pairs={{0,64},{16,80},{32,96},{48,112},{64,0},{80,16},{96,32},{112,48},{1... | collective-permute-start | bytes 49160 | tf_op jit(solution)/shard_map/ppermute | solution.py:248
  28.4 0.7 copy-start.4
  40.1 27.5 %all-to-all-start.1 = ((f16[8,128,128]{2,1,0:T(8,128)(2,1)}), f16[8,128,128]{2,1,0:T(8,128)(2,1)S(1)}, u32[]{:S(2)}, u32[]{:S(2)}) async-start(f16[8,128,128]{2,1,0:T(8,128)(2,1)} %pad_maximum_fusion), calls=%async_computation.1 | async-start | bytes 524288 | tf_op jit(solution)/shard_map/all_to_all | solution.py:24
  46.8 18.8 %collective-permute-start.1 = (bf16[2,2,8,512]{3,2,1,0:T(8,128)(2,1)S(1)}, bf16[2,2,8,512]{3,2,1,0:T(8,128)(2,1)S(1)}, u32[]{:S(2)}, u32[]{:S(2)}) collective-permute-start(bf16[2,2,8,512]{3,2,1,0:T(8,128)(2,1)S(1)} %maximum_bitcast_fusion), channel_id=1, source_target_pairs={{0,32},{16,48},{32,0},{48,16},{64,96},{80,112},{96,64},{112,80},{1... | collective-permute-start | bytes 98312 | tf_op jit(solution)/shard_map/ppermute | solution.py:248
  65.6 6.6 %collective-permute-start.2 = (bf16[4,2,8,512]{3,2,1,0:T(8,128)(2,1)S(1)}, bf16[4,2,8,512]{3,2,1,0:T(8,128)(2,1)S(1)}, u32[]{:S(2)}, u32[]{:S(2)}) collective-permute-start(bf16[4,2,8,512]{3,2,1,0:T(8,128)(2,1)S(1)} %bitcast.54), channel_id=1, source_target_pairs={{0,16},{16,0},{32,48},{48,32},{64,80},{80,64},{96,112},{112,96},{1... | collective-permute-start | bytes 196616 | tf_op jit(solution)/shard_map/ppermute | solution.py:248
  68.8 8.9 %all-to-all-start.2 = ((bf16[8,64,128]{2,1,0:T(8,128)(2,1)}), bf16[8,64,128]{2,1,0:T(8,128)(2,1)S(1)}, u32[]{:S(2)}, u32[]{:S(2)}) async-start(bf16[8,64,128]{2,1,0:T(8,128)(2,1)} %get-tuple-element.19), calls=%async_computation.2 | async-start | bytes 262144 | tf_op jit(solution)/shard_map/all_to_all | solution.py:24
  72.2 28.2 %copy-start = (bf16[2,512,512]{2,1,0:T(8,128)(2,1)S(1)}, bf16[2,512,512]{2,1,0:T(8,128)(2,1)}, u32[]{:S(2)}) copy-start(bf16[2,512,512]{2,1,0:T(8,128)(2,1)} %left_ref.1) | copy-start | bytes 3145732
  78.6 21.8 %all-to-all-start.3 = ((bf16[8,80,128]{2,1,0:T(8,128)(2,1)}), bf16[8,80,128]{2,1,0:T(8,128)(2,1)S(1)}, u32[]{:S(2)}, u32[]{:S(2)}) async-start(bf16[8,80,128]{2,1,0:T(8,128)(2,1)} %right_side.1), calls=%async_computation.3 | async-start | bytes 327680 | tf_op jit(solution)/shard_map/all_to_all | solution.py:24
  110.6 27.2 %all-to-all-start.5 = ((bf16[64,64,128]{2,1,0:T(8,128)(2,1)}), bf16[64,64,128]{2,1,0:T(8,128)(2,1)S(1)}, u32[]{:S(2)}, u32[]{:S(2)}) async-start(bf16[64,64,128]{2,1,0:T(8,128)(2,1)} %get-tuple-element.26), calls=%async_computation.5 | async-start | bytes 2097152 | tf_op jit(solution)/shard_map/all_to_all | solution.py:24

commit v6 on v5

--- a/solution.py
+++ b/solution.py
@@ -313,6 +313,7 @@
             roots,
             sq,
         )
+        base_t, packed = lax.optimization_barrier((base_t, packed))
         bands = exchange(packed, "zh")
         precond, base, sums = call(
             left_kernel,

time: 141 us -> 140 us (level)
  blocking collectives: 7.7 us -> 29.3 us
  waiting for transfers between devices: 57.5 us -> 43.6 us
  starting transfers between devices: 61.4 us -> 53.5 us
    all_to_all x1 -> x2, blocking collectives: 7.7 us -> 29.3 us  [exchange(): return lax.all_to_all(value, axes, split_axis=0, concat_axis=0, tiled=True)]
    all_to_all x5 -> x4, waiting for transfers between devices: 36.1 us -> 22.2 us  [exchange(): return lax.all_to_all(value, axes, split_axis=0, concat_axis=0, tiled=True)]
    all_to_all x5 -> x4, starting transfers between devices: 38.3 us -> 30.4 us  [exchange(): return lax.all_to_all(value, axes, split_axis=0, concat_axis=0, tiled=True)]
  transfers between devices with their start and end apart: 8 -> 7, of which waited for: 5 -> 4; matrix products, arithmetic and copies ran while one was open for 1% -> 1% of each run, Pallas kernels for 1% -> 1%
where the time goes in v6:
time: 140 us; the launch traced here: 139 us
  starting transfers between devices  53.5 us (38%)
  waiting for transfers between devices  43.6 us (31%)
  blocking collectives  29.3 us (21%)
  Pallas kernels  8.58 us (6%)
  other arithmetic  2.14 us (2%)
    all_to_all x4, starting transfers between devices, exchange(): return lax.all_to_all(value, axes, split_axis=0, concat_axis=0, tiled=True)  30.4 us
    all_to_all x2, blocking collectives, exchange(): return lax.all_to_all(value, axes, split_axis=0, concat_axis=0, tiled=True)  29.3 us
    ppermute x3, starting transfers between devices, swap(): other = lax.ppermute(held, 'zh', pairs)  23.1 us
    all_to_all x4, waiting for transfers between devices, exchange(): return lax.all_to_all(value, axes, split_axis=0, concat_axis=0, tiled=True)  22.2 us
    ppermute x3, waiting for transfers between devices, swap(): other = lax.ppermute(held, 'zh', pairs)  21.4 us
    pallas_call x6, Pallas kernels, call(): pl.pallas_call(kernel, out_shape=out, in_specs=specs, out_specs=[in_hbm i...  8.58 us
  transfers between devices with their start and end apart: 7, of which 4 were waited for; matrix products, arithmetic and copies ran while one was open for 1% of the time, Pallas kernels for 1%

profile of v6, /device:TPU:1, one launch (start us, length us, event | category | flops | bytes accessed | tf_op | source)
XLA Modules:
  0.0 139.0 jit_solution(5274180027744254499)
XLA Ops:
  0.6 2.6 %blocks_to_owners.1 = bf16[64,64,128]{2,1,0:T(8,128)(2,1)} custom-call(s32[16]{0:T(128)} %slots_ref.1, bf16[16,64,512]{2,1,0:T(8,128)(2,1)} %bitcast.51), custom_call_target="tpu_custom_call" | custom-call | tf_op jit(solution)/shard_map/blocks_to_owners/pallas_call | solution.py:215
  3.3 11.1 %all-to-all-start = ((bf16[64,64,128]{2,1,0:T(8,128)(2,1)}), bf16[64,64,128]{2,1,0:T(8,128)(2,1)S(1)}, u32[]{:S(2)}, u32[]{:S(2)}) async-start(bf16[64,64,128]{2,1,0:T(8,128)(2,1)} %blocks_to_owners.1), calls=%async_computation | async-start | bytes 2097152 | tf_op jit(solution)/shard_map/all_to_all | solution.py:24
  14.4 13.9 %collective-permute-start = (bf16[1,2,8,512]{3,2,1,0:T(8,128)(2,1)S(1)}, bf16[1,2,8,512]{3,2,1,0:T(8,128)(2,1)S(1)}, u32[]{:S(2)}, u32[]{:S(2)}) collective-permute-start(bf16[1,2,8,512]{3,2,1,0:T(8,128)(2,1)S(1)} %bitcast.57), channel_id=1, source_target_pairs={{0,64},{16,80},{32,96},{48,112},{64,0},{80,16},{96,32},{112,48},{1... | collective-permute-start | bytes 49160 | tf_op jit(solution)/shard_map/ppermute | solution.py:248
  28.4 0.6 copy-done.4
  29.2 9.9 %collective-permute-done = bf16[1,2,8,512]{3,2,1,0:T(8,128)(2,1)S(1)} collective-permute-done((bf16[1,2,8,512]{3,2,1,0:T(8,128)(2,1)S(1)}, bf16[1,2,8,512]{3,2,1,0:T(8,128)(2,1)S(1)}, u32[]{:S(2)}, u32[]{:S(2)}) %collective-permute-start) | collective-permute-done | bytes 16416 | tf_op jit(solution)/shard_map/ppermute | solution.py:248
  39.1 0.2 multiply_convert_fusion
  39.3 0.8 pad_maximum_fusion
  40.1 6.7 %all-to-all-start.1 = ((f16[8,128,128]{2,1,0:T(8,128)(2,1)}), f16[8,128,128]{2,1,0:T(8,128)(2,1)S(1)}, u32[]{:S(2)}, u32[]{:S(2)}) async-start(f16[8,128,128]{2,1,0:T(8,128)(2,1)} %pad_maximum_fusion), calls=%async_computation.1 | async-start | bytes 524288 | tf_op jit(solution)/shard_map/all_to_all | solution.py:24
  46.8 7.3 %collective-permute-start.1 = (bf16[2,2,8,512]{3,2,1,0:T(8,128)(2,1)S(1)}, bf16[2,2,8,512]{3,2,1,0:T(8,128)(2,1)S(1)}, u32[]{:S(2)}, u32[]{:S(2)}) collective-permute-start(bf16[2,2,8,512]{3,2,1,0:T(8,128)(2,1)S(1)} %maximum_bitcast_fusion), channel_id=1, source_target_pairs={{0,32},{16,48},{32,0},{48,16},{64,96},{80,112},{96,64},{112,80},{1... | collective-permute-start | bytes 98312 | tf_op jit(solution)/shard_map/ppermute | solution.py:248
  54.1 11.5 %collective-permute-done.1 = bf16[2,2,8,512]{3,2,1,0:T(8,128)(2,1)S(1)} collective-permute-done((bf16[2,2,8,512]{3,2,1,0:T(8,128)(2,1)S(1)}, bf16[2,2,8,512]{3,2,1,0:T(8,128)(2,1)S(1)}, u32[]{:S(2)}, u32[]{:S(2)}) %collective-permute-start.1) | collective-permute-done | bytes 32800 | tf_op jit(solution)/shard_map/ppermute | solution.py:248
  65.6 1.9 %collective-permute-start.2 = (bf16[4,2,8,512]{3,2,1,0:T(8,128)(2,1)S(1)}, bf16[4,2,8,512]{3,2,1,0:T(8,128)(2,1)S(1)}, u32[]{:S(2)}, u32[]{:S(2)}) collective-permute-start(bf16[4,2,8,512]{3,2,1,0:T(8,128)(2,1)S(1)} %bitcast.54), channel_id=1, source_target_pairs={{0,16},{16,0},{32,48},{48,32},{64,80},{80,64},{96,112},{112,96},{1... | collective-permute-start | bytes 196616 | tf_op jit(solution)/shard_map/ppermute | solution.py:248
  67.6 1.2 masked_grad.1
  68.8 3.4 %all-to-all-start.2 = ((bf16[8,64,128]{2,1,0:T(8,128)(2,1)}), bf16[8,64,128]{2,1,0:T(8,128)(2,1)S(1)}, u32[]{:S(2)}, u32[]{:S(2)}) async-start(bf16[8,64,128]{2,1,0:T(8,128)(2,1)} %get-tuple-element.21), calls=%async_computation.2 | async-start | bytes 262144 | tf_op jit(solution)/shard_map/all_to_all | solution.py:24
  72.3 5.3 %all-to-all-done.2.cols_ref = bf16[8,64,128]{2,1,0:T(8,128)(2,1)S(1)} async-done(((bf16[8,64,128]{2,1,0:T(8,128)(2,1)}), bf16[8,64,128]{2,1,0:T(8,128)(2,1)S(1)}, u32[]{:S(2)}, u32[]{:S(2)}) %all-to-all-start.2) | async-done | bytes 131104 | tf_op jit(solution)/shard_map/all_to_all | solution.py:24
  77.7 0.3 right_side.1
  78.0 21.6 %all_to_all.30.bands_ref = bf16[8,80,128]{2,1,0:T(8,128)(2,1)S(1)} all-to-all(bf16[8,80,128]{2,1,0:T(8,128)(2,1)S(1)} %right_side.1), channel_id=1, replica_groups=mesh['x'=4,'zh'=8,'zl'=2,'mp'=8] {'zh'}, dimensions={0} | all-to-all | bytes 327680 | tf_op jit(solution)/shard_map/all_to_all | solution.py:24
  99.6 0.4 left_side.1
  100.0 7.7 %all_to_all.31.sums_ref = f32[8,8,128]{2,1,0:T(8,128)S(1)} all-to-all(f32[8,8,128]{2,1,0:T(8,128)S(1)} %get-tuple-element.26), channel_id=1, replica_groups=mesh['x'=4,'zh'=8,'zl'=2,'mp'=8] {'x','zl'}, dimensions={0} | all-to-all | bytes 65536 | tf_op jit(solution)/shard_map/all_to_all | solution.py:24
  107.7 2.0 %new_weights.1 = (bf16[64,64,128]{2,1,0:T(8,128)(2,1)}, f32[512,128]{1,0:T(8,128)S(1)}) custom-call(s32[48]{0:T(128)S(1)} %pad_add_fusion.meta_ref, f32[8,8,128]{2,1,0:T(8,128)S(1)} %all_to_all.31.sums_ref, f32[512,128]{1,0:T(8,128)S(1)} %get-tuple-element.27.precond_ref, f32[512,128]{1,0:T(8,128)S(1)} %get-tuple-element.28.base_ref), custom_call_target="tpu_custom_call" | custom-call | tf_op jit(solution)/shard_map/new_weights/pallas_call | solution.py:215
  109.7 9.2 %all-to-all-start.5 = ((bf16[64,64,128]{2,1,0:T(8,128)(2,1)}), bf16[64,64,128]{2,1,0:T(8,128)(2,1)S(1)}, u32[]{:S(2)}, u32[]{:S(2)}) async-start(bf16[64,64,128]{2,1,0:T(8,128)(2,1)} %get-tuple-element.30), calls=%async_computation.5 | async-start | bytes 2097152 | tf_op jit(solution)/shard_map/all_to_all | solution.py:24
  119.2 0.1 and_convert_fusion.place_ref
  119.4 0.6 multiply_subtract_fusion
  120.1 16.9 %all-to-all-done.5.back_ref = bf16[64,64,128]{2,1,0:T(8,128)(2,1)S(1)} async-done(((bf16[64,64,128]{2,1,0:T(8,128)(2,1)}), bf16[64,64,128]{2,1,0:T(8,128)(2,1)S(1)}, u32[]{:S(2)}, u32[]{:S(2)}) %all-to-all-start.5) | async-done | bytes 1048608 | tf_op jit(solution)/shard_map/all_to_all | solution.py:24
  137.0 2.0 %blocks_in_order.1 = bf16[16,64,512]{2,1,0:T(8,128)(2,1)} custom-call(s32[48]{0:T(128)S(1)} %pad_add_fusion.meta_ref, bf16[64,64,128]{2,1,0:T(8,128)(2,1)S(1)} %all-to-all-done.5.back_ref, bf16[2,256,128]{2,1,0:T(8,128)(2,1)S(1)} %and_convert_fusion.place_ref), custom_call_target="tpu_custom_call" | custom-call | tf_op jit(solution)/shard_map/blocks_in_order/pallas_call | solution.py:215
  (38 shorter events, 0.7 us)
Async XLA Ops:
  3.2 11.2 %copy-start.3 = (bf16[2,512,8]{1,2,0:T(8,128)(2,1)S(1)}, bf16[2,512,8]{1,2,0:T(8,128)(2,1)}, u32[]{:S(2)}) copy-start(bf16[2,512,8]{1,2,0:T(8,128)(2,1)} %param.11) | copy-start | bytes 49156
  3.2 25.1 %copy-start.5 = (s32[16,2]{0,1:T(2,128)S(1)}, s32[16,2]{0,1:T(2,128)}, u32[]{:S(2)}) copy-start(s32[16,2]{0,1:T(2,128)} %param.9) | copy-start | bytes 388
  3.2 25.1 %copy-start.1 = (f32[2,512,8]{1,2,0:T(8,128)S(1)}, f32[2,512,8]{1,2,0:T(8,128)}, u32[]{:S(2)}) copy-start(f32[2,512,8]{1,2,0:T(8,128)} %param.13) | copy-start | bytes 98308
  3.3 25.1 %copy-start.2 = (f32[2,512,8]{1,2,0:T(8,128)S(1)}, f32[2,512,8]{1,2,0:T(8,128)}, u32[]{:S(2)}) copy-start(f32[2,512,8]{1,2,0:T(8,128)} %param.12) | copy-start | bytes 98308
  3.3 35.8 %all-to-all-start = ((bf16[64,64,128]{2,1,0:T(8,128)(2,1)}), bf16[64,64,128]{2,1,0:T(8,128)(2,1)S(1)}, u32[]{:S(2)}, u32[]{:S(2)}) async-start(bf16[64,64,128]{2,1,0:T(8,128)(2,1)} %blocks_to_owners.1), calls=%async_computation | async-start | bytes 2097152 | tf_op jit(solution)/shard_map/all_to_all | solution.py:24
  14.4 24.6 %collective-permute-start = (bf16[1,2,8,512]{3,2,1,0:T(8,128)(2,1)S(1)}, bf16[1,2,8,512]{3,2,1,0:T(8,128)(2,1)S(1)}, u32[]{:S(2)}, u32[]{:S(2)}) collective-permute-start(bf16[1,2,8,512]{3,2,1,0:T(8,128)(2,1)S(1)} %bitcast.57), channel_id=1, source_target_pairs={{0,64},{16,80},{32,96},{48,112},{64,0},{80,16},{96,32},{112,48},{1... | collective-permute-start | bytes 49160 | tf_op jit(solution)/shard_map/ppermute | solution.py:248
  28.4 0.7 copy-start.4
  40.1 27.5 %all-to-all-start.1 = ((f16[8,128,128]{2,1,0:T(8,128)(2,1)}), f16[8,128,128]{2,1,0:T(8,128)(2,1)S(1)}, u32[]{:S(2)}, u32[]{:S(2)}) async-start(f16[8,128,128]{2,1,0:T(8,128)(2,1)} %pad_maximum_fusion), calls=%async_computation.1 | async-start | bytes 524288 | tf_op jit(solution)/shard_map/all_to_all | solution.py:24
  46.8 18.8 %collective-permute-start.1 = (bf16[2,2,8,512]{3,2,1,0:T(8,128)(2,1)S(1)}, bf16[2,2,8,512]{3,2,1,0:T(8,128)(2,1)S(1)}, u32[]{:S(2)}, u32[]{:S(2)}) collective-permute-start(bf16[2,2,8,512]{3,2,1,0:T(8,128)(2,1)S(1)} %maximum_bitcast_fusion), channel_id=1, source_target_pairs={{0,32},{16,48},{32,0},{48,16},{64,96},{80,112},{96,64},{112,80},{1... | collective-permute-start | bytes 98312 | tf_op jit(solution)/shard_map/ppermute | solution.py:248
  65.6 6.6 %collective-permute-start.2 = (bf16[4,2,8,512]{3,2,1,0:T(8,128)(2,1)S(1)}, bf16[4,2,8,512]{3,2,1,0:T(8,128)(2,1)S(1)}, u32[]{:S(2)}, u32[]{:S(2)}) collective-permute-start(bf16[4,2,8,512]{3,2,1,0:T(8,128)(2,1)S(1)} %bitcast.54), channel_id=1, source_target_pairs={{0,16},{16,0},{32,48},{48,32},{64,80},{80,64},{96,112},{112,96},{1... | collective-permute-start | bytes 196616 | tf_op jit(solution)/shard_map/ppermute | solution.py:248
  68.8 8.9 %all-to-all-start.2 = ((bf16[8,64,128]{2,1,0:T(8,128)(2,1)}), bf16[8,64,128]{2,1,0:T(8,128)(2,1)S(1)}, u32[]{:S(2)}, u32[]{:S(2)}) async-start(bf16[8,64,128]{2,1,0:T(8,128)(2,1)} %get-tuple-element.21), calls=%async_computation.2 | async-start | bytes 262144 | tf_op jit(solution)/shard_map/all_to_all | solution.py:24
  72.2 27.3 %copy-start = (bf16[2,512,512]{2,1,0:T(8,128)(2,1)S(1)}, bf16[2,512,512]{2,1,0:T(8,128)(2,1)}, u32[]{:S(2)}) copy-start(bf16[2,512,512]{2,1,0:T(8,128)(2,1)} %left_ref.1) | copy-start | bytes 3145732
  109.7 27.2 %all-to-all-start.5 = ((bf16[64,64,128]{2,1,0:T(8,128)(2,1)}), bf16[64,64,128]{2,1,0:T(8,128)(2,1)S(1)}, u32[]{:S(2)}, u32[]{:S(2)}) async-start(bf16[64,64,128]{2,1,0:T(8,128)(2,1)} %get-tuple-element.30), calls=%async_computation.5 | async-start | bytes 2097152 | tf_op jit(solution)/shard_map/all_to_all | solution.py:24

commit v7 on v5

--- a/solution.py
+++ b/solution.py
@@ -139,7 +139,7 @@
 
 
 def fresh_kernel(
-    nm, owned, slab, meta_ref, sums_ref, precond_ref, base_ref, out_ref, step_ref, held_ref, sem
+    nm, owned, slab, meta_ref, sums_ref, precond_ref, base_ref, out_ref, step_ref
 ):
     width, lanes = precond_ref.shape
     mine = lanes // owned
@@ -163,29 +163,33 @@
         scale = jnp.where(place == s, jnp.sqrt(grad_sq / (pre_sq + epsilon)), scale)
         height = jnp.where(place == s, jnp.where(column < wide, tall, 0), height)
     rows = width // nm
-    copies = []
     for i in range(nm):
         at = slice(i * rows, (i + 1) * rows)
         ok = i * rows + iota((rows, lanes), 0) < height
         step = jnp.where(ok, scale * precond_ref[at], 0.0)
         step_ref[at] = step
         fresh = (base_ref[at] - step_rate * step).astype(bf16)
-        held_ref[i] = fresh
-        if i % 2 == 0:
-            continue
         for g in range(ng):
-            copy = pltpu.make_async_copy(
-                held_ref.at[i - 1 : i + 1],
-                out_ref.at[g * nm + i - 1 : g * nm + i + 1],
-                sem.at[i // 2 * ng + g],
-            )
-            copy.start()
-            copies.append(copy)
-    for copy in copies:
-        copy.wait()
-
-
-def place_kernel(nx, nm, owned, meta_ref, back_ref, place_ref, out_ref, held_ref, sem):
+            out_ref[g * nm + i] = fresh
+
+
+def place_kernel(
+    nx,
+    nm,
+    owned,
+    meta_ref,
+    back_ref,
+    place_ref,
+    step_ref,
+    momentum_ref,
+    master_ref,
+    out_ref,
+    new_momentum_ref,
+    new_master_ref,
+    held_ref,
+    flip_ref,
+    sem,
+):
     blocks, rows, width = out_ref.shape
     cols = width // nx
     copies = []
@@ -204,6 +208,15 @@
         copy = pltpu.make_async_copy(held_ref.at[b], out_ref.at[b], sem.at[b])
         copy.start()
         copies.append(copy)
+    _, slab, _ = momentum_ref.shape
+    mine = step_ref.shape[1] // owned
+    flip_ref[...] = step_ref[...].T
+    zh = lax.axis_index("zh")
+    for s in range(owned):
+        own = flip_ref[pl.ds(pl.multiple_of(s * mine + zh * slab, slab), slab), :]
+        new_momentum = beta_decay * momentum_ref[s] + own
+        new_momentum_ref[s] = new_momentum
+        new_master_ref[s] = master_ref[s] - step_rate * new_momentum
     for copy in copies:
         copy.wait()
 
@@ -258,7 +271,6 @@
         cols = width // nx
         mine_cols = slab * nzh
         lanes = owned * mine_cols
-        zh = lax.axis_index("zh")
 
         roots = jnp.swapaxes(right_roots, 1, 2)[None]
         strides = [nzh >> i for i in range(1, nzh.bit_length())]
@@ -313,6 +325,16 @@
             roots,
             sq,
         )
+        lane = jnp.arange(lanes, dtype=jnp.int32)
+        c = lane % mine_cols
+        to = jnp.arange(nzl, dtype=jnp.int32)[:, None] * slab + (c // slab) * (slab * nzl) + c % slab
+        to = to.reshape(nzl * lanes)
+        from_slot = jnp.tile(lane // mine_cols, nzl)
+        place = (to[None, :, None] == jnp.arange(cols, dtype=jnp.int32)) & (
+            from_slot[None, :, None] == jnp.arange(owned, dtype=jnp.int32)[:, None, None]
+        )
+        place = place.astype(bf16)
+        base_t, place, packed = lax.optimization_barrier((base_t, place, packed))
         bands = exchange(packed, "zh")
         precond, base, sums = call(
             left_kernel,
@@ -331,34 +353,30 @@
             sums,
             precond,
             base,
-            scratch=[pltpu.VMEM((nm, rows, lanes), bf16), pltpu.SemaphoreType.DMA((nm // 2 * ng,))],
-            far_out=(0,),
         )
         back = exchange(fresh, wide)
-        lane = jnp.arange(lanes, dtype=jnp.int32)
-        c = lane % mine_cols
-        to = jnp.arange(nzl, dtype=jnp.int32)[:, None] * slab + (c // slab) * (slab * nzl) + c % slab
-        to = to.reshape(nzl * lanes)
-        from_slot = jnp.tile(lane // mine_cols, nzl)
-        place = (to[None, :, None] == jnp.arange(cols, dtype=jnp.int32)) & (
-            from_slot[None, :, None] == jnp.arange(owned, dtype=jnp.int32)[:, None, None]
-        )
-        (weights,) = call(
+        weights, new_momentum, new_master = call(
             functools.partial(place_kernel, nx, nm, owned),
             "blocks_in_order",
-            [shape((blocks, rows, width), bf16)],
+            (
+                shape((blocks, rows, width), bf16),
+                shape((owned, slab, width), f32),
+                shape((owned, slab, width), f32),
+            ),
             meta,
             back,
-            place.astype(bf16),
-            scratch=[pltpu.VMEM((blocks, rows, width), bf16), pltpu.SemaphoreType.DMA((blocks,))],
+            place,
+            step,
+            jnp.swapaxes(momentum, 1, 2),
+            jnp.swapaxes(master, 1, 2),
+            scratch=[
+                pltpu.VMEM((blocks, rows, width), bf16),
+                pltpu.VMEM((lanes, width), f32),
+                pltpu.SemaphoreType.DMA((blocks,)),
+            ],
             far_out=(0,),
         )
-
-        step = step.reshape(width, owned, mine_cols)
-        own_step = lax.dynamic_slice_in_dim(step, zh * slab, slab, 2).transpose(1, 0, 2)
-        new_momentum = beta_decay * momentum + own_step
-        new_master = master - step_rate * new_momentum
-        return (new_momentum, new_master, weights)
+        return (jnp.swapaxes(new_momentum, 1, 2), jnp.swapaxes(new_master, 1, 2), weights)
 
     return local
 

time: 141 us -> 138 us (0.979)
  blocking collectives: 7.7 us -> 55.8 us
  waiting for transfers between devices: 57.5 us -> 25.7 us
  starting transfers between devices: 61.4 us -> 44.3 us
    all_to_all x1 -> x3, blocking collectives: 7.7 us -> 55.8 us  [exchange(): return lax.all_to_all(value, axes, split_axis=0, concat_axis=0, tiled=True)]
    all_to_all x5 -> x3, waiting for transfers between devices: 36.1 us -> 5.33 us  [exchange(): return lax.all_to_all(value, axes, split_axis=0, concat_axis=0, tiled=True)]
    all_to_all x5 -> x3, starting transfers between devices: 38.3 us -> 21.2 us  [exchange(): return lax.all_to_all(value, axes, split_axis=0, concat_axis=0, tiled=True)]
  transfers between devices with their start and end apart: 8 -> 6, of which waited for: 5 -> 3; matrix products, arithmetic and copies ran while one was open for 1% -> 0% of each run, Pallas kernels for 1% -> 1%
where the time goes in v7:
time: 138 us
  blocking collectives  55.8 us (40%)
  starting transfers between devices  44.3 us (32%)
  waiting for transfers between devices  25.7 us (19%)
  Pallas kernels  8.03 us (6%)
  other arithmetic  1.49 us (1%)
  local copies, waits for them, and re-layouts  1.44 us (1%)
    all_to_all x3, blocking collectives, exchange(): return lax.all_to_all(value, axes, split_axis=0, concat_axis=0, tiled=True)  55.8 us
    ppermute x3, starting transfers between devices, swap(): other = lax.ppermute(held, 'zh', pairs)  23.1 us
    all_to_all x3, starting transfers between devices, exchange(): return lax.all_to_all(value, axes, split_axis=0, concat_axis=0, tiled=True)  21.2 us
    ppermute x3, waiting for transfers between devices, swap(): other = lax.ppermute(held, 'zh', pairs)  20.3 us
    pallas_call x6, Pallas kernels, call(): pl.pallas_call(kernel, out_shape=out, in_specs=specs, out_specs=[in_hbm i...  8.03 us
    all_to_all x3, waiting for transfers between devices, exchange(): return lax.all_to_all(value, axes, split_axis=0, concat_axis=0, tiled=True)  5.33 us
  transfers between devices with their start and end apart: 6, of which 3 were waited for; matrix products, arithmetic and copies ran while one was open for 0% of the time, Pallas kernels for 1%

profile of v7, /device:TPU:1, one launch (start us, length us, event | category | flops | bytes accessed | tf_op | source)
XLA Modules:
  0.0 137.7 jit_solution(2679880842190270942)
XLA Ops:
  0.6 2.6 %blocks_to_owners.1 = bf16[64,64,128]{2,1,0:T(8,128)(2,1)} custom-call(s32[16]{0:T(128)} %slots_ref.1, bf16[16,64,512]{2,1,0:T(8,128)(2,1)} %bitcast.53), custom_call_target="tpu_custom_call" | custom-call | tf_op jit(solution)/shard_map/blocks_to_owners/pallas_call | solution.py:228
  3.3 11.1 %all-to-all-start = ((bf16[64,64,128]{2,1,0:T(8,128)(2,1)}), bf16[64,64,128]{2,1,0:T(8,128)(2,1)S(1)}, u32[]{:S(2)}, u32[]{:S(2)}) async-start(bf16[64,64,128]{2,1,0:T(8,128)(2,1)} %blocks_to_owners.1), calls=%async_computation | async-start | bytes 2097152 | tf_op jit(solution)/shard_map/all_to_all | solution.py:24
  14.4 13.9 %collective-permute-start = (bf16[1,2,8,512]{3,2,1,0:T(8,128)(2,1)S(1)}, bf16[1,2,8,512]{3,2,1,0:T(8,128)(2,1)S(1)}, u32[]{:S(2)}, u32[]{:S(2)}) collective-permute-start(bf16[1,2,8,512]{3,2,1,0:T(8,128)(2,1)S(1)} %bitcast.58), channel_id=1, source_target_pairs={{0,64},{16,80},{32,96},{48,112},{64,0},{80,16},{96,32},{112,48},{1... | collective-permute-start | bytes 49160 | tf_op jit(solution)/shard_map/ppermute | solution.py:261
  28.4 0.7 copy-done.5
  29.1 0.6 copy-done.4
  29.9 9.1 %collective-permute-done = bf16[1,2,8,512]{3,2,1,0:T(8,128)(2,1)S(1)} collective-permute-done((bf16[1,2,8,512]{3,2,1,0:T(8,128)(2,1)S(1)}, bf16[1,2,8,512]{3,2,1,0:T(8,128)(2,1)S(1)}, u32[]{:S(2)}, u32[]{:S(2)}) %collective-permute-start) | collective-permute-done | bytes 16416 | tf_op jit(solution)/shard_map/ppermute | solution.py:261
  39.1 0.2 multiply_convert_fusion
  39.3 0.8 pad_maximum_fusion
  40.0 6.7 %all-to-all-start.1 = ((f16[8,128,128]{2,1,0:T(8,128)(2,1)}), f16[8,128,128]{2,1,0:T(8,128)(2,1)S(1)}, u32[]{:S(2)}, u32[]{:S(2)}) async-start(f16[8,128,128]{2,1,0:T(8,128)(2,1)} %pad_maximum_fusion), calls=%async_computation.1 | async-start | bytes 524288 | tf_op jit(solution)/shard_map/all_to_all | solution.py:24
  46.8 0.1 iota_compare_fusion
  46.9 7.3 %collective-permute-start.1 = (bf16[2,2,8,512]{3,2,1,0:T(8,128)(2,1)S(1)}, bf16[2,2,8,512]{3,2,1,0:T(8,128)(2,1)S(1)}, u32[]{:S(2)}, u32[]{:S(2)}) collective-permute-start(bf16[2,2,8,512]{3,2,1,0:T(8,128)(2,1)S(1)} %maximum_bitcast_fusion), channel_id=1, source_target_pairs={{0,32},{16,48},{32,0},{48,16},{64,96},{80,112},{96,64},{112,80},{1... | collective-permute-start | bytes 98312 | tf_op jit(solution)/shard_map/ppermute | solution.py:261
  54.2 0.1 and_convert_fusion.place_ref
  54.3 11.2 %collective-permute-done.1 = bf16[2,2,8,512]{3,2,1,0:T(8,128)(2,1)S(1)} collective-permute-done((bf16[2,2,8,512]{3,2,1,0:T(8,128)(2,1)S(1)}, bf16[2,2,8,512]{3,2,1,0:T(8,128)(2,1)S(1)}, u32[]{:S(2)}, u32[]{:S(2)}) %collective-permute-start.1) | collective-permute-done | bytes 32800 | tf_op jit(solution)/shard_map/ppermute | solution.py:261
  65.6 1.9 %collective-permute-start.2 = (bf16[4,2,8,512]{3,2,1,0:T(8,128)(2,1)S(1)}, bf16[4,2,8,512]{3,2,1,0:T(8,128)(2,1)S(1)}, u32[]{:S(2)}, u32[]{:S(2)}) collective-permute-start(bf16[4,2,8,512]{3,2,1,0:T(8,128)(2,1)S(1)} %bitcast.55), channel_id=1, source_target_pairs={{0,16},{16,0},{32,48},{48,32},{64,80},{80,64},{96,112},{112,96},{1... | collective-permute-start | bytes 196616 | tf_op jit(solution)/shard_map/ppermute | solution.py:261
  67.6 1.2 masked_grad.1
  68.8 3.4 %all-to-all-start.2 = ((bf16[8,64,128]{2,1,0:T(8,128)(2,1)}), bf16[8,64,128]{2,1,0:T(8,128)(2,1)S(1)}, u32[]{:S(2)}, u32[]{:S(2)}) async-start(bf16[8,64,128]{2,1,0:T(8,128)(2,1)} %get-tuple-element.25), calls=%async_computation.2 | async-start | bytes 262144 | tf_op jit(solution)/shard_map/all_to_all | solution.py:24
  72.3 5.3 %all-to-all-done.2.cols_ref = bf16[8,64,128]{2,1,0:T(8,128)(2,1)S(1)} async-done(((bf16[8,64,128]{2,1,0:T(8,128)(2,1)}), bf16[8,64,128]{2,1,0:T(8,128)(2,1)S(1)}, u32[]{:S(2)}, u32[]{:S(2)}) %all-to-all-start.2) | async-done | bytes 131104 | tf_op jit(solution)/shard_map/all_to_all | solution.py:24
  77.7 0.3 right_side.1
  77.9 21.6 %all_to_all.30.bands_ref = bf16[8,80,128]{2,1,0:T(8,128)(2,1)S(1)} all-to-all(bf16[8,80,128]{2,1,0:T(8,128)(2,1)S(1)} %right_side.1), channel_id=1, replica_groups=mesh['x'=4,'zh'=8,'zl'=2,'mp'=8] {'zh'}, dimensions={0} | all-to-all | bytes 327680 | tf_op jit(solution)/shard_map/all_to_all | solution.py:24
  99.5 0.4 left_side.1
  100.0 7.7 %all_to_all.31.sums_ref = f32[8,8,128]{2,1,0:T(8,128)S(1)} all-to-all(f32[8,8,128]{2,1,0:T(8,128)S(1)} %get-tuple-element.30), channel_id=1, replica_groups=mesh['x'=4,'zh'=8,'zl'=2,'mp'=8] {'x','zl'}, dimensions={0} | all-to-all | bytes 65536 | tf_op jit(solution)/shard_map/all_to_all | solution.py:24
  107.7 0.8 new_weights.1
  108.5 26.5 %all_to_all.32.back_ref = bf16[64,64,128]{2,1,0:T(8,128)(2,1)S(1)} all-to-all(bf16[64,64,128]{2,1,0:T(8,128)(2,1)S(1)} %get-tuple-element.33), channel_id=1, replica_groups=mesh['x'=4,'zh'=8,'zl'=2,'mp'=8] {'x','zl','mp'}, dimensions={0} | all-to-all | bytes 2097152 | tf_op jit(solution)/shard_map/all_to_all | solution.py:24
  135.0 2.7 %blocks_in_order.1 = (bf16[16,64,512]{2,1,0:T(8,128)(2,1)}, f32[2,8,512]{2,1,0:T(8,128)}, f32[2,8,512]{2,1,0:T(8,128)}) custom-call(s32[48]{0:T(128)S(1)} %pad_add_fusion.meta_ref, bf16[64,64,128]{2,1,0:T(8,128)(2,1)S(1)} %all_to_all.32.back_ref, bf16[2,256,128]{2,1,0:T(8,128)(2,1)S(1)} %and_convert_fusion.place_ref, ...), custom_call_target="tpu_custom_call" | custom-call | tf_op jit(solution)/shard_map/blocks_in_order/pallas_call | solution.py:228
  (35 shorter events, 0.4 us)
Async XLA Ops:
  3.2 11.2 %copy-start.3 = (bf16[2,512,8]{1,2,0:T(8,128)(2,1)S(1)}, bf16[2,512,8]{1,2,0:T(8,128)(2,1)}, u32[]{:S(2)}) copy-start(bf16[2,512,8]{1,2,0:T(8,128)(2,1)} %param.11) | copy-start | bytes 49156
  3.2 25.9 %copy-start.1 = (f32[2,512,8]{1,2,0:T(8,128)S(1)}, f32[2,512,8]{1,2,0:T(8,128)}, u32[]{:S(2)}) copy-start(f32[2,512,8]{1,2,0:T(8,128)} %param.13) | copy-start | bytes 98308
  3.2 25.9 %copy-start.2 = (f32[2,512,8]{1,2,0:T(8,128)S(1)}, f32[2,512,8]{1,2,0:T(8,128)}, u32[]{:S(2)}) copy-start(f32[2,512,8]{1,2,0:T(8,128)} %param.12) | copy-start | bytes 98308
  3.3 35.8 %all-to-all-start = ((bf16[64,64,128]{2,1,0:T(8,128)(2,1)}), bf16[64,64,128]{2,1,0:T(8,128)(2,1)S(1)}, u32[]{:S(2)}, u32[]{:S(2)}) async-start(bf16[64,64,128]{2,1,0:T(8,128)(2,1)} %blocks_to_owners.1), calls=%async_computation | async-start | bytes 2097152 | tf_op jit(solution)/shard_map/all_to_all | solution.py:24
  14.4 24.6 %collective-permute-start = (bf16[1,2,8,512]{3,2,1,0:T(8,128)(2,1)S(1)}, bf16[1,2,8,512]{3,2,1,0:T(8,128)(2,1)S(1)}, u32[]{:S(2)}, u32[]{:S(2)}) collective-permute-start(bf16[1,2,8,512]{3,2,1,0:T(8,128)(2,1)S(1)} %bitcast.58), channel_id=1, source_target_pairs={{0,64},{16,80},{32,96},{48,112},{64,0},{80,16},{96,32},{112,48},{1... | collective-permute-start | bytes 49160 | tf_op jit(solution)/shard_map/ppermute | solution.py:261
  28.4 0.7 copy-start.5
  29.1 0.7 copy-start.4
  40.0 27.5 %all-to-all-start.1 = ((f16[8,128,128]{2,1,0:T(8,128)(2,1)}), f16[8,128,128]{2,1,0:T(8,128)(2,1)S(1)}, u32[]{:S(2)}, u32[]{:S(2)}) async-start(f16[8,128,128]{2,1,0:T(8,128)(2,1)} %pad_maximum_fusion), calls=%async_computation.1 | async-start | bytes 524288 | tf_op jit(solution)/shard_map/all_to_all | solution.py:24
  46.9 18.6 %collective-permute-start.1 = (bf16[2,2,8,512]{3,2,1,0:T(8,128)(2,1)S(1)}, bf16[2,2,8,512]{3,2,1,0:T(8,128)(2,1)S(1)}, u32[]{:S(2)}, u32[]{:S(2)}) collective-permute-start(bf16[2,2,8,512]{3,2,1,0:T(8,128)(2,1)S(1)} %maximum_bitcast_fusion), channel_id=1, source_target_pairs={{0,32},{16,48},{32,0},{48,16},{64,96},{80,112},{96,64},{112,80},{1... | collective-permute-start | bytes 98312 | tf_op jit(solution)/shard_map/ppermute | solution.py:261
  65.6 6.6 %collective-permute-start.2 = (bf16[4,2,8,512]{3,2,1,0:T(8,128)(2,1)S(1)}, bf16[4,2,8,512]{3,2,1,0:T(8,128)(2,1)S(1)}, u32[]{:S(2)}, u32[]{:S(2)}) collective-permute-start(bf16[4,2,8,512]{3,2,1,0:T(8,128)(2,1)S(1)} %bitcast.55), channel_id=1, source_target_pairs={{0,16},{16,0},{32,48},{48,32},{64,80},{80,64},{96,112},{112,96},{1... | collective-permute-start | bytes 196616 | tf_op jit(solution)/shard_map/ppermute | solution.py:261
  68.8 8.9 %all-to-all-start.2 = ((bf16[8,64,128]{2,1,0:T(8,128)(2,1)}), bf16[8,64,128]{2,1,0:T(8,128)(2,1)S(1)}, u32[]{:S(2)}, u32[]{:S(2)}) async-start(bf16[8,64,128]{2,1,0:T(8,128)(2,1)} %get-tuple-element.25), calls=%async_computation.2 | async-start | bytes 262144 | tf_op jit(solution)/shard_map/all_to_all | solution.py:24
  72.2 27.3 %copy-start = (bf16[2,512,512]{2,1,0:T(8,128)(2,1)S(1)}, bf16[2,512,512]{2,1,0:T(8,128)(2,1)}, u32[]{:S(2)}) copy-start(bf16[2,512,512]{2,1,0:T(8,128)(2,1)} %left_ref.1) | copy-start | bytes 3145732

commit v8 on v7

--- a/solution.py
+++ b/solution.py
@@ -188,11 +188,27 @@
     new_master_ref,
     held_ref,
     flip_ref,
+    held_momentum_ref,
+    held_master_ref,
     sem,
 ):
     blocks, rows, width = out_ref.shape
     cols = width // nx
-    copies = []
+    _, slab, _ = momentum_ref.shape
+    mine = step_ref.shape[1] // owned
+    flip_ref[...] = step_ref[...].T
+    zh = lax.axis_index("zh")
+    for s in range(owned):
+        own = flip_ref[pl.ds(pl.multiple_of(s * mine + zh * slab, slab), slab), :]
+        new_momentum = beta_decay * momentum_ref[s] + own
+        held_momentum_ref[s] = new_momentum
+        held_master_ref[s] = master_ref[s] - step_rate * new_momentum
+    copies = [
+        pltpu.make_async_copy(held_momentum_ref, new_momentum_ref, sem.at[blocks]),
+        pltpu.make_async_copy(held_master_ref, new_master_ref, sem.at[blocks + 1]),
+    ]
+    for copy in copies:
+        copy.start()
     for b in range(blocks):
         slot = meta_ref[b]
         owner, s = slot // owned, slot % owned
@@ -208,15 +224,6 @@
         copy = pltpu.make_async_copy(held_ref.at[b], out_ref.at[b], sem.at[b])
         copy.start()
         copies.append(copy)
-    _, slab, _ = momentum_ref.shape
-    mine = step_ref.shape[1] // owned
-    flip_ref[...] = step_ref[...].T
-    zh = lax.axis_index("zh")
-    for s in range(owned):
-        own = flip_ref[pl.ds(pl.multiple_of(s * mine + zh * slab, slab), slab), :]
-        new_momentum = beta_decay * momentum_ref[s] + own
-        new_momentum_ref[s] = new_momentum
-        new_master_ref[s] = master_ref[s] - step_rate * new_momentum
     for copy in copies:
         copy.wait()
 
@@ -372,9 +379,11 @@
             scratch=[
                 pltpu.VMEM((blocks, rows, width), bf16),
                 pltpu.VMEM((lanes, width), f32),
-                pltpu.SemaphoreType.DMA((blocks,)),
+                pltpu.VMEM((owned, slab, width), f32),
+                pltpu.VMEM((owned, slab, width), f32),
+                pltpu.SemaphoreType.DMA((blocks + 2,)),
             ],
-            far_out=(0,),
+            far_out=(0, 1, 2),
         )
         return (jnp.swapaxes(new_momentum, 1, 2), jnp.swapaxes(new_master, 1, 2), weights)
 

time: 138 us -> 138 us (level)
  no operation moved by 1% of the time
where the time goes in v8:
time: 138 us; the launch traced here: 137 us
  blocking collectives  55.8 us (40%)
  starting transfers between devices  44.3 us (32%)
  waiting for transfers between devices  25.7 us (19%)
  Pallas kernels  7.42 us (5%)
  other arithmetic  1.49 us (1%)
  local copies, waits for them, and re-layouts  1.44 us (1%)
    all_to_all x3, blocking collectives, exchange(): return lax.all_to_all(value, axes, split_axis=0, concat_axis=0, tiled=True)  55.8 us
    ppermute x3, starting transfers between devices, swap(): other = lax.ppermute(held, 'zh', pairs)  23.1 us
    all_to_all x3, starting transfers between devices, exchange(): return lax.all_to_all(value, axes, split_axis=0, concat_axis=0, tiled=True)  21.2 us
    ppermute x3, waiting for transfers between devices, swap(): other = lax.ppermute(held, 'zh', pairs)  20.3 us
    pallas_call x6, Pallas kernels, call(): pl.pallas_call(kernel, out_shape=out, in_specs=specs, out_specs=[in_hbm i...  7.42 us
    all_to_all x3, waiting for transfers between devices, exchange(): return lax.all_to_all(value, axes, split_axis=0, concat_axis=0, tiled=True)  5.33 us
  transfers between devices with their start and end apart: 6, of which 3 were waited for; matrix products, arithmetic and copies ran while one was open for 0% of the time, Pallas kernels for 1%

profile of v8, /device:TPU:1, one launch (start us, length us, event | category | flops | bytes accessed | tf_op | source)
XLA Modules:
  0.0 137.1 jit_solution(2058919129406958838)
XLA Ops:
  0.6 2.6 %blocks_to_owners.1 = bf16[64,64,128]{2,1,0:T(8,128)(2,1)} custom-call(s32[16]{0:T(128)} %slots_ref.1, bf16[16,64,512]{2,1,0:T(8,128)(2,1)} %bitcast.53), custom_call_target="tpu_custom_call" | custom-call | tf_op jit(solution)/shard_map/blocks_to_owners/pallas_call | solution.py:235
  3.3 11.1 %all-to-all-start = ((bf16[64,64,128]{2,1,0:T(8,128)(2,1)}), bf16[64,64,128]{2,1,0:T(8,128)(2,1)S(1)}, u32[]{:S(2)}, u32[]{:S(2)}) async-start(bf16[64,64,128]{2,1,0:T(8,128)(2,1)} %blocks_to_owners.1), calls=%async_computation | async-start | bytes 2097152 | tf_op jit(solution)/shard_map/all_to_all | solution.py:24
  14.4 13.9 %collective-permute-start = (bf16[1,2,8,512]{3,2,1,0:T(8,128)(2,1)S(1)}, bf16[1,2,8,512]{3,2,1,0:T(8,128)(2,1)S(1)}, u32[]{:S(2)}, u32[]{:S(2)}) collective-permute-start(bf16[1,2,8,512]{3,2,1,0:T(8,128)(2,1)S(1)} %bitcast.58), channel_id=1, source_target_pairs={{0,64},{16,80},{32,96},{48,112},{64,0},{80,16},{96,32},{112,48},{1... | collective-permute-start | bytes 49160 | tf_op jit(solution)/shard_map/ppermute | solution.py:268
  28.4 0.7 copy-done.5
  29.1 0.6 copy-done.4
  29.9 9.1 %collective-permute-done = bf16[1,2,8,512]{3,2,1,0:T(8,128)(2,1)S(1)} collective-permute-done((bf16[1,2,8,512]{3,2,1,0:T(8,128)(2,1)S(1)}, bf16[1,2,8,512]{3,2,1,0:T(8,128)(2,1)S(1)}, u32[]{:S(2)}, u32[]{:S(2)}) %collective-permute-start) | collective-permute-done | bytes 16416 | tf_op jit(solution)/shard_map/ppermute | solution.py:268
  39.1 0.2 multiply_convert_fusion
  39.3 0.8 pad_maximum_fusion
  40.0 6.7 %all-to-all-start.1 = ((f16[8,128,128]{2,1,0:T(8,128)(2,1)}), f16[8,128,128]{2,1,0:T(8,128)(2,1)S(1)}, u32[]{:S(2)}, u32[]{:S(2)}) async-start(f16[8,128,128]{2,1,0:T(8,128)(2,1)} %pad_maximum_fusion), calls=%async_computation.1 | async-start | bytes 524288 | tf_op jit(solution)/shard_map/all_to_all | solution.py:24
  46.8 0.1 iota_compare_fusion
  46.9 7.3 %collective-permute-start.1 = (bf16[2,2,8,512]{3,2,1,0:T(8,128)(2,1)S(1)}, bf16[2,2,8,512]{3,2,1,0:T(8,128)(2,1)S(1)}, u32[]{:S(2)}, u32[]{:S(2)}) collective-permute-start(bf16[2,2,8,512]{3,2,1,0:T(8,128)(2,1)S(1)} %maximum_bitcast_fusion), channel_id=1, source_target_pairs={{0,32},{16,48},{32,0},{48,16},{64,96},{80,112},{96,64},{112,80},{1... | collective-permute-start | bytes 98312 | tf_op jit(solution)/shard_map/ppermute | solution.py:268
  54.2 0.1 and_convert_fusion.place_ref
  54.3 11.2 %collective-permute-done.1 = bf16[2,2,8,512]{3,2,1,0:T(8,128)(2,1)S(1)} collective-permute-done((bf16[2,2,8,512]{3,2,1,0:T(8,128)(2,1)S(1)}, bf16[2,2,8,512]{3,2,1,0:T(8,128)(2,1)S(1)}, u32[]{:S(2)}, u32[]{:S(2)}) %collective-permute-start.1) | collective-permute-done | bytes 32800 | tf_op jit(solution)/shard_map/ppermute | solution.py:268
  65.6 1.9 %collective-permute-start.2 = (bf16[4,2,8,512]{3,2,1,0:T(8,128)(2,1)S(1)}, bf16[4,2,8,512]{3,2,1,0:T(8,128)(2,1)S(1)}, u32[]{:S(2)}, u32[]{:S(2)}) collective-permute-start(bf16[4,2,8,512]{3,2,1,0:T(8,128)(2,1)S(1)} %bitcast.55), channel_id=1, source_target_pairs={{0,16},{16,0},{32,48},{48,32},{64,80},{80,64},{96,112},{112,96},{1... | collective-permute-start | bytes 196616 | tf_op jit(solution)/shard_map/ppermute | solution.py:268
  67.6 1.2 masked_grad.1
  68.8 3.4 %all-to-all-start.2 = ((bf16[8,64,128]{2,1,0:T(8,128)(2,1)}), bf16[8,64,128]{2,1,0:T(8,128)(2,1)S(1)}, u32[]{:S(2)}, u32[]{:S(2)}) async-start(bf16[8,64,128]{2,1,0:T(8,128)(2,1)} %get-tuple-element.25), calls=%async_computation.2 | async-start | bytes 262144 | tf_op jit(solution)/shard_map/all_to_all | solution.py:24
  72.3 5.3 %all-to-all-done.2.cols_ref = bf16[8,64,128]{2,1,0:T(8,128)(2,1)S(1)} async-done(((bf16[8,64,128]{2,1,0:T(8,128)(2,1)}), bf16[8,64,128]{2,1,0:T(8,128)(2,1)S(1)}, u32[]{:S(2)}, u32[]{:S(2)}) %all-to-all-start.2) | async-done | bytes 131104 | tf_op jit(solution)/shard_map/all_to_all | solution.py:24
  77.7 0.3 right_side.1
  77.9 21.6 %all_to_all.30.bands_ref = bf16[8,80,128]{2,1,0:T(8,128)(2,1)S(1)} all-to-all(bf16[8,80,128]{2,1,0:T(8,128)(2,1)S(1)} %right_side.1), channel_id=1, replica_groups=mesh['x'=4,'zh'=8,'zl'=2,'mp'=8] {'zh'}, dimensions={0} | all-to-all | bytes 327680 | tf_op jit(solution)/shard_map/all_to_all | solution.py:24
  99.5 0.4 left_side.1
  100.0 7.7 %all_to_all.31.sums_ref = f32[8,8,128]{2,1,0:T(8,128)S(1)} all-to-all(f32[8,8,128]{2,1,0:T(8,128)S(1)} %get-tuple-element.30), channel_id=1, replica_groups=mesh['x'=4,'zh'=8,'zl'=2,'mp'=8] {'x','zl'}, dimensions={0} | all-to-all | bytes 65536 | tf_op jit(solution)/shard_map/all_to_all | solution.py:24
  107.7 0.8 new_weights.1
  108.5 26.5 %all_to_all.32.back_ref = bf16[64,64,128]{2,1,0:T(8,128)(2,1)S(1)} all-to-all(bf16[64,64,128]{2,1,0:T(8,128)(2,1)S(1)} %get-tuple-element.33), channel_id=1, replica_groups=mesh['x'=4,'zh'=8,'zl'=2,'mp'=8] {'x','zl','mp'}, dimensions={0} | all-to-all | bytes 2097152 | tf_op jit(solution)/shard_map/all_to_all | solution.py:24
  135.0 2.1 %blocks_in_order.1 = (bf16[16,64,512]{2,1,0:T(8,128)(2,1)}, f32[2,8,512]{2,1,0:T(8,128)}, f32[2,8,512]{2,1,0:T(8,128)}) custom-call(s32[48]{0:T(128)S(1)} %pad_add_fusion.meta_ref, bf16[64,64,128]{2,1,0:T(8,128)(2,1)S(1)} %all_to_all.32.back_ref, bf16[2,256,128]{2,1,0:T(8,128)(2,1)S(1)} %and_convert_fusion.place_ref, ...), custom_call_target="tpu_custom_call" | custom-call | tf_op jit(solution)/shard_map/blocks_in_order/pallas_call | solution.py:235
  (35 shorter events, 0.4 us)
Async XLA Ops:
  3.2 11.2 %copy-start.3 = (bf16[2,512,8]{1,2,0:T(8,128)(2,1)S(1)}, bf16[2,512,8]{1,2,0:T(8,128)(2,1)}, u32[]{:S(2)}) copy-start(bf16[2,512,8]{1,2,0:T(8,128)(2,1)} %param.11) | copy-start | bytes 49156
  3.2 25.9 %copy-start.1 = (f32[2,512,8]{1,2,0:T(8,128)S(1)}, f32[2,512,8]{1,2,0:T(8,128)}, u32[]{:S(2)}) copy-start(f32[2,512,8]{1,2,0:T(8,128)} %param.13) | copy-start | bytes 98308
  3.2 25.9 %copy-start.2 = (f32[2,512,8]{1,2,0:T(8,128)S(1)}, f32[2,512,8]{1,2,0:T(8,128)}, u32[]{:S(2)}) copy-start(f32[2,512,8]{1,2,0:T(8,128)} %param.12) | copy-start | bytes 98308
  3.3 35.8 %all-to-all-start = ((bf16[64,64,128]{2,1,0:T(8,128)(2,1)}), bf16[64,64,128]{2,1,0:T(8,128)(2,1)S(1)}, u32[]{:S(2)}, u32[]{:S(2)}) async-start(bf16[64,64,128]{2,1,0:T(8,128)(2,1)} %blocks_to_owners.1), calls=%async_computation | async-start | bytes 2097152 | tf_op jit(solution)/shard_map/all_to_all | solution.py:24
  14.4 24.6 %collective-permute-start = (bf16[1,2,8,512]{3,2,1,0:T(8,128)(2,1)S(1)}, bf16[1,2,8,512]{3,2,1,0:T(8,128)(2,1)S(1)}, u32[]{:S(2)}, u32[]{:S(2)}) collective-permute-start(bf16[1,2,8,512]{3,2,1,0:T(8,128)(2,1)S(1)} %bitcast.58), channel_id=1, source_target_pairs={{0,64},{16,80},{32,96},{48,112},{64,0},{80,16},{96,32},{112,48},{1... | collective-permute-start | bytes 49160 | tf_op jit(solution)/shard_map/ppermute | solution.py:268
  28.4 0.7 copy-start.5
  29.1 0.7 copy-start.4
  40.0 27.5 %all-to-all-start.1 = ((f16[8,128,128]{2,1,0:T(8,128)(2,1)}), f16[8,128,128]{2,1,0:T(8,128)(2,1)S(1)}, u32[]{:S(2)}, u32[]{:S(2)}) async-start(f16[8,128,128]{2,1,0:T(8,128)(2,1)} %pad_maximum_fusion), calls=%async_computation.1 | async-start | bytes 524288 | tf_op jit(solution)/shard_map/all_to_all | solution.py:24
  46.9 18.6 %collective-permute-start.1 = (bf16[2,2,8,512]{3,2,1,0:T(8,128)(2,1)S(1)}, bf16[2,2,8,512]{3,2,1,0:T(8,128)(2,1)S(1)}, u32[]{:S(2)}, u32[]{:S(2)}) collective-permute-start(bf16[2,2,8,512]{3,2,1,0:T(8,128)(2,1)S(1)} %maximum_bitcast_fusion), channel_id=1, source_target_pairs={{0,32},{16,48},{32,0},{48,16},{64,96},{80,112},{96,64},{112,80},{1... | collective-permute-start | bytes 98312 | tf_op jit(solution)/shard_map/ppermute | solution.py:268
  65.6 6.6 %collective-permute-start.2 = (bf16[4,2,8,512]{3,2,1,0:T(8,128)(2,1)S(1)}, bf16[4,2,8,512]{3,2,1,0:T(8,128)(2,1)S(1)}, u32[]{:S(2)}, u32[]{:S(2)}) collective-permute-start(bf16[4,2,8,512]{3,2,1,0:T(8,128)(2,1)S(1)} %bitcast.55), channel_id=1, source_target_pairs={{0,16},{16,0},{32,48},{48,32},{64,80},{80,64},{96,112},{112,96},{1... | collective-permute-start | bytes 196616 | tf_op jit(solution)/shard_map/ppermute | solution.py:268
  68.8 8.9 %all-to-all-start.2 = ((bf16[8,64,128]{2,1,0:T(8,128)(2,1)}), bf16[8,64,128]{2,1,0:T(8,128)(2,1)S(1)}, u32[]{:S(2)}, u32[]{:S(2)}) async-start(bf16[8,64,128]{2,1,0:T(8,128)(2,1)} %get-tuple-element.25), calls=%async_computation.2 | async-start | bytes 262144 | tf_op jit(solution)/shard_map/all_to_all | solution.py:24
  72.2 27.3 %copy-start = (bf16[2,512,512]{2,1,0:T(8,128)(2,1)S(1)}, bf16[2,512,512]{2,1,0:T(8,128)(2,1)}, u32[]{:S(2)}) copy-start(bf16[2,512,512]{2,1,0:T(8,128)(2,1)} %left_ref.1) | copy-start | bytes 3145732
